TPU v7x, 128 devices: a whole 4x4x4 slice. The times are simulated.
128 devices in a mesh: bx: 8 (over x, core), by: 16 (over y, z).
Axes of the slice: x: 4, y: 4, z: 4, core: 2. Of those that a mesh axis runs over, the one named last changes fastest.
Arguments:
- tetrahedron_defect_values: float32 [1048576], P(('bx', 'by')), may hold values from -6 to 6
- tetrahedron_destination_block: int32 [1048576, 1], P(('bx', 'by')), may hold values from 0 to 127; in each aligned block of 8192 rows (0 to 8191, 8192 to 16383, ...) at most 96 rows name the same one
- active_entries_per_part: int32 [128], P(('bx', 'by')), may hold values from 1 to 8192, 786432 in all
- corner_factor_block_index: int32 [4, 1572864], P(None, ('bx', 'by')), may hold values from 0 to 511
- corner_factor_elevation: int32 [4, 1572864], P(None, ('bx', 'by')), may hold values from 0 to 255
- corner_interpolation_factors: float32 [4, 1572864], P(None, ('bx', 'by')), may hold values from 0.1 to 1
- baseline_heat_coefficient: float32 [128, 512, 256], P('bx', 'by'), may hold values from 0.5 to 5
- thermal_state_iterate: float32 [128, 512, 256], P('bx', 'by'), may hold values from -3 to 3
Outputs:
- grid_correction: float32 [128, 512, 256], P('bx', 'by')
- tet_correction: float32 [1048576], P(('bx', 'by'))
Inputs may be any that keep to these rules, and one draw needn't show every extreme that they name: `tetrahedron_destination_block`: among the 8192 rows of one device no brick is named more than 96 times, a bound that some block reaches. `active_entries_per_part`: some device has all 8192 rows live.
All inputs are finite; a program needn't handle non-finite values.
Results may differ from a plain program's by a relative error of at most 0.0003.
Values sent between devices are 32-bit elements; how exact they have to be, the bound alone decides.
No kernel may reach another device: no remote copies, remote signals or barrier semaphores. Data moves between devices by JAX's collectives and lax.ppermute only.
A program may use at most 128 MiB of HBM per device.

v0:
```python
import jax
import jax.numpy as jnp
from jax import lax
from jax.sharding import PartitionSpec as P

LEVELS = 3
NU = 3
CSWEEPS = 8


damping_rate = 0.05
relax_weight = 0.6
link_scale = 1.0 / 52.0
neighbours = [
    (a, b, c) for a in (-1, 0, 1) for b in (-1, 0, 1) for c in (-1, 0, 1) if (a, b, c) != (0, 0, 0)
]


def padded(x, sides, width):
    for axis, dim in sides:
        count, length = (lax.axis_size(axis), x.shape[dim])
        up = [(i, (i + 1) % count) for i in range(count - 1)]
        down = [(j, i) for i, j in up]
        last = lax.slice_in_dim(x, length - width, length, axis=dim)
        leading = lax.slice_in_dim(x, 0, width, axis=dim)
        before = lax.ppermute(last, axis, up)
        after = lax.ppermute(leading, axis, down)
        x = jnp.concatenate([before, x, after], axis=dim)
    return x


def nearby(x, a, b, c, shape_now):
    return x[
        1 + a : 1 + a + shape_now[0], 1 + b : 1 + b + shape_now[1], 1 + c : 1 + c + shape_now[2]
    ]


def operate(field, heat_flux_operator, field_wide, conduct_wide):
    accum = damping_rate * heat_flux_operator * field
    for a, b, c in neighbours:
        accum = accum + link_scale * (
            heat_flux_operator + nearby(conduct_wide, a, b, c, field.shape)
        ) * (field - nearby(field_wide, a, b, c, field.shape))
    return accum


def diagonal_of(heat_flux_operator, conduct_wide):
    accum = damping_rate * heat_flux_operator
    for a, b, c in neighbours:
        accum = accum + link_scale * (
            heat_flux_operator + nearby(conduct_wide, a, b, c, heat_flux_operator.shape)
        )
    return accum


def restrict(x):
    s = x.shape
    return 0.5 * jnp.sum(x.reshape(s[0] // 2, 2, s[1] // 2, 2, s[2] // 2, 2), axis=(1, 3, 5))


def coarsen(x):
    s = x.shape
    return 0.125 * jnp.sum(x.reshape(s[0] // 2, 2, s[1] // 2, 2, s[2] // 2, 2), axis=(1, 3, 5))


def prolong(x):
    return jnp.repeat(jnp.repeat(jnp.repeat(x, 2, axis=0), 2, axis=1), 2, axis=2)


def relax(error_now, source_term, heat_flux_operator, conduct_wide, diag_term, widen):
    return (
        error_now
        + relax_weight
        * (source_term - operate(error_now, heat_flux_operator, widen(error_now), conduct_wide))
        / diag_term
    )


def depth_pad(x):
    return jnp.pad(x, ((0, 0), (0, 0), (1, 1)))


def widen_field(x):
    return depth_pad(padded(x, (("bx", 0), ("by", 1)), 1))


def widen_kappa(x):
    return depth_pad(padded(x, (("bx", 0), ("by", 1)), 1))


def widen_all(x):
    return jnp.pad(x, 1)


def sweeps_from_zero(source_term, heat_flux_operator, widen):
    kappa_wide = widen(heat_flux_operator)
    diag_term = diagonal_of(heat_flux_operator, kappa_wide)
    error_now = relax_weight * source_term / diag_term
    for j in range(CSWEEPS - 1):
        error_now = relax(error_now, source_term, heat_flux_operator, kappa_wide, diag_term, widen)
    return error_now


def assemble(packed, count_x, count_y):
    s = packed.shape
    return (
        packed.reshape(count_x, count_y, s[1], s[2], s[3])
        .transpose(0, 2, 1, 3, 4)
        .reshape(count_x * s[1], count_y * s[2], s[3])
    )


def solve_gathered(source_term, heat_flux_operator):
    count_x = lax.axis_size("bx")
    count_y = lax.axis_size("by")
    packed_source, packed_kappa = (
        lax.all_gather(source_term[None], ("bx", "by"), axis=0, tiled=True),
        lax.all_gather(heat_flux_operator[None], ("bx", "by"), axis=0, tiled=True),
    )
    whole_error = sweeps_from_zero(
        assemble(packed_source, count_x, count_y),
        assemble(packed_kappa, count_x, count_y),
        widen_all,
    )
    s = source_term.shape
    return lax.dynamic_slice(
        whole_error, (lax.axis_index("bx") * s[0], lax.axis_index("by") * s[1], 0), s
    )


def vcycle(source_term, heat_flux_operator, coarse_solve):
    kappas = [heat_flux_operator]
    for i in range(LEVELS):
        kappas.append(coarsen(kappas[-1]))
    saved = []
    for i in range(LEVELS):
        kappa_wide = widen_kappa(kappas[i])
        diag_term = diagonal_of(kappas[i], kappa_wide)
        error_now = relax_weight * source_term / diag_term
        for j in range(NU - 1):
            error_now = relax(error_now, source_term, kappas[i], kappa_wide, diag_term, widen_field)
        leftover = source_term - operate(error_now, kappas[i], widen_field(error_now), kappa_wide)
        saved.append((error_now, source_term, kappa_wide, diag_term))
        source_term = restrict(leftover)
    error_now = coarse_solve(source_term, kappas[LEVELS])
    for i in reversed(range(LEVELS)):
        fine_error, fine_source, kappa_wide, diag_term = saved[i]
        error_now = fine_error + prolong(error_now)
        for j in range(NU):
            error_now = relax(error_now, fine_source, kappas[i], kappa_wide, diag_term, widen_field)
    return error_now


def shards(
    tetrahedron_defect_values,
    tetrahedron_destination_block,
    active_entries_per_part,
    corner_factor_block_index,
    corner_factor_elevation,
    corner_interpolation_factors,
    baseline_heat_coefficient,
    thermal_state_iterate,
):
    count_x = lax.axis_size("bx")
    count_y = lax.axis_size("by")
    devices = count_x * count_y
    row_count = tetrahedron_defect_values.shape[0]
    capacity = corner_interpolation_factors.shape[1] // devices
    target_brick = tetrahedron_destination_block[:, 0]
    positions = jnp.arange(row_count, dtype=jnp.int32)
    is_live = positions < active_entries_per_part[0]
    brick_ids = jnp.arange(devices, dtype=jnp.int32)
    block_rows = min(4096, row_count)
    tile_index = jnp.arange(128, dtype=jnp.int32)
    lower_ones = (tile_index[:, None] >= tile_index[None, :]).astype(jnp.bfloat16)

    def count_step(running, block):
        target_row, live_row = block
        one_hot = ((target_row[:, None] == brick_ids[None, :]) & live_row[:, None]).astype(
            jnp.bfloat16
        )
        tile_hot = one_hot.reshape(block_rows // 128, 128, devices)
        within = jnp.einsum("ij,bjd->bid", lower_ones, tile_hot, preferred_element_type=jnp.float32)
        totals = within[:, -1, :]
        before = jnp.cumsum(totals, axis=0) - totals
        counts = within + before[:, None, :] + running[None, None, :]
        slot_rank = jnp.sum(tile_hot.astype(jnp.float32) * counts, axis=2).reshape(block_rows) - 1.0
        return (running + jnp.sum(totals, axis=0), slot_rank.astype(jnp.int32))

    unused, slot_rank = lax.scan(
        count_step,
        jnp.zeros((devices,), jnp.float32),
        (target_brick.reshape(-1, block_rows), is_live.reshape(-1, block_rows)),
    )
    slot_rank = slot_rank.reshape(row_count)
    target_slot = jnp.where(is_live, target_brick * capacity + slot_rank, devices * capacity)
    outgoing = (
        jnp.zeros((devices * capacity,), jnp.float32)
        .at[target_slot]
        .set(tetrahedron_defect_values, mode="drop")
    )
    incoming = lax.all_to_all(
        outgoing.reshape(devices, capacity), ("bx", "by"), split_axis=0, concat_axis=0, tiled=True
    ).reshape(-1)
    grid_shape = baseline_heat_coefficient.shape
    depth_count = grid_shape[2]
    column_count = grid_shape[0] * grid_shape[1]
    deposits = corner_interpolation_factors * incoming[None, :]
    rhs = (
        jnp.zeros((column_count, depth_count), jnp.float32)
        .at[corner_factor_block_index, corner_factor_elevation]
        .add(deposits)
        .reshape(grid_shape)
    )
    heat_flux_operator = baseline_heat_coefficient * jnp.exp(0.4 * thermal_state_iterate)
    grid_correction = vcycle(rhs, heat_flux_operator, solve_gathered)
    grid_columns = grid_correction.reshape(column_count, depth_count)
    read_back = jnp.sum(
        corner_interpolation_factors
        * grid_columns[corner_factor_block_index, corner_factor_elevation],
        axis=0,
    )
    returned = lax.all_to_all(
        read_back.reshape(devices, capacity), ("bx", "by"), split_axis=0, concat_axis=0, tiled=True
    ).reshape(-1)
    picked = returned[jnp.where(is_live, target_slot, 0)]
    tet_correction = jnp.where(is_live, picked, jnp.zeros_like(picked))
    return (grid_correction, tet_correction)


def solution(mesh):
    placed = (
        P(("bx", "by")),
        P(("bx", "by"), None),
        P(("bx", "by")),
        P(None, ("bx", "by")),
        P(None, ("bx", "by")),
        P(None, ("bx", "by")),
        P("bx", "by", None),
        P("bx", "by", None),
    )
    return jax.shard_map(
        shards,
        mesh=mesh,
        in_specs=placed,
        out_specs=(P("bx", "by", None), P(("bx", "by"))),
        check_vma=False,
    )
```

profile of v0, /device:TPU:1, one launch (start us, length us, event | category | flops | bytes accessed | tf_op | source)
XLA Modules:
  0.0 1458.1 jit_solution(16192130098618220116)
XLA Ops:
  10.4 14.2 while.15
  25.4 30.7 %scatter_custom_fusion = f32[12288]{0:T(1024)S(1)} fusion(s32[8192]{0:T(1024)S(1)} %bitcast.96, f32[8192]{0:T(1024)} %param.10, f32[]{:T(128)} %constant.34.clone.1), kind=kCustom, calls=%fused_computation.2143 | custom fusion | bytes 49664 | tf_op jit(solution)/shard_map/scatter | solution.py:200
  56.8 10.6 all-to-all-start
  78.6 256.4 %scatter_custom_fusion.1 = f32[131072]{0:T(1024)S(1)} fusion(s32[49152]{0:T(1024)S(1)} %bitcast.88, f32[49152]{0:T(1024)S(1)} %bitcast.89, f32[]{:T(128)} %constant.34.clone.1), kind=kCustom, calls=%fused_computation.1467 | custom fusion | flops 49152 | bytes 524292
  345.3 34.8 %reshape.186 = f32[8,2,16,2,128,2]{5,4,3,2,1,0:T(8,128)} reshape(f32[16,32,256]{2,1,0:T(8,128)S(1)} %exponential_multiply_fusion) | data formatting | bytes 1048576 | tf_op jit(solution)/shard_map/reshape | solution.py:63
  380.1 12.2 reduce_sum.88
  443.9 6.4 collective-permute-start.14
  455.7 5.3 fusion.194
  461.0 35.6 %reshape.185 = f32[8,2,16,2,128,2]{5,4,3,2,1,0:T(8,128)} reshape(f32[16,32,256]{2,1,0:T(8,128)} %fusion.194) | data formatting | bytes 1048576 | tf_op jit(solution)/shard_map/reshape | solution.py:58
  496.6 12.8 reduce_sum.87
  517.1 6.3 mul.3454
  531.9 5.2 collective-permute-done.23
  553.3 5.7 collective-permute-start.26
  587.2 6.3 reshape.187
  610.8 5.4 collective-permute-done.39
  626.1 6.3 collective-permute-start.42
  654.3 52.8 %all-gather.1 = f32[256,4,32]{2,1,0:T(4,128)S(1)} all-gather(f32[2,4,32]{2,1,0:T(4,128)S(1)} %broadcast_multiply_fusion.2), channel_id=3, replica_groups=mesh['bx'=8,'by'=16] {'bx','by'}, dimensions={0}, use_global_device_ids=true | all-gather | bytes 132096 | tf_op jit(solution)/shard_map/all_gather | solution.py:118
  718.2 50.5 %all-gather = f32[256,4,32]{2,1,0:T(4,128)S(1)} all-gather(f32[2,4,32]{2,1,0:T(4,128)S(1)} %broadcast_multiply_fusion.3), channel_id=2, replica_groups=mesh['bx'=8,'by'=16] {'bx','by'}, dimensions={0}, use_global_device_ids=true | all-gather | bytes 132096 | tf_op jit(solution)/shard_map/all_gather | solution.py:117
  771.8 7.0 multiply_divide_fusion
  778.8 8.1 fusion.517
  1002.6 387.4 %gather_fusion = f32[49152]{0:T(1024)S(1)} fusion(f32[512,256]{1,0:T(8,128)S(1)} %bitcast.70, s32[49152]{0:T(1024)S(1)} %bitcast.71), kind=kCustom, calls=%fused_computation | custom fusion | bytes 786432 | tf_op jit(solution)/shard_map/gather | solution.py:220
  1390.9 10.0 all-to-all-start.1
  1401.0 9.6 all-to-all-done.1
  1411.5 45.5 %gather_fusion.1 = f32[8192]{0:T(1024)S(1)} fusion(f32[12288]{0:T(1024)S(1)} %reshape.203, s32[8192]{0:T(1024)S(1)} %broadcast_clamp_fusion), kind=kCustom, calls=%fused_computation.1 | custom fusion | bytes 98304 | tf_op jit(solution)/shard_map/gather | solution.py:226
  (475 shorter events, 442.5 us)
Async XLA Ops:
  2.0 66.2 %collective-permute-start = (f32[1,32,256]{2,1,0:T(8,128)S(1)}, f32[1,32,256]{2,1,0:T(8,128)S(1)}, u32[]{:S(2)}, u32[]{:S(2)}) collective-permute-start(f32[1,32,256]{2,1,0:T(8,128)S(1)} %get-tuple-element.173), channel_id=1, source_target_pairs={{0,16},{16,32},{32,48},{48,64},{64,80},{80,96},{96,112},{1,17},{17... | collective-permute-start | bytes 98312 | tf_op jit(solution)/shard_map/ppermute | solution.py:26
  6.5 61.7 %collective-permute-start.1 = (f32[1,32,256]{2,1,0:T(8,128)S(1)}, f32[1,32,256]{2,1,0:T(8,128)S(1)}, u32[]{:S(2)}, u32[]{:S(2)}) collective-permute-start(f32[1,32,256]{2,1,0:T(8,128)S(1)} %get-tuple-element.172), channel_id=1, source_target_pairs={{16,0},{32,16},{48,32},{64,48},{80,64},{96,80},{112,96},{17,1},{33... | collective-permute-start | bytes 98312 | tf_op jit(solution)/shard_map/ppermute | solution.py:27
  56.8 20.1 %all-to-all-start = ((f32[128,1,96]{2,1,0:T(1,128)}), f32[128,1,96]{2,1,0:T(1,128)S(1)}, u32[]{:S(2)}, u32[]{:S(2)}) async-start(f32[128,1,96]{2,1,0:T(1,128)} %bitcast.4), calls=%async_computation | async-start | bytes 131072 | tf_op jit(solution)/shard_map/all_to_all | solution.py:202
  68.2 267.7 %collective-permute-start.2 = (f32[18,1,256]{2,1,0:T(1,128)S(1)}, f32[18,1,256]{2,1,0:T(1,128)S(1)}, u32[]{:S(2)}, u32[]{:S(2)}) collective-permute-start(f32[18,1,256]{2,1,0:T(1,128)S(1)} %get-tuple-element.156), channel_id=1, source_target_pairs={{0,1},{1,2},{2,3},{3,4},{4,5},{5,6},{6,7},{7,8},{8,9},{9,10},{10,1... | collective-permute-start | bytes 55304 | tf_op jit(solution)/shard_map/ppermute | solution.py:26
  71.6 264.3 %collective-permute-start.3 = (f32[18,1,256]{2,1,0:T(1,128)S(1)}, f32[18,1,256]{2,1,0:T(1,128)S(1)}, u32[]{:S(2)}, u32[]{:S(2)}) collective-permute-start(f32[18,1,256]{2,1,0:T(1,128)S(1)} %get-tuple-element.157), channel_id=1, source_target_pairs={{1,0},{2,1},{3,2},{4,3},{5,4},{6,5},{7,6},{8,7},{9,8},{10,9},{11,1... | collective-permute-start | bytes 55304 | tf_op jit(solution)/shard_map/ppermute | solution.py:27
  340.3 52.0 %collective-permute-start.4 = (f32[1,32,256]{2,1,0:T(8,128)S(1)}, f32[1,32,256]{2,1,0:T(8,128)S(1)}, u32[]{:S(2)}, u32[]{:S(2)}) collective-permute-start(f32[1,32,256]{2,1,0:T(8,128)S(1)} %get-tuple-element.170), channel_id=1, source_target_pairs={{0,16},{16,32},{32,48},{48,64},{64,80},{80,96},{96,112},{1,17},{17... | collective-permute-start | bytes 98312 | tf_op jit(solution)/shard_map/ppermute | solution.py:26
  343.4 49.0 %collective-permute-start.5 = (f32[1,32,256]{2,1,0:T(8,128)S(1)}, f32[1,32,256]{2,1,0:T(8,128)S(1)}, u32[]{:S(2)}, u32[]{:S(2)}) collective-permute-start(f32[1,32,256]{2,1,0:T(8,128)S(1)} %get-tuple-element.171), channel_id=1, source_target_pairs={{16,0},{32,16},{48,32},{64,48},{80,64},{96,80},{112,96},{17,1},{33... | collective-permute-start | bytes 98312 | tf_op jit(solution)/shard_map/ppermute | solution.py:27
  406.7 12.6 collective-permute-start.8
  413.7 8.7 collective-permute-start.16
  419.4 9.2 collective-permute-start.10
  422.5 18.1 %collective-permute-start.18 = (f32[10,1,128]{2,1,0:T(1,128)S(1)}, f32[10,1,128]{2,1,0:T(1,128)S(1)}, u32[]{:S(2)}, u32[]{:S(2)}) collective-permute-start(f32[10,1,128]{2,1,0:T(1,128)S(1)} %get-tuple-element.203), channel_id=1, source_target_pairs={{0,1},{1,2},{2,3},{3,4},{4,5},{5,6},{6,7},{7,8},{8,9},{9,10},{10,1... | collective-permute-start | bytes 15368 | tf_op jit(solution)/shard_map/ppermute | solution.py:26
  427.1 13.5 collective-permute-start.19
  512.1 13.9 collective-permute-start.20
  515.2 10.8 collective-permute-start.21
  540.9 12.3 collective-permute-start.24
  547.7 12.7 collective-permute-start.32
  551.3 9.0 collective-permute-start.33
  553.3 12.7 collective-permute-start.26
  560.4 12.7 collective-permute-start.34
  564.7 8.4 collective-permute-start.35
  626.1 11.4 collective-permute-start.42
  648.8 61.4 %collective-permute-start.46 = (f32[6,1,64]{2,1,0:T(1,128)}, f32[6,1,64]{2,1,0:T(1,128)}, u32[]{:S(2)}, u32[]{:S(2)}) collective-permute-start(f32[6,1,64]{2,1,0:T(1,128)} %get-tuple-element.233), channel_id=1, source_target_pairs={{0,1},{1,2},{2,3},{3,4},{4,5},{5,6},{6,7},{7,8},{8,9},{9,10},{10,1... | collective-permute-start | bytes 4616 | tf_op jit(solution)/shard_map/ppermute | solution.py:26
  653.0 57.2 %collective-permute-start.47 = (f32[6,1,64]{2,1,0:T(1,128)}, f32[6,1,64]{2,1,0:T(1,128)}, u32[]{:S(2)}, u32[]{:S(2)}) collective-permute-start(f32[6,1,64]{2,1,0:T(1,128)} %get-tuple-element.234), channel_id=1, source_target_pairs={{1,0},{2,1},{3,2},{4,3},{5,4},{6,5},{7,6},{8,7},{9,8},{10,9},{11,1... | collective-permute-start | bytes 4616 | tf_op jit(solution)/shard_map/ppermute | solution.py:27
  1390.9 19.6 %all-to-all-start.1 = ((f32[128,1,96]{2,1,0:T(1,128)}), f32[128,1,96]{2,1,0:T(1,128)S(1)}, u32[]{:S(2)}, u32[]{:S(2)}) async-start(f32[128,1,96]{2,1,0:T(1,128)} %bitcast.21), calls=%async_computation.1 | async-start | bytes 131072 | tf_op jit(solution)/shard_map/all_to_all | solution.py:223
  (119 other events, 3871.5 us)
where the time goes:
time: 1470 us; the launch traced here: 1460 us
  local copies, waits for them, and re-layouts  588 us (40%)
  other arithmetic  403 us (27%)
  starting transfers between devices  246 us (17%)
  waiting for transfers between devices  104 us (7%)
  blocking collectives  103 us (7%)
    gather x2, local copies, waits for them, and re-layouts, shards(): grid_columns[corner_factor_block_index, corner_factor_elevation]  387 us
    unnamed x8, other arithmetic  258 us
    ppermute x42, starting transfers between devices, padded(): before = lax.ppermute(last, axis, up)  156 us
    ppermute x42, waiting for transfers between devices, padded(): after = lax.ppermute(leading, axis, down)  90.4 us
    ppermute x42, starting transfers between devices, padded(): after = lax.ppermute(leading, axis, down)  68.9 us
    add x22, other arithmetic, relax(): error_now + relax_weight * (source_term - operate(error_now, heat_flux_op...  57.6 us
    all_gather x1, blocking collectives, solve_gathered(): lax.all_gather(heat_flux_operator[None], ('bx', 'by'), axis=0, tiled=True)  52.8 us
    all_gather x1, blocking collectives, solve_gathered(): lax.all_gather(source_term[None], ('bx', 'by'), axis=0, tiled=True)  50.5 us
  transfers between devices with their start and end apart: 86, of which 30 were waited for; matrix products, arithmetic and copies ran while one was open for 26% of the time, Pallas kernels for 0%

commit v1 on v0

v1 whole, which is shorter than its diff:
```python
import functools

import jax
import jax.numpy as jnp
from jax import lax
from jax.experimental import pallas as pl
from jax.experimental.pallas import tpu as pltpu
from jax.sharding import PartitionSpec as P

NX, NY = 8, 16
DEVICES = NX * NY
CAP = 96
ROWS = 8192
SLOTS = DEVICES * CAP
F32 = jnp.float32
BF16 = jnp.bfloat16
VMEM_BYTES = 56 * 1024 * 1024


def iota(shape, dim):
    return lax.broadcasted_iota(jnp.int32, shape, dim)


def pieces(x, count):
    parts = []
    for _ in range(count):
        part = x.astype(BF16)
        parts.append(part)
        x = x - part.astype(F32)
    return parts


def dot(a, b):
    return jnp.dot(a, b, preferred_element_type=F32)


def dot_nt(a, b):
    return lax.dot_general(a, b, (((1,), (1,)), ((), ())), preferred_element_type=F32)


def split_dot(x, m, count=3):
    return sum(dot(p, m) for p in pieces(x, count))


def dot_split(m, x, count=3):
    return sum(dot(m, p) for p in pieces(x, count))


def as_bf16(mask):
    return jnp.where(mask, 1.0, 0.0).astype(BF16)


def pair_rows(coarse, fine):
    return as_bf16(iota((coarse, fine), 1) // 2 == iota((coarse, fine), 0))


def pair_lanes(fine, coarse, at=0):
    return as_bf16(iota((fine, coarse), 0) // 2 + at == iota((fine, coarse), 1))


def rank_kernel(active_ref, dest_ref, value_ref, out_ref, rank_ref, run_ref, acc_ref):
    active = active_ref[0]
    wide = 256
    upper = as_bf16(iota((wide, wide), 0) < iota((wide, wide), 1))
    ones = jnp.ones((wide, wide), BF16)
    bricks = iota((DEVICES, wide), 0)
    ranks = iota((CAP, wide), 0)
    run_ref[...] = jnp.zeros_like(run_ref)
    acc_ref[...] = jnp.zeros_like(acc_ref)

    def step(i, carry):
        def row(ref):
            return jnp.concatenate([ref[pl.ds(2 * i, 1), :], ref[pl.ds(2 * i + 1, 1), :]], axis=1)

        live = i * wide + iota((1, wide), 1) < active
        dest = jnp.where(live, row(dest_ref), -1)
        hot = jnp.where(bricks == dest, 1.0, 0.0)
        hot16 = hot.astype(BF16)
        run = run_ref[...]
        rank = jnp.sum(hot * (dot(hot16, upper) + run), axis=0, keepdims=True).astype(jnp.int32)
        run_ref[...] = run + dot(hot16, ones)
        rank_ref[pl.ds(2 * i, 1), :] = rank[:, :128]
        rank_ref[pl.ds(2 * i + 1, 1), :] = rank[:, 128:]
        value = row(value_ref)
        at = ranks == rank
        total = acc_ref[...]
        for part in pieces(value, 3):
            total = total + dot_nt(hot16, jnp.where(at, part.astype(F32), 0.0).astype(BF16))
        acc_ref[...] = total
        return carry

    lax.fori_loop(0, ROWS // wide, step, 0)
    out_ref[...] = acc_ref[...]


def pick_kernel(active_ref, dest_ref, rank_ref, back_ref, out_ref):
    active = active_ref[0]
    wide = 256
    bricks = iota((DEVICES, wide), 0)
    ranks = iota((CAP, wide), 0)
    table = jnp.transpose(back_ref[...])
    parts = pieces(table, 3)

    def step(i, carry):
        def row(ref):
            return jnp.concatenate([ref[pl.ds(2 * i, 1), :], ref[pl.ds(2 * i + 1, 1), :]], axis=1)

        live = i * wide + iota((1, wide), 1) < active
        dest = jnp.where(live, row(dest_ref), -1)
        hot16 = as_bf16(bricks == dest)
        columns = dot(parts[0], hot16) + dot(parts[1], hot16) + dot(parts[2], hot16)
        picked = jnp.sum(jnp.where(ranks == row(rank_ref), columns, 0.0), axis=0, keepdims=True)
        out_ref[pl.ds(2 * i, 1), :] = picked[:, :128]
        out_ref[pl.ds(2 * i + 1, 1), :] = picked[:, 128:]
        return carry

    lax.fori_loop(0, ROWS // wide, step, 0)


CHUNK = 1024


def deposit_kernel(value_ref, column_ref, depth_ref, factor_ref, rhs_ref, low_ref, high_ref, acc_ref):
    acc_ref[...] = jnp.zeros_like(acc_ref)
    columns = iota((512, CHUNK), 0)
    depths = iota((256, CHUNK), 0)

    def step(i, carry):
        at = pl.ds(pl.multiple_of(i * CHUNK, CHUNK), CHUNK)
        value = value_ref[:, at]
        total = acc_ref[...]
        for k in range(4):
            amount = factor_ref[k : k + 1, at] * value
            hi = amount.astype(BF16).astype(F32)
            lo = amount - hi
            hot = as_bf16(columns == column_ref[k : k + 1, at])
            here = depths == depth_ref[k : k + 1, at]
            spread = jnp.concatenate(
                [jnp.where(here, hi, 0.0).astype(BF16), jnp.where(here, lo, 0.0).astype(BF16)], axis=0
            )
            total = total + dot_nt(hot, spread)
        acc_ref[...] = total
        return carry

    lax.fori_loop(0, SLOTS // CHUNK, step, 0)
    rhs = (acc_ref[:, :256] + acc_ref[:, 256:]).reshape(16, 32, 256)
    rhs_ref[...] = rhs
    low_ref[...] = rhs[:, :8]
    high_ref[...] = rhs[:, 24:]


def box(v, z, depth, rows=None):
    n, m = v.shape
    v = (
        v
        + jnp.where(z == 0, 0.0, pltpu.roll(v, 1, axis=1))
        + jnp.where(z == depth - 1, 0.0, pltpu.roll(v, m - 1, axis=1))
    )
    up, down = pltpu.roll(v, 1, axis=0), pltpu.roll(v, n - 1, axis=0)
    if rows is not None:
        up = jnp.where(rows == 0, 0.0, up)
        down = jnp.where(rows == n - 1, 0.0, down)
    return v + up + down


def near(ref, x):
    return ref[x - 1] + ref[x] + ref[x + 1]


def flow(e, c, q, x, boxed):
    return q[x] * boxed(near(e, x)) + boxed(near(c, x)) - 2.0 * c[x]


def set_weights(q, w, diag, lo, hi, boxed):
    def body(x, carry):
        here = q[x]
        d = 27.6 * here + boxed(near(q, x))
        w[x] = jnp.where(here > 0.0, 0.6 / d, 0.0)
        if diag is not None:
            diag[x] = d
        return carry

    lax.fori_loop(lo, hi, body, 0)


def first_guess(e, c, q, w, r, lo, hi):
    def body(x, carry):
        first = w[x] * r[x]
        e[x] = first
        c[x] = q[x] * first
        return carry

    lax.fori_loop(lo, hi, body, 0)


def sweep(e, c, e2, c2, q, w, r, lo, hi, boxed):
    def body(x, carry):
        new = 0.4 * e[x] + w[x] * (r[x] + flow(e, c, q, x, boxed))
        e2[x] = new
        if c2 is not None:
            c2[x] = q[x] * new
        return carry

    lax.fori_loop(lo, hi, body, 0)


def pack_two(pairs):
    both = dot_split(pair_rows(32, 64), pairs.reshape(64, 128))
    return split_dot(both[:16], pair_lanes(128, 128)) + split_dot(both[16:], pair_lanes(128, 128, 64))


def halve(pairs):
    thin = split_dot(pairs.reshape(256, 256), pair_lanes(256, 128))
    return dot_split(pair_rows(128, 256), thin)


def kappa_kernel(base_ref, state_ref, q_ref, q1_ref, low_ref, high_ref, q2_ref):
    q = base_ref[...] * jnp.exp(0.4 * state_ref[...]) * (1.0 / 52.0)
    q_ref[...] = q
    q1 = 0.125 * halve(jnp.sum(q.reshape(8, 2, 32, 256), axis=1)).reshape(8, 16, 128)
    packed = jnp.concatenate([q1[:4], q1[4:]], axis=2)
    q1_ref[...] = packed
    low_ref[0:16] = q[:, :8]
    high_ref[0:16] = q[:, 24:]
    low_ref[16:20] = packed[:, :8]
    high_ref[16:20] = packed[:, 8:]
    q2_ref[...] = 0.125 * pack_two(jnp.sum(q1.reshape(4, 2, 16, 128), axis=1))


def down_kernel(
    q_own, q_ylo, q_yhi, q_xlo, q_xhi, r_own, r_ylo, r_yhi, r_xlo, r_xhi,
    q, w, r, e, r1_ref, low_ref, high_ref,
    c, e2, c2, diag, pairs,
):
    z = iota((48, 256), 1)
    boxed = functools.partial(box, z=z, depth=256)
    q[0:6] = q_xlo[0:6]
    q[22:28] = q_xhi[0:6]
    q[6:22, 0:8] = q_ylo[0:16]
    q[6:22, 8:40] = q_own[...]
    q[6:22, 40:48] = q_yhi[0:16]
    r[1:6] = r_xlo[...]
    r[22:27] = r_xhi[...]
    r[6:22, 0:8] = r_ylo[...]
    r[6:22, 8:40] = r_own[...]
    r[6:22, 40:48] = r_yhi[...]
    set_weights(q, w, diag, 1, 27, boxed)
    first_guess(e, c, q, w, r, 1, 27)
    sweep(e, c, e2, c2, q, w, r, 2, 26, boxed)
    sweep(e2, c2, e, c, q, w, r, 3, 25, boxed)

    def left(x):
        return (r[x] + flow(e, c, q, x, boxed) - diag[x] * e[x])[8:40]

    def body(i, carry):
        pairs[i] = left(6 + 2 * i) + left(7 + 2 * i)
        return carry

    lax.fori_loop(0, 8, body, 0)
    r1 = 0.5 * halve(pairs[...]).reshape(8, 16, 128)
    r1_ref[...] = r1
    low_ref[...] = r1[:, :8]
    high_ref[...] = r1[:, 8:]


def unpack_one(packed):
    return jnp.concatenate([packed[..., :128], packed[..., 128:]], axis=0)


def down_one_kernel(
    q_own, q_ylo, q_yhi, q_xlo, q_xhi, r_cat, r_xlo, r_xhi,
    q, w, r, e, out_ref,
    c, e2, c2, diag, pairs,
):
    z = iota((32, 128), 1)
    boxed = functools.partial(box, z=z, depth=128)
    q[0:8] = unpack_one(q_xlo[6:10, 0:32])
    q[16:24] = unpack_one(q_xhi[6:10, 0:32])
    q[8:16, 0:8] = unpack_one(q_ylo[16:20])
    q[8:16, 8:24] = unpack_one(q_own[...])
    q[8:16, 24:32] = unpack_one(q_yhi[16:20])
    r[0:8] = r_xlo[...]
    r[8:16] = r_cat[...]
    r[16:24] = r_xhi[...]
    set_weights(q, w, diag, 1, 23, boxed)
    first_guess(e, c, q, w, r, 1, 23)
    sweep(e, c, e2, c2, q, w, r, 2, 22, boxed)
    sweep(e2, c2, e, c, q, w, r, 3, 21, boxed)

    def left(x):
        return (r[x] + flow(e, c, q, x, boxed) - diag[x] * e[x])[8:24]

    def body(i, carry):
        pairs[i] = left(8 + 2 * i) + left(9 + 2 * i)
        return carry

    lax.fori_loop(0, 4, body, 0)
    r2 = 0.5 * pack_two(pairs[...])
    out_ref[...] = jnp.broadcast_to(r2[None], (DEVICES, 16, 128))


def ghosts(ref, count, group):
    lane = iota(ref.shape[1:], 1)
    ref[0] = jnp.where(lane >= group, pltpu.roll(ref[count], group, axis=1), 0.0)
    ref[count + 1] = jnp.where(lane < 128 - group, pltpu.roll(ref[1], 128 - group, axis=1), 0.0)


def assemble_two(gathered, ref):
    lane = iota((8, 128), 1)
    for bx in range(4):
        for by in range(NY):
            for j in range(2):
                a = gathered[bx * NY + by, j * 8 : j * 8 + 8]
                b = gathered[(bx + 4) * NY + by, j * 8 : j * 8 + 8]
                rows = slice(by * 8, by * 8 + 8)
                ref[1 + bx * 4 + j, rows] = jnp.where(lane < 64, a, pltpu.roll(b, 64, axis=1))
                ref[1 + bx * 4 + 2 + j, rows] = jnp.where(lane < 64, pltpu.roll(a, 64, axis=1), b)


def up_kernel(
    place_ref, r2_all, q2_all, q1, w1, r1, e1, q0, w0, r0, e0,
    column_ref, depth_ref, factor_ref,
    grid_ref, back_ref,
    q2, w2, d2, r2, a2, ca2, b2, cb2,
    q3, w3, r3, a3, ca3, b3, cb3,
    last2, s1, c1, t1, ct1, s0, c0, t0, ct0, hi_ref, lo_ref,
):
    bx, by = place_ref[0], place_ref[1]
    z2 = iota((128, 128), 1) % 64
    rows2 = iota((128, 128), 0)
    boxed2 = functools.partial(box, z=z2, depth=64, rows=rows2)
    assemble_two(q2_all, q2)
    assemble_two(r2_all, r2)
    ghosts(q2, 16, 64)
    set_weights(q2, w2, d2, 1, 17, boxed2)
    first_guess(a2, ca2, q2, w2, r2, 1, 17)

    def sweep2(e, c, e_to, c_to):
        ghosts(e, 16, 64)
        ghosts(c, 16, 64)
        sweep(e, c, e_to, c_to, q2, w2, r2, 1, 17, boxed2)

    sweep2(a2, ca2, b2, cb2)
    sweep2(b2, cb2, a2, ca2)
    ghosts(a2, 16, 64)
    ghosts(ca2, 16, 64)
    lanes_low, lanes_high = pair_lanes(128, 128), None
    src, dst = iota((128, 128), 0), iota((128, 128), 1)
    lane_maps = [as_bf16(src // 64 * 64 + at + src % 64 // 2 == dst) for at in (0, 32)]
    rows_half = pair_rows(64, 128)

    def left(x):
        return r2[x] + flow(a2, ca2, q2, x, boxed2) - d2[x] * a2[x]

    def coarse_plane(low, high):
        return dot_split(rows_half, split_dot(low, lane_maps[0]) + split_dot(high, lane_maps[1]))

    for x in range(4):
        r3[1 + x] = 0.5 * coarse_plane(
            left(1 + 2 * x) + left(2 + 2 * x), left(9 + 2 * x) + left(10 + 2 * x)
        )
        q3[1 + x] = 0.125 * coarse_plane(
            q2[1 + 2 * x] + q2[2 + 2 * x], q2[9 + 2 * x] + q2[10 + 2 * x]
        )
    z3 = iota((64, 128), 1) % 32
    rows3 = iota((64, 128), 0)
    boxed3 = functools.partial(box, z=z3, depth=32, rows=rows3)
    ghosts(q3, 4, 32)
    set_weights(q3, w3, None, 1, 5, boxed3)
    first_guess(a3, ca3, q3, w3, r3, 1, 5)
    now, later = (a3, ca3), (b3, cb3)
    for _ in range(7):
        ghosts(now[0], 4, 32)
        ghosts(now[1], 4, 32)
        sweep(*now, *later, q3, w3, r3, 1, 5, boxed3)
        now, later = later, now
    e3 = now[0]
    src, dst = iota((128, 128), 1), iota((128, 128), 0)
    lane_back = [as_bf16(src // 64 * 64 + at + src % 64 // 2 == dst) for at in (0, 32)]
    rows_double = as_bf16(iota((128, 64), 0) // 2 == iota((128, 64), 1))
    for x in range(8):
        more = dot_split(rows_double, split_dot(e3[1 + x % 4], lane_back[x // 4]))
        for j in (1 + 2 * x, 2 + 2 * x):
            new = a2[j] + more
            a2[j] = new
            ca2[j] = q2[j] * new
    sweep2(a2, ca2, b2, cb2)
    sweep2(b2, cb2, a2, ca2)
    ghosts(a2, 16, 64)
    ghosts(ca2, 16, 64)
    last2[:, 0:8] = jnp.zeros((16, 8, 128), F32)
    last2[:, 136:144] = jnp.zeros((16, 8, 128), F32)

    def final2(x, carry):
        last2[x - 1, 8:136] = 0.4 * a2[x] + w2[x] * (r2[x] + flow(a2, ca2, q2, x, boxed2))
        return carry

    lax.fori_loop(1, 17, final2, 0)
    z1 = iota((32, 128), 1)
    boxed1 = functools.partial(box, z=z1, depth=128)
    widen_lanes = as_bf16(iota((128, 128), 1) // 2 == iota((128, 128), 0))
    widen_rows = as_bf16((iota((32, 24), 0) + 8) // 2 == iota((32, 24), 1))
    for j in range(10):
        x = bx * 4 - 3 + j
        inside = jnp.logical_and(x >= 0, x < 32)
        at = jnp.clip(x, 0, 31)
        window = last2[lax.rem(at, 16), pl.ds(pl.multiple_of(by * 8, 8), 24), :]
        window = jnp.where(at >= 16, pltpu.roll(window, 64, axis=1), window)
        window = jnp.where(inside, window, 0.0)
        more = dot_split(widen_rows, split_dot(window, widen_lanes))
        for p in (2 * j + 2, 2 * j + 3):
            if 3 <= p < 21:
                new = e1[p] + more
                s1[p] = new
                c1[p] = q1[p] * new
    sweep(s1, c1, t1, ct1, q1, w1, r1, 4, 20, boxed1)
    sweep(t1, ct1, s1, c1, q1, w1, r1, 5, 19, boxed1)
    sweep(s1, c1, t1, None, q1, w1, r1, 6, 18, boxed1)
    z0 = iota((48, 256), 1)
    boxed0 = functools.partial(box, z=z0, depth=256)
    wide_lanes = as_bf16(iota((128, 256), 1) // 2 == iota((128, 256), 0))
    wide_rows = as_bf16((iota((48, 32), 0) + 8) // 2 == iota((48, 32), 1))

    def widen(j, carry):
        more = dot_split(wide_rows, split_dot(t1[6 + j], wide_lanes))
        for p in (2 * j + 2, 2 * j + 3):
            new = e0[p] + more
            s0[p] = new
            c0[p] = q0[p] * new
        return carry

    lax.fori_loop(0, 12, widen, 0)
    sweep(s0, c0, t0, ct0, q0, w0, r0, 4, 24, boxed0)
    sweep(t0, ct0, s0, c0, q0, w0, r0, 5, 23, boxed0)

    def final0(x, carry):
        new = 0.4 * s0[x] + w0[x] * (r0[x] + flow(s0, c0, q0, x, boxed0))
        grid_ref[x - 6] = new[8:40]
        return carry

    lax.fori_loop(6, 22, final0, 0)
    grid = jnp.transpose(grid_ref[...].reshape(512, 256))
    hi, lo = pieces(grid, 2)
    hi_ref[...] = hi
    lo_ref[...] = lo
    columns = iota((512, CHUNK), 0)
    depths = iota((256, CHUNK), 0)

    def step(i, carry):
        at = pl.ds(pl.multiple_of(i * CHUNK, CHUNK), CHUNK)
        total = jnp.zeros((1, CHUNK), F32)
        for k in range(4):
            hot = as_bf16(columns == column_ref[k : k + 1, at])
            found = dot(hi_ref[...], hot) + dot(lo_ref[...], hot)
            here = depths == depth_ref[k : k + 1, at]
            picked = jnp.sum(jnp.where(here, found, 0.0), axis=0, keepdims=True)
            total = total + factor_ref[k : k + 1, at] * picked
        back_ref[:, at] = total
        return carry

    lax.fori_loop(0, SLOTS // CHUNK, step, 0)


def struct(*shape, dtype=F32):
    return jax.ShapeDtypeStruct(shape, dtype)


def call(kernel, outs, *args, smem=0, scratch=()):
    vmem = pl.BlockSpec(memory_space=pltpu.VMEM)
    return pl.pallas_call(
        kernel,
        out_shape=outs,
        in_specs=[pl.BlockSpec(memory_space=pltpu.SMEM)] * smem + [vmem] * (len(args) - smem),
        out_specs=tuple(vmem for _ in outs),
        scratch_shapes=[pltpu.VMEM(s, d) for s, d in scratch],
        compiler_params=pltpu.CompilerParams(vmem_limit_bytes=VMEM_BYTES),
    )(*args)


def swap(to_lower, to_upper, axis, count):
    up = [(i, i + 1) for i in range(count - 1)]
    down = [(j, i) for i, j in up]
    return lax.ppermute(to_upper, axis, up), lax.ppermute(to_lower, axis, down)


def shards(values, dest, active, column, depth, factor, base, state):
    dest = dest.reshape(64, 128)
    outgoing, rank = call(
        rank_kernel,
        (struct(DEVICES, CAP), struct(64, 128, dtype=jnp.int32)),
        active, dest, values.reshape(64, 128),
        smem=1, scratch=(((DEVICES, 256), F32), ((DEVICES, CAP), F32)),
    )
    incoming = lax.all_to_all(outgoing, ("bx", "by"), split_axis=0, concat_axis=0, tiled=True)

    q, q1, q_low, q_high, q2 = call(
        kappa_kernel,
        (struct(16, 32, 256), struct(4, 16, 256), struct(20, 8, 256), struct(20, 8, 256), struct(16, 128)),
        base, state,
    )
    q2_all = lax.all_gather(q2[None], ("bx", "by"), axis=0, tiled=True)
    q_ylo, q_yhi = swap(q_low, q_high, "by", NY)
    q1_cat = jnp.pad(jnp.concatenate([q_ylo[16:], q1, q_yhi[16:]], axis=1), ((0, 0), (0, 16), (0, 0)))

    def faces(lo, own, hi, planes, extra=None):
        cat = jnp.concatenate([lo[planes], own[planes], hi[planes]], axis=1)
        return cat if extra is None else jnp.concatenate([cat, extra], axis=0)

    q_xlo, q_xhi = swap(
        faces(q_ylo, q, q_yhi, slice(0, 6), q1_cat), faces(q_ylo, q, q_yhi, slice(10, 16), q1_cat), "bx", NX
    )

    rhs, r_low, r_high = call(
        deposit_kernel,
        (struct(16, 32, 256), struct(16, 8, 256), struct(16, 8, 256)),
        incoming.reshape(1, SLOTS), column, depth, factor,
        scratch=(((512, 512), F32),),
    )
    r_ylo, r_yhi = swap(r_low, r_high, "by", NY)
    r_xlo, r_xhi = swap(
        faces(r_ylo, rhs, r_yhi, slice(0, 5)), faces(r_ylo, rhs, r_yhi, slice(11, 16)), "bx", NX
    )

    ext0, ext1 = (28, 48, 256), (24, 32, 128)
    q0e, w0e, r0e, e0e, r1, low1, high1 = call(
        down_kernel,
        (struct(*ext0),) * 4 + (struct(8, 16, 128), struct(8, 8, 128), struct(8, 8, 128)),
        q, q_ylo, q_yhi, q_xlo, q_xhi, rhs, r_ylo, r_yhi, r_xlo, r_xhi,
        scratch=((ext0, F32),) * 4 + (((8, 32, 256), F32),),
    )
    r1_ylo, r1_yhi = swap(low1, high1, "by", NY)
    r1_cat = jnp.concatenate([r1_ylo, r1, r1_yhi], axis=1)
    r1_xlo, r1_xhi = swap(r1_cat, r1_cat, "bx", NX)

    q1e, w1e, r1e, e1e, r2_out = call(
        down_one_kernel,
        (struct(*ext1),) * 4 + (struct(DEVICES, 16, 128),),
        q1, q_ylo, q_yhi, q_xlo, q_xhi, r1_cat, r1_xlo, r1_xhi,
        scratch=((ext1, F32),) * 4 + (((4, 16, 128), F32),),
    )
    r2_all = lax.all_to_all(r2_out, ("bx", "by"), split_axis=0, concat_axis=0, tiled=True)

    place = jnp.stack([lax.axis_index("bx"), lax.axis_index("by")]).astype(jnp.int32)
    whole2, whole3 = (18, 128, 128), (6, 64, 128)
    grid, back = call(
        up_kernel,
        (struct(16, 32, 256), struct(1, SLOTS)),
        place, r2_all, q2_all, q1e, w1e, r1e, e1e, q0e, w0e, r0e, e0e, column, depth, factor,
        smem=1,
        scratch=((whole2, F32),) * 8
        + ((whole3, F32),) * 7
        + (((16, 144, 128), F32),)
        + ((ext1, F32),) * 4
        + ((ext0, F32),) * 4
        + (((256, 512), BF16),) * 2,
    )
    returned = lax.all_to_all(
        back.reshape(DEVICES, CAP), ("bx", "by"), split_axis=0, concat_axis=0, tiled=True
    )
    (picked,) = call(pick_kernel, (struct(64, 128),), active, dest, rank, returned, smem=1)
    return grid, picked.reshape(ROWS)


def solution(mesh):
    placed = (
        P(("bx", "by")),
        P(("bx", "by"), None),
        P(("bx", "by")),
        P(None, ("bx", "by")),
        P(None, ("bx", "by")),
        P(None, ("bx", "by")),
        P("bx", "by", None),
        P("bx", "by", None),
    )
    return jax.shard_map(
        shards,
        mesh=mesh,
        in_specs=placed,
        out_specs=(P("bx", "by", None), P(("bx", "by"))),
        check_vma=False,
    )
```

time: 1470 us -> 303 us (0.21)
  local copies, waits for them, and re-layouts: 588 us -> 7.65 us
  other arithmetic: 403 us -> 2.93 us
  starting transfers between devices: 246 us -> 52.2 us
  Pallas kernels: 0 us -> 169 us
  blocking collectives: 103 us -> 14.5 us
  waiting for transfers between devices: 104 us -> 40.4 us
    gather x3 -> x0, local copies, waits for them, and re-layouts: 433 us -> none  [the longest x2 387 us: shards(): grid_columns[corner_factor_block_index, corner_factor_elevation]]
    unnamed x8 -> x0, other arithmetic: 258 us -> none
    ppermute x84 -> x12, starting transfers between devices: 225 us -> 30.9 us  [the longest x6 21.2 us: swap(): lax.ppermute(to_upper, axis, up)]
    pallas_call x0 -> x7, Pallas kernels: none -> 169 us  [call(): pl.pallas_call(kernel, out_shape=outs, in_specs=[pl.BlockSpec(memory_spac...]
    all_gather x2 -> x0, blocking collectives: 103 us -> none  [the longest x1 52.8 us: solve_gathered(): lax.all_gather(heat_flux_operator[None], ('bx', 'by'), axis=0, tiled=True)]
    reshape x14 -> x1, local copies, waits for them, and re-layouts: 96 us -> 0.74 us  [shards(): incoming.reshape(1, SLOTS)]
    ppermute x84 -> x12, waiting for transfers between devices: 90.5 us -> 13.7 us  [the longest x6 11.8 us: swap(): lax.ppermute(to_lower, axis, down)]
    add x28 -> x0, other arithmetic: 64.5 us -> none  [the longest x22 57.6 us: relax(): error_now + relax_weight * (source_term - operate(error_now, heat_flux_op...]
  transfers between devices with their start and end apart: 86 -> 15, of which waited for: 30 -> 6; matrix products, arithmetic and copies ran while one was open for 26% -> 2% of each run, Pallas kernels for 0% -> 24%
where the time goes in v1:
time: 303 us; the launch traced here: 302 us
  Pallas kernels  169 us (56%)
  starting transfers between devices  52.2 us (17%)
  waiting for transfers between devices  40.4 us (13%)
  between operations  15 us (5%)
  blocking collectives  14.5 us (5%)
  local copies, waits for them, and re-layouts  7.65 us (3%)
    pallas_call x7, Pallas kernels, call(): pl.pallas_call(kernel, out_shape=outs, in_specs=[pl.BlockSpec(memory_spac...  169 us
    ppermute x6, starting transfers between devices, swap(): lax.ppermute(to_upper, axis, up)  21.2 us
    all_to_all x1, waiting for transfers between devices, shards(): lax.all_to_all(r2_out, ('bx', 'by'), split_axis=0, concat_axis=0, tiled=T...  18.3 us
    all_to_all x1, blocking collectives, shards(): lax.all_to_all(back.reshape(DEVICES, CAP), ('bx', 'by'), split_axis=0, co...  14.5 us
    ppermute x6, waiting for transfers between devices, swap(): lax.ppermute(to_lower, axis, down)  11.8 us
    all_to_all x1, starting transfers between devices, shards(): lax.all_to_all(outgoing, ('bx', 'by'), split_axis=0, concat_axis=0, tiled...  11.7 us
    ppermute x6, starting transfers between devices, swap(): lax.ppermute(to_lower, axis, down)  9.64 us
    all_to_all x1, starting transfers between devices, shards(): lax.all_to_all(r2_out, ('bx', 'by'), split_axis=0, concat_axis=0, tiled=T...  9.63 us
  transfers between devices with their start and end apart: 15, of which 6 were waited for; matrix products, arithmetic and copies ran while one was open for 2% of the time, Pallas kernels for 24%

profile of v1, /device:TPU:1, one launch (start us, length us, event | category | flops | bytes accessed | tf_op | source)
XLA Modules:
  0.0 301.8 jit_solution(3048633951644787356)
XLA Ops:
  7.2 2.7 shard_map.95
  9.9 4.5 %collective-permute-start = (f32[20,8,256]{2,1,0:T(8,128)}, f32[20,8,256]{2,1,0:T(8,128)S(1)}, u32[]{:S(2)}, u32[]{:S(2)}) collective-permute-start(f32[20,8,256]{2,1,0:T(8,128)} %get-tuple-element.27), channel_id=1, source_target_pairs={{0,1},{1,2},{2,3},{3,4},{4,5},{5,6},{6,7},{7,8},{8,9},{9,10},{10,1... | collective-permute-start | bytes 491528 | tf_op jit(solution)/shard_map/ppermute | solution.py:483
  16.3 15.2 %shard_map.96 = (f32[128,96]{1,0:T(8,128)}, s32[64,128]{1,0:T(8,128)}) custom-call(s32[1]{0:T(128)S(6)} %copy.14.active_ref, s32[64,128]{1,0:T(8,128)} %bitcast.14, f32[64,128]{1,0:T(8,128)} %bitcast.18), custom_call_target="tpu_custom_call" | custom-call | tf_op jit(solution)/shard_map/pallas_call | solution.py:470
  31.5 11.7 %all-to-all-start = ((f32[128,1,96]{2,1,0:T(1,128)}), f32[128,1,96]{2,1,0:T(1,128)S(1)}, u32[]{:S(2)}, u32[]{:S(2)}) async-start(f32[128,1,96]{2,1,0:T(1,128)} %bitcast.16), calls=%async_computation | async-start | bytes 131072 | tf_op jit(solution)/shard_map/all_to_all | solution.py:494
  45.0 7.8 %all-to-all-done = f32[128,1,96]{2,1,0:T(1,128)S(1)} async-done(((f32[128,1,96]{2,1,0:T(1,128)}), f32[128,1,96]{2,1,0:T(1,128)S(1)}, u32[]{:S(2)}, u32[]{:S(2)}) %all-to-all-start) | async-done | bytes 49184 | tf_op jit(solution)/shard_map/all_to_all | solution.py:494
  54.7 31.0 %shard_map.97 = (f32[16,32,256]{2,1,0:T(8,128)}, f32[16,8,256]{2,1,0:T(8,128)}, f32[16,8,256]{2,1,0:T(8,128)}) custom-call(f32[1,12288]{1,0:T(1,128)} %reshape.25.value_ref, s32[4,12288]{1,0:T(4,128)} %column_ref.3, s32[4,12288]{1,0:T(4,128)} %depth_ref.3, f32[4,12288]{1,0:T(4,128)} %factor_ref.3), custom_call_target="tpu_custom_call" | custom-call | tf_op jit(solution)/shard_map/pallas_call | solution.py:470
  85.7 2.5 collective-permute-start.4
  90.7 3.3 %collective-permute-start.2 = (f32[10,48,256]{2,1,0:T(8,128)S(1)}, f32[10,48,256]{2,1,0:T(8,128)S(1)}, u32[]{:S(2)}, u32[]{:S(2)}) collective-permute-start(f32[10,48,256]{2,1,0:T(8,128)S(1)} %get-tuple-element.55), channel_id=1, source_target_pairs={{0,16},{16,32},{32,48},{48,64},{64,80},{80,96},{96,112},{1,17},{17... | collective-permute-start | bytes 1474568 | tf_op jit(solution)/shard_map/ppermute | solution.py:483
  94.1 1.9 collective-permute-start.3
  96.1 3.6 %collective-permute-start.6 = (f32[5,48,256]{2,1,0:T(8,128)S(1)}, f32[5,48,256]{2,1,0:T(8,128)S(1)}, u32[]{:S(2)}, u32[]{:S(2)}) collective-permute-start(f32[5,48,256]{2,1,0:T(8,128)S(1)} %pad_maximum_fusion.2), channel_id=1, source_target_pairs={{0,16},{16,32},{32,48},{48,64},{64,80},{80,96},{96,112},{1,17},{17... | collective-permute-start | bytes 737288 | tf_op jit(solution)/shard_map/ppermute | solution.py:483
  99.8 1.9 collective-permute-start.7
  103.5 4.8 %collective-permute-done.7.r_xhi = f32[5,48,256]{2,1,0:T(8,128)S(1)} collective-permute-done((f32[5,48,256]{2,1,0:T(8,128)S(1)}, f32[5,48,256]{2,1,0:T(8,128)S(1)}, u32[]{:S(2)}, u32[]{:S(2)}) %collective-permute-start.7) | collective-permute-done | bytes 245792 | tf_op jit(solution)/shard_map/ppermute | solution.py:483
  110.1 15.9 %shard_map.98 = (f32[28,48,256]{2,1,0:T(8,128)}, f32[28,48,256]{2,1,0:T(8,128)}, f32[28,48,256]{2,1,0:T(8,128)}, f32[28,48,256]{2,1,0:T(8,128)}, f32[8,16,128]{2...) custom-call(f32[16,32,256]{2,1,0:T(8,128)} %get-tuple-element.29.q_own, f32[20,8,256]{2,1,0:T(8,128)} %copy-done.3, ...), custom_call_target="tpu_custom_call" | custom-call | tf_op jit(solution)/shard_map/pallas_call | solution.py:470
  126.0 4.3 %collective-permute-start.8 = (f32[8,8,128]{2,1,0:T(8,128)}, f32[8,8,128]{2,1,0:T(8,128)S(1)}, u32[]{:S(2)}, u32[]{:S(2)}) collective-permute-start(f32[8,8,128]{2,1,0:T(8,128)} %get-tuple-element.34), channel_id=1, source_target_pairs={{0,1},{1,2},{2,3},{3,4},{4,5},{5,6},{6,7},{7,8},{8,9},{9,10},{10,1... | collective-permute-start | bytes 98312 | tf_op jit(solution)/shard_map/ppermute | solution.py:483
  132.4 2.7 collective-permute-done.9
  135.1 3.1 %collective-permute-start.10 = (f32[8,32,128]{2,1,0:T(8,128)S(1)}, f32[8,32,128]{2,1,0:T(8,128)S(1)}, u32[]{:S(2)}, u32[]{:S(2)}) collective-permute-start(f32[8,32,128]{2,1,0:T(8,128)S(1)} %constant_dynamic-update-slice_fusion.r_cat), channel_id=1, source_target_pairs={{0,16},{16,32},{32,48},{48,64},{64,80},{80,96},{96,112},{1,17},{17... | collective-permute-start | bytes 393224 | tf_op jit(solution)/shard_map/ppermute | solution.py:483
  138.2 1.9 collective-permute-start.11
  140.1 4.3 %collective-permute-done.11.r_xhi = f32[8,32,128]{2,1,0:T(8,128)S(1)} collective-permute-done((f32[8,32,128]{2,1,0:T(8,128)S(1)}, f32[8,32,128]{2,1,0:T(8,128)S(1)}, u32[]{:S(2)}, u32[]{:S(2)}) %collective-permute-start.11) | collective-permute-done | bytes 131104 | tf_op jit(solution)/shard_map/ppermute | solution.py:483
  145.1 9.2 %shard_map.99 = (f32[24,32,128]{2,1,0:T(8,128)}, f32[24,32,128]{2,1,0:T(8,128)}, f32[24,32,128]{2,1,0:T(8,128)}, f32[24,32,128]{2,1,0:T(8,128)}, f32[128,16,128]{2,1,0:T(8,128)}) custom-call(f32[4,16,256]{2,1,0:T(8,128)} %get-tuple-element.26.q_own, f32[20,8,256]{2,1,0:T(8,128)} %copy-done.3, f32[20,8,256]{2,1,0:T(8,128)} %copy-done.4, ...), custom_call_target="tpu_custom_call" | custom-call | tf_op jit(solution)/shard_map/pallas_call | solution.py:470
  154.3 9.6 %all-to-all-start.1 = ((f32[128,16,128]{2,1,0:T(8,128)}), f32[128,16,128]{2,1,0:T(8,128)S(1)}, u32[]{:S(2)}, u32[]{:S(2)}) async-start(f32[128,16,128]{2,1,0:T(8,128)} %get-tuple-element.37), calls=%async_computation.1 | async-start | bytes 2097152 | tf_op jit(solution)/shard_map/all_to_all | solution.py:541
  164.5 18.3 %all-to-all-done.1.r2_all = f32[128,16,128]{2,1,0:T(8,128)S(1)} async-done(((f32[128,16,128]{2,1,0:T(8,128)}), f32[128,16,128]{2,1,0:T(8,128)S(1)}, u32[]{:S(2)}, u32[]{:S(2)}) %all-to-all-start.1) | async-done | bytes 1048608 | tf_op jit(solution)/shard_map/all_to_all | solution.py:541
  183.8 86.9 %shard_map.100 = (f32[16,32,256]{2,1,0:T(8,128)}, f32[1,12288]{1,0:T(1,128)}) custom-call(s32[2]{0:T(128)} %pad_add_fusion.place_ref, f32[128,16,128]{2,1,0:T(8,128)} %copy-done, f32[128,16,128]{2,1,0:T(8,128)} %bitcast.11, f32[24,32,128]{2,1,0:T(8,128)} %get-tuple-element.39.q1, f32[24,32,128]{2,1,0:T(8,128)} %get-tuple-element.40.w1, ...), custom_call_target="tpu_custom_call" | custom-call | tf_op jit(solution)/shard_map/pallas_call | solution.py:470
  272.3 14.5 %all_to_all.25 = f32[128,1,96]{2,1,0:T(1,128)} all-to-all(f32[128,1,96]{2,1,0:T(1,128)S(1)} %bitcast.12), channel_id=1, replica_groups=mesh['bx'=8,'by'=16] {'bx','by'}, dimensions={0} | all-to-all | bytes 98304 | tf_op jit(solution)/shard_map/all_to_all | solution.py:557
  286.8 8.1 %shard_map.101 = f32[64,128]{1,0:T(8,128)} custom-call(s32[1]{0:T(128)S(6)} %copy.14.active_ref, s32[64,128]{1,0:T(8,128)} %bitcast.15, s32[64,128]{1,0:T(8,128)} %get-tuple-element.48.rank_ref, f32[128,96]{1,0:T(8,128)} %bitcast.13), custom_call_target="tpu_custom_call" | custom-call | tf_op jit(solution)/shard_map/pallas_call | solution.py:470
  (62 shorter events, 17.0 us)
Async XLA Ops:
  9.9 80.7 %copy-start.7 = (f32[4,16,256]{2,1,0:T(8,128)S(1)}, f32[4,16,256]{2,1,0:T(8,128)}, u32[]{:S(2)}) copy-start(f32[4,16,256]{2,1,0:T(8,128)} %get-tuple-element.26.q_own) | copy-start | bytes 196612
  9.9 80.7 %collective-permute-start = (f32[20,8,256]{2,1,0:T(8,128)}, f32[20,8,256]{2,1,0:T(8,128)S(1)}, u32[]{:S(2)}, u32[]{:S(2)}) collective-permute-start(f32[20,8,256]{2,1,0:T(8,128)} %get-tuple-element.27), channel_id=1, source_target_pairs={{0,1},{1,2},{2,3},{3,4},{4,5},{5,6},{6,7},{7,8},{8,9},{9,10},{10,1... | collective-permute-start | bytes 491528 | tf_op jit(solution)/shard_map/ppermute | solution.py:483
  14.4 76.2 %collective-permute-start.1 = (f32[20,8,256]{2,1,0:T(8,128)}, f32[20,8,256]{2,1,0:T(8,128)S(1)}, u32[]{:S(2)}, u32[]{:S(2)}) collective-permute-start(f32[20,8,256]{2,1,0:T(8,128)} %get-tuple-element.28), channel_id=1, source_target_pairs={{1,0},{2,1},{3,2},{4,3},{5,4},{6,5},{7,6},{8,7},{9,8},{10,9},{11,1... | collective-permute-start | bytes 491528 | tf_op jit(solution)/shard_map/ppermute | solution.py:483
  31.5 21.3 %all-to-all-start = ((f32[128,1,96]{2,1,0:T(1,128)}), f32[128,1,96]{2,1,0:T(1,128)S(1)}, u32[]{:S(2)}, u32[]{:S(2)}) async-start(f32[128,1,96]{2,1,0:T(1,128)} %bitcast.16), calls=%async_computation | async-start | bytes 131072 | tf_op jit(solution)/shard_map/all_to_all | solution.py:494
  43.2 139.7 %all-gather.3.cloned.1.call-start = ((), (), s32[]{:S(2)}) async-start(), calls=%async_computation.3 | async-start | bytes 1056768 | tf_op jit(solution)/shard_map/all_gather | solution.py:501
  85.7 10.3 %collective-permute-start.4 = (f32[16,8,256]{2,1,0:T(8,128)}, f32[16,8,256]{2,1,0:T(8,128)S(1)}, u32[]{:S(2)}, u32[]{:S(2)}) collective-permute-start(f32[16,8,256]{2,1,0:T(8,128)} %get-tuple-element.32), channel_id=1, source_target_pairs={{0,1},{1,2},{2,3},{3,4},{4,5},{5,6},{6,7},{7,8},{8,9},{9,10},{10,1... | collective-permute-start | bytes 393224 | tf_op jit(solution)/shard_map/ppermute | solution.py:483
  88.2 7.9 %collective-permute-start.5 = (f32[16,8,256]{2,1,0:T(8,128)}, f32[16,8,256]{2,1,0:T(8,128)S(1)}, u32[]{:S(2)}, u32[]{:S(2)}) collective-permute-start(f32[16,8,256]{2,1,0:T(8,128)} %get-tuple-element.33), channel_id=1, source_target_pairs={{1,0},{2,1},{3,2},{4,3},{5,4},{6,5},{7,6},{8,7},{9,8},{10,9},{11,1... | collective-permute-start | bytes 393224 | tf_op jit(solution)/shard_map/ppermute | solution.py:483
  90.5 5.5 %copy-start.3 = (f32[20,8,256]{2,1,0:T(8,128)}, f32[20,8,256]{2,1,0:T(8,128)S(1)}, u32[]{:S(2)}) copy-start(f32[20,8,256]{2,1,0:T(8,128)S(1)} %collective-permute-done.q_ylo) | copy-start | bytes 491524
  90.5 5.6 %copy-start.4 = (f32[20,8,256]{2,1,0:T(8,128)}, f32[20,8,256]{2,1,0:T(8,128)S(1)}, u32[]{:S(2)}) copy-start(f32[20,8,256]{2,1,0:T(8,128)S(1)} %collective-permute-done.1.q_yhi) | copy-start | bytes 491524
  90.7 17.6 %collective-permute-start.2 = (f32[10,48,256]{2,1,0:T(8,128)S(1)}, f32[10,48,256]{2,1,0:T(8,128)S(1)}, u32[]{:S(2)}, u32[]{:S(2)}) collective-permute-start(f32[10,48,256]{2,1,0:T(8,128)S(1)} %get-tuple-element.55), channel_id=1, source_target_pairs={{0,16},{16,32},{32,48},{48,64},{64,80},{80,96},{96,112},{1,17},{17... | collective-permute-start | bytes 1474568 | tf_op jit(solution)/shard_map/ppermute | solution.py:483
  94.1 14.2 %collective-permute-start.3 = (f32[10,48,256]{2,1,0:T(8,128)S(1)}, f32[10,48,256]{2,1,0:T(8,128)S(1)}, u32[]{:S(2)}, u32[]{:S(2)}) collective-permute-start(f32[10,48,256]{2,1,0:T(8,128)S(1)} %get-tuple-element.54), channel_id=1, source_target_pairs={{16,0},{32,16},{48,32},{64,48},{80,64},{96,80},{112,96},{17,1},{33... | collective-permute-start | bytes 1474568 | tf_op jit(solution)/shard_map/ppermute | solution.py:483
  96.0 12.3 %copy-start.5 = (f32[16,8,256]{2,1,0:T(8,128)}, f32[16,8,256]{2,1,0:T(8,128)S(1)}, u32[]{:S(2)}) copy-start(f32[16,8,256]{2,1,0:T(8,128)S(1)} %collective-permute-done.4.r_ylo) | copy-start | bytes 393220
  96.1 12.3 %copy-start.6 = (f32[16,8,256]{2,1,0:T(8,128)}, f32[16,8,256]{2,1,0:T(8,128)S(1)}, u32[]{:S(2)}) copy-start(f32[16,8,256]{2,1,0:T(8,128)S(1)} %collective-permute-done.5.r_yhi) | copy-start | bytes 393220
  96.1 7.4 %collective-permute-start.6 = (f32[5,48,256]{2,1,0:T(8,128)S(1)}, f32[5,48,256]{2,1,0:T(8,128)S(1)}, u32[]{:S(2)}, u32[]{:S(2)}) collective-permute-start(f32[5,48,256]{2,1,0:T(8,128)S(1)} %pad_maximum_fusion.2), channel_id=1, source_target_pairs={{0,16},{16,32},{32,48},{48,64},{64,80},{80,96},{96,112},{1,17},{17... | collective-permute-start | bytes 737288 | tf_op jit(solution)/shard_map/ppermute | solution.py:483
  99.8 8.5 %collective-permute-start.7 = (f32[5,48,256]{2,1,0:T(8,128)S(1)}, f32[5,48,256]{2,1,0:T(8,128)S(1)}, u32[]{:S(2)}, u32[]{:S(2)}) collective-permute-start(f32[5,48,256]{2,1,0:T(8,128)S(1)} %pad_maximum_fusion.3), channel_id=1, source_target_pairs={{16,0},{32,16},{48,32},{64,48},{80,64},{96,80},{112,96},{17,1},{33... | collective-permute-start | bytes 737288 | tf_op jit(solution)/shard_map/ppermute | solution.py:483
  103.5 4.8 %copy-start.8 = (f32[5,48,256]{2,1,0:T(8,128)}, f32[5,48,256]{2,1,0:T(8,128)S(1)}, u32[]{:S(2)}) copy-start(f32[5,48,256]{2,1,0:T(8,128)S(1)} %collective-permute-done.6.r_xlo) | copy-start | bytes 737284
  126.0 5.6 %collective-permute-start.8 = (f32[8,8,128]{2,1,0:T(8,128)}, f32[8,8,128]{2,1,0:T(8,128)S(1)}, u32[]{:S(2)}, u32[]{:S(2)}) collective-permute-start(f32[8,8,128]{2,1,0:T(8,128)} %get-tuple-element.34), channel_id=1, source_target_pairs={{0,1},{1,2},{2,3},{3,4},{4,5},{5,6},{6,7},{7,8},{8,9},{9,10},{10,1... | collective-permute-start | bytes 98312 | tf_op jit(solution)/shard_map/ppermute | solution.py:483
  130.2 4.9 %collective-permute-start.9 = (f32[8,8,128]{2,1,0:T(8,128)}, f32[8,8,128]{2,1,0:T(8,128)S(1)}, u32[]{:S(2)}, u32[]{:S(2)}) collective-permute-start(f32[8,8,128]{2,1,0:T(8,128)} %get-tuple-element.36), channel_id=1, source_target_pairs={{1,0},{2,1},{3,2},{4,3},{5,4},{6,5},{7,6},{8,7},{9,8},{10,9},{11,1... | collective-permute-start | bytes 98312 | tf_op jit(solution)/shard_map/ppermute | solution.py:483
  135.1 9.4 %copy-start.10 = (f32[8,32,128]{2,1,0:T(8,128)}, f32[8,32,128]{2,1,0:T(8,128)S(1)}, u32[]{:S(2)}) copy-start(f32[8,32,128]{2,1,0:T(8,128)S(1)} %constant_dynamic-update-slice_fusion.r_cat) | copy-start | bytes 393220
  135.1 5.0 %collective-permute-start.10 = (f32[8,32,128]{2,1,0:T(8,128)S(1)}, f32[8,32,128]{2,1,0:T(8,128)S(1)}, u32[]{:S(2)}, u32[]{:S(2)}) collective-permute-start(f32[8,32,128]{2,1,0:T(8,128)S(1)} %constant_dynamic-update-slice_fusion.r_cat), channel_id=1, source_target_pairs={{0,16},{16,32},{32,48},{48,64},{64,80},{80,96},{96,112},{1,17},{17... | collective-permute-start | bytes 393224 | tf_op jit(solution)/shard_map/ppermute | solution.py:483
  138.2 6.3 %collective-permute-start.11 = (f32[8,32,128]{2,1,0:T(8,128)S(1)}, f32[8,32,128]{2,1,0:T(8,128)S(1)}, u32[]{:S(2)}, u32[]{:S(2)}) collective-permute-start(f32[8,32,128]{2,1,0:T(8,128)S(1)} %constant_dynamic-update-slice_fusion.r_cat), channel_id=1, source_target_pairs={{16,0},{32,16},{48,32},{64,48},{80,64},{96,80},{112,96},{17,1},{33... | collective-permute-start | bytes 393224 | tf_op jit(solution)/shard_map/ppermute | solution.py:483
  140.1 4.4 %copy-start.11 = (f32[8,32,128]{2,1,0:T(8,128)}, f32[8,32,128]{2,1,0:T(8,128)S(1)}, u32[]{:S(2)}) copy-start(f32[8,32,128]{2,1,0:T(8,128)S(1)} %collective-permute-done.10.r_xlo) | copy-start | bytes 393220
  154.3 28.5 %all-to-all-start.1 = ((f32[128,16,128]{2,1,0:T(8,128)}), f32[128,16,128]{2,1,0:T(8,128)S(1)}, u32[]{:S(2)}, u32[]{:S(2)}) async-start(f32[128,16,128]{2,1,0:T(8,128)} %get-tuple-element.37), calls=%async_computation.1 | async-start | bytes 2097152 | tf_op jit(solution)/shard_map/all_to_all | solution.py:541
  182.9 1.0 copy-start
  (4 other events, 3.1 us)
Sparse Core Ops, SparseCore 0:
  46.8 65.6 all-gather.2

commit v2 on v1

--- a/solution.py
+++ b/solution.py
@@ -14,6 +14,10 @@
 SLOTS = DEVICES * CAP
 F32 = jnp.float32
 BF16 = jnp.bfloat16
+F8 = jnp.float8_e4m3fn
+I16 = jnp.int16
+UNROLL = 4
+RANK_UNROLL = 16
 VMEM_BYTES = 56 * 1024 * 1024
 
 
@@ -50,6 +54,18 @@
     return jnp.where(mask, 1.0, 0.0).astype(BF16)
 
 
+def row16(x):
+    return jnp.broadcast_to(x, (16, x.shape[1])).astype(I16)[0:1]
+
+
+def iota16(shape, dim):
+    return iota(shape, dim).astype(I16)
+
+
+def hot16(rows, row):
+    return jnp.where(rows == row, jnp.ones((), BF16), jnp.zeros((), BF16))
+
+
 def pair_rows(coarse, fine):
     return as_bf16(iota((coarse, fine), 1) // 2 == iota((coarse, fine), 0))
 
@@ -63,8 +79,9 @@
     wide = 256
     upper = as_bf16(iota((wide, wide), 0) < iota((wide, wide), 1))
     ones = jnp.ones((wide, wide), BF16)
-    bricks = iota((DEVICES, wide), 0)
-    ranks = iota((CAP, wide), 0)
+    bricks = iota16((DEVICES, wide), 0)
+    ranks = iota16((CAP, wide), 0)
+    zero = jnp.zeros((), BF16)
     run_ref[...] = jnp.zeros_like(run_ref)
     acc_ref[...] = jnp.zeros_like(acc_ref)
 
@@ -73,77 +90,86 @@
             return jnp.concatenate([ref[pl.ds(2 * i, 1), :], ref[pl.ds(2 * i + 1, 1), :]], axis=1)
 
         live = i * wide + iota((1, wide), 1) < active
-        dest = jnp.where(live, row(dest_ref), -1)
-        hot = jnp.where(bricks == dest, 1.0, 0.0)
-        hot16 = hot.astype(BF16)
+        dest = row16(jnp.where(live, row(dest_ref), -1))
+        hot = hot16(bricks, dest)
         run = run_ref[...]
-        rank = jnp.sum(hot * (dot(hot16, upper) + run), axis=0, keepdims=True).astype(jnp.int32)
-        run_ref[...] = run + dot(hot16, ones)
+        rank = jnp.sum(hot.astype(F32) * (dot(hot, upper) + run), axis=0, keepdims=True)
+        rank = rank.astype(jnp.int32)
+        run_ref[...] = run + dot(hot, ones)
         rank_ref[pl.ds(2 * i, 1), :] = rank[:, :128]
         rank_ref[pl.ds(2 * i + 1, 1), :] = rank[:, 128:]
-        value = row(value_ref)
-        at = ranks == rank
+        at = ranks == row16(rank)
         total = acc_ref[...]
-        for part in pieces(value, 3):
-            total = total + dot_nt(hot16, jnp.where(at, part.astype(F32), 0.0).astype(BF16))
+        for part in pieces(jnp.broadcast_to(row(value_ref), (16, wide)), 2):
+            total = total + dot_nt(hot, jnp.where(at, part[0:1], zero))
         acc_ref[...] = total
         return carry
 
-    lax.fori_loop(0, ROWS // wide, step, 0)
+    lax.fori_loop(0, ROWS // wide, step, 0, unroll=RANK_UNROLL)
     out_ref[...] = acc_ref[...]
 
 
 def pick_kernel(active_ref, dest_ref, rank_ref, back_ref, out_ref):
     active = active_ref[0]
     wide = 256
-    bricks = iota((DEVICES, wide), 0)
+    bricks = iota16((DEVICES, wide), 0)
     ranks = iota((CAP, wide), 0)
     table = jnp.transpose(back_ref[...])
-    parts = pieces(table, 3)
+    hi, lo = pieces(table, 2)
 
     def step(i, carry):
         def row(ref):
             return jnp.concatenate([ref[pl.ds(2 * i, 1), :], ref[pl.ds(2 * i + 1, 1), :]], axis=1)
 
         live = i * wide + iota((1, wide), 1) < active
-        dest = jnp.where(live, row(dest_ref), -1)
-        hot16 = as_bf16(bricks == dest)
-        columns = dot(parts[0], hot16) + dot(parts[1], hot16) + dot(parts[2], hot16)
+        hot = hot16(bricks, row16(jnp.where(live, row(dest_ref), -1)))
+        columns = dot(hi, hot) + dot(lo, hot)
         picked = jnp.sum(jnp.where(ranks == row(rank_ref), columns, 0.0), axis=0, keepdims=True)
         out_ref[pl.ds(2 * i, 1), :] = picked[:, :128]
         out_ref[pl.ds(2 * i + 1, 1), :] = picked[:, 128:]
         return carry
 
-    lax.fori_loop(0, ROWS // wide, step, 0)
-
-
-CHUNK = 1024
+    lax.fori_loop(0, ROWS // wide, step, 0, unroll=RANK_UNROLL)
+
+
+CHUNK = 2048
+TOP = 32768.0
+
+
+def scale_of(x):
+    largest = jnp.maximum(jnp.max(jnp.abs(x), axis=(0, 1), keepdims=True), 1e-30)
+    return TOP / largest, largest * (1.0 / TOP)
+
+
+def two_parts(x):
+    hi = x.astype(BF16)
+    return hi, x - hi.astype(F32)
 
 
 def deposit_kernel(value_ref, column_ref, depth_ref, factor_ref, rhs_ref, low_ref, high_ref, acc_ref):
+    up, down = scale_of(value_ref[...])
     acc_ref[...] = jnp.zeros_like(acc_ref)
-    columns = iota((512, CHUNK), 0)
-    depths = iota((256, CHUNK), 0)
+    columns = iota16((512, CHUNK), 0)
+    depths = iota16((256, CHUNK), 0)
+    zero = jnp.zeros((), BF16)
 
     def step(i, carry):
         at = pl.ds(pl.multiple_of(i * CHUNK, CHUNK), CHUNK)
-        value = value_ref[:, at]
+        value = value_ref[:, at] * up
         total = acc_ref[...]
         for k in range(4):
-            amount = factor_ref[k : k + 1, at] * value
-            hi = amount.astype(BF16).astype(F32)
-            lo = amount - hi
-            hot = as_bf16(columns == column_ref[k : k + 1, at])
-            here = depths == depth_ref[k : k + 1, at]
-            spread = jnp.concatenate(
-                [jnp.where(here, hi, 0.0).astype(BF16), jnp.where(here, lo, 0.0).astype(BF16)], axis=0
-            )
-            total = total + dot_nt(hot, spread)
+            amount = jnp.broadcast_to(factor_ref[k : k + 1, at] * value, (16, CHUNK))
+            hi, lo = two_parts(amount)
+            lo = lo.astype(BF16)
+            hot = hot16(columns, row16(column_ref[k : k + 1, at]))
+            here = depths == row16(depth_ref[k : k + 1, at])
+            total = total + dot_nt(hot, jnp.where(here, hi[0:1], zero))
+            total = total + dot_nt(hot.astype(F8), jnp.where(here, lo[0:1], zero).astype(F8))
         acc_ref[...] = total
         return carry
 
     lax.fori_loop(0, SLOTS // CHUNK, step, 0)
-    rhs = (acc_ref[:, :256] + acc_ref[:, 256:]).reshape(16, 32, 256)
+    rhs = (acc_ref[...] * down).reshape(16, 32, 256)
     rhs_ref[...] = rhs
     low_ref[...] = rhs[:, :8]
     high_ref[...] = rhs[:, 24:]
@@ -180,7 +206,7 @@
             diag[x] = d
         return carry
 
-    lax.fori_loop(lo, hi, body, 0)
+    lax.fori_loop(lo, hi, body, 0, unroll=UNROLL)
 
 
 def first_guess(e, c, q, w, r, lo, hi):
@@ -190,7 +216,7 @@
         c[x] = q[x] * first
         return carry
 
-    lax.fori_loop(lo, hi, body, 0)
+    lax.fori_loop(lo, hi, body, 0, unroll=UNROLL)
 
 
 def sweep(e, c, e2, c2, q, w, r, lo, hi, boxed):
@@ -201,7 +227,7 @@
             c2[x] = q[x] * new
         return carry
 
-    lax.fori_loop(lo, hi, body, 0)
+    lax.fori_loop(lo, hi, body, 0, unroll=UNROLL)
 
 
 def pack_two(pairs):
@@ -256,7 +282,7 @@
         pairs[i] = left(6 + 2 * i) + left(7 + 2 * i)
         return carry
 
-    lax.fori_loop(0, 8, body, 0)
+    lax.fori_loop(0, 8, body, 0, unroll=UNROLL // 2)
     r1 = 0.5 * halve(pairs[...]).reshape(8, 16, 128)
     r1_ref[...] = r1
     low_ref[...] = r1[:, :8]
@@ -294,7 +320,7 @@
         pairs[i] = left(8 + 2 * i) + left(9 + 2 * i)
         return carry
 
-    lax.fori_loop(0, 4, body, 0)
+    lax.fori_loop(0, 4, body, 0, unroll=UNROLL // 2)
     r2 = 0.5 * pack_two(pairs[...])
     out_ref[...] = jnp.broadcast_to(r2[None], (DEVICES, 16, 128))
 
@@ -395,7 +421,7 @@
         last2[x - 1, 8:136] = 0.4 * a2[x] + w2[x] * (r2[x] + flow(a2, ca2, q2, x, boxed2))
         return carry
 
-    lax.fori_loop(1, 17, final2, 0)
+    lax.fori_loop(1, 17, final2, 0, unroll=UNROLL)
     z1 = iota((32, 128), 1)
     boxed1 = functools.partial(box, z=z1, depth=128)
     widen_lanes = as_bf16(iota((128, 128), 1) // 2 == iota((128, 128), 0))
@@ -429,7 +455,7 @@
             c0[p] = q0[p] * new
         return carry
 
-    lax.fori_loop(0, 12, widen, 0)
+    lax.fori_loop(0, 12, widen, 0, unroll=UNROLL)
     sweep(s0, c0, t0, ct0, q0, w0, r0, 4, 24, boxed0)
     sweep(t0, ct0, s0, c0, q0, w0, r0, 5, 23, boxed0)
 
@@ -438,24 +464,25 @@
         grid_ref[x - 6] = new[8:40]
         return carry
 
-    lax.fori_loop(6, 22, final0, 0)
+    lax.fori_loop(6, 22, final0, 0, unroll=UNROLL)
     grid = jnp.transpose(grid_ref[...].reshape(512, 256))
-    hi, lo = pieces(grid, 2)
+    up, down = scale_of(grid)
+    hi, lo = two_parts(grid * up)
     hi_ref[...] = hi
-    lo_ref[...] = lo
-    columns = iota((512, CHUNK), 0)
+    lo_ref[...] = lo.astype(F8)
+    columns = iota16((512, CHUNK), 0)
     depths = iota((256, CHUNK), 0)
 
     def step(i, carry):
         at = pl.ds(pl.multiple_of(i * CHUNK, CHUNK), CHUNK)
         total = jnp.zeros((1, CHUNK), F32)
         for k in range(4):
-            hot = as_bf16(columns == column_ref[k : k + 1, at])
-            found = dot(hi_ref[...], hot) + dot(lo_ref[...], hot)
+            hot = hot16(columns, row16(column_ref[k : k + 1, at]))
+            found = dot(hi_ref[...], hot) + dot(lo_ref[...], hot.astype(F8))
             here = depths == depth_ref[k : k + 1, at]
             picked = jnp.sum(jnp.where(here, found, 0.0), axis=0, keepdims=True)
             total = total + factor_ref[k : k + 1, at] * picked
-        back_ref[:, at] = total
+        back_ref[:, at] = total * down
         return carry
 
     lax.fori_loop(0, SLOTS // CHUNK, step, 0)
@@ -514,7 +541,7 @@
         deposit_kernel,
         (struct(16, 32, 256), struct(16, 8, 256), struct(16, 8, 256)),
         incoming.reshape(1, SLOTS), column, depth, factor,
-        scratch=(((512, 512), F32),),
+        scratch=(((512, 256), F32),),
     )
     r_ylo, r_yhi = swap(r_low, r_high, "by", NY)
     r_xlo, r_xhi = swap(
@@ -552,7 +579,7 @@
         + (((16, 144, 128), F32),)
         + ((ext1, F32),) * 4
         + ((ext0, F32),) * 4
-        + (((256, 512), BF16),) * 2,
+        + (((256, 512), BF16), ((256, 512), F8)),
     )
     returned = lax.all_to_all(
         back.reshape(DEVICES, CAP), ("bx", "by"), split_axis=0, concat_axis=0, tiled=True

time: 303 us -> 236 us (0.78)
  Pallas kernels: 169 us -> 103 us
    pallas_call x7, Pallas kernels: 169 us -> 103 us  [call(): pl.pallas_call(kernel, out_shape=outs, in_specs=[pl.BlockSpec(memory_spac...]
  transfers between devices with their start and end apart: 15 -> 15, of which waited for: 6 -> 6; matrix products, arithmetic and copies ran while one was open for 2% -> 2% of each run, Pallas kernels for 24% -> 19%
where the time goes in v2:
time: 236 us; the launch traced here: 235 us
  Pallas kernels  103 us (44%)
  starting transfers between devices  53.1 us (22%)
  waiting for transfers between devices  39.4 us (17%)
  between operations  15 us (6%)
  blocking collectives  14.5 us (6%)
  local copies, waits for them, and re-layouts  7.65 us (3%)
  other arithmetic  2.93 us (1%)
    pallas_call x7, Pallas kernels, call(): pl.pallas_call(kernel, out_shape=outs, in_specs=[pl.BlockSpec(memory_spac...  103 us
    ppermute x6, starting transfers between devices, swap(): lax.ppermute(to_upper, axis, up)  21.8 us
    all_to_all x1, waiting for transfers between devices, shards(): lax.all_to_all(r2_out, ('bx', 'by'), split_axis=0, concat_axis=0, tiled=T...  18.3 us
    all_to_all x1, blocking collectives, shards(): lax.all_to_all(back.reshape(DEVICES, CAP), ('bx', 'by'), split_axis=0, co...  14.5 us
    all_to_all x1, starting transfers between devices, shards(): lax.all_to_all(outgoing, ('bx', 'by'), split_axis=0, concat_axis=0, tiled...  11.7 us
    ppermute x6, waiting for transfers between devices, swap(): lax.ppermute(to_lower, axis, down)  11.5 us
    all_to_all x1, starting transfers between devices, shards(): lax.all_to_all(r2_out, ('bx', 'by'), split_axis=0, concat_axis=0, tiled=T...  9.91 us
    ppermute x6, starting transfers between devices, swap(): lax.ppermute(to_lower, axis, down)  9.64 us
  transfers between devices with their start and end apart: 15, of which 6 were waited for; matrix products, arithmetic and copies ran while one was open for 2% of the time, Pallas kernels for 19%

profile of v2, /device:TPU:1, one launch (start us, length us, event | category | flops | bytes accessed | tf_op | source)
XLA Modules:
  0.0 235.4 jit_solution(13518854631712627843)
XLA Ops:
  7.2 2.7 %shard_map.95 = (f32[16,32,256]{2,1,0:T(8,128)}, f32[4,16,256]{2,1,0:T(8,128)}, f32[20,8,256]{2,1,0:T(8,128)}, f32[20,8,256]{2,1,0:T(8,128)}, f32[16,128]{1,0:T(8,128)}) custom-call(f32[16,32,256]{2,1,0:T(8,128)} %base_ref.1, f32[16,32,256]{2,1,0:T(8,128)} %state_ref.1), custom_call_target="tpu_custom_call" | custom-call | tf_op jit(solution)/shard_map/pallas_call | solution.py:497
  9.9 4.5 %collective-permute-start = (f32[20,8,256]{2,1,0:T(8,128)}, f32[20,8,256]{2,1,0:T(8,128)S(1)}, u32[]{:S(2)}, u32[]{:S(2)}) collective-permute-start(f32[20,8,256]{2,1,0:T(8,128)} %get-tuple-element.27), channel_id=1, source_target_pairs={{0,1},{1,2},{2,3},{3,4},{4,5},{5,6},{6,7},{7,8},{8,9},{9,10},{10,1... | collective-permute-start | bytes 491528 | tf_op jit(solution)/shard_map/ppermute | solution.py:510
  16.3 4.3 %shard_map.96 = (f32[128,96]{1,0:T(8,128)}, s32[64,128]{1,0:T(8,128)}) custom-call(s32[1]{0:T(128)S(6)} %copy.14.active_ref, s32[64,128]{1,0:T(8,128)} %bitcast.14, f32[64,128]{1,0:T(8,128)} %bitcast.18), custom_call_target="tpu_custom_call" | custom-call | tf_op jit(solution)/shard_map/pallas_call | solution.py:497
  20.7 11.7 %all-to-all-start = ((f32[128,1,96]{2,1,0:T(1,128)}), f32[128,1,96]{2,1,0:T(1,128)S(1)}, u32[]{:S(2)}, u32[]{:S(2)}) async-start(f32[128,1,96]{2,1,0:T(1,128)} %bitcast.16), calls=%async_computation | async-start | bytes 131072 | tf_op jit(solution)/shard_map/all_to_all | solution.py:521
  34.1 7.8 %all-to-all-done = f32[128,1,96]{2,1,0:T(1,128)S(1)} async-done(((f32[128,1,96]{2,1,0:T(1,128)}), f32[128,1,96]{2,1,0:T(1,128)S(1)}, u32[]{:S(2)}, u32[]{:S(2)}) %all-to-all-start) | async-done | bytes 49184 | tf_op jit(solution)/shard_map/all_to_all | solution.py:521
  43.9 22.9 %shard_map.97 = (f32[16,32,256]{2,1,0:T(8,128)}, f32[16,8,256]{2,1,0:T(8,128)}, f32[16,8,256]{2,1,0:T(8,128)}) custom-call(f32[1,12288]{1,0:T(1,128)} %reshape.25.value_ref, s32[4,12288]{1,0:T(4,128)} %column_ref.3, s32[4,12288]{1,0:T(4,128)} %depth_ref.3, f32[4,12288]{1,0:T(4,128)} %factor_ref.3), custom_call_target="tpu_custom_call" | custom-call | tf_op jit(solution)/shard_map/pallas_call | solution.py:497
  66.8 2.5 %collective-permute-start.4 = (f32[16,8,256]{2,1,0:T(8,128)}, f32[16,8,256]{2,1,0:T(8,128)S(1)}, u32[]{:S(2)}, u32[]{:S(2)}) collective-permute-start(f32[16,8,256]{2,1,0:T(8,128)} %get-tuple-element.32), channel_id=1, source_target_pairs={{0,1},{1,2},{2,3},{3,4},{4,5},{5,6},{6,7},{7,8},{8,9},{9,10},{10,1... | collective-permute-start | bytes 393224 | tf_op jit(solution)/shard_map/ppermute | solution.py:510
  71.8 3.3 %collective-permute-start.2 = (f32[10,48,256]{2,1,0:T(8,128)S(1)}, f32[10,48,256]{2,1,0:T(8,128)S(1)}, u32[]{:S(2)}, u32[]{:S(2)}) collective-permute-start(f32[10,48,256]{2,1,0:T(8,128)S(1)} %get-tuple-element.55), channel_id=1, source_target_pairs={{0,16},{16,32},{32,48},{48,64},{64,80},{80,96},{96,112},{1,17},{17... | collective-permute-start | bytes 1474568 | tf_op jit(solution)/shard_map/ppermute | solution.py:510
  75.2 1.9 collective-permute-start.3
  77.2 3.6 %collective-permute-start.6 = (f32[5,48,256]{2,1,0:T(8,128)S(1)}, f32[5,48,256]{2,1,0:T(8,128)S(1)}, u32[]{:S(2)}, u32[]{:S(2)}) collective-permute-start(f32[5,48,256]{2,1,0:T(8,128)S(1)} %pad_maximum_fusion.2), channel_id=1, source_target_pairs={{0,16},{16,32},{32,48},{48,64},{64,80},{80,96},{96,112},{1,17},{17... | collective-permute-start | bytes 737288 | tf_op jit(solution)/shard_map/ppermute | solution.py:510
  80.9 1.9 collective-permute-start.7
  84.0 4.4 %collective-permute-done.7.r_xhi = f32[5,48,256]{2,1,0:T(8,128)S(1)} collective-permute-done((f32[5,48,256]{2,1,0:T(8,128)S(1)}, f32[5,48,256]{2,1,0:T(8,128)S(1)}, u32[]{:S(2)}, u32[]{:S(2)}) %collective-permute-start.7) | collective-permute-done | bytes 245792 | tf_op jit(solution)/shard_map/ppermute | solution.py:510
  90.2 10.9 %shard_map.98 = (f32[28,48,256]{2,1,0:T(8,128)}, f32[28,48,256]{2,1,0:T(8,128)}, f32[28,48,256]{2,1,0:T(8,128)}, f32[28,48,256]{2,1,0:T(8,128)}, f32[8,16,128]{2...) custom-call(f32[16,32,256]{2,1,0:T(8,128)} %get-tuple-element.29.q_own, f32[20,8,256]{2,1,0:T(8,128)} %copy-done.3, ...), custom_call_target="tpu_custom_call" | custom-call | tf_op jit(solution)/shard_map/pallas_call | solution.py:497
  101.1 5.1 %collective-permute-start.8 = (f32[8,8,128]{2,1,0:T(8,128)}, f32[8,8,128]{2,1,0:T(8,128)S(1)}, u32[]{:S(2)}, u32[]{:S(2)}) collective-permute-start(f32[8,8,128]{2,1,0:T(8,128)} %get-tuple-element.34), channel_id=1, source_target_pairs={{0,1},{1,2},{2,3},{3,4},{4,5},{5,6},{6,7},{7,8},{8,9},{9,10},{10,1... | collective-permute-start | bytes 98312 | tf_op jit(solution)/shard_map/ppermute | solution.py:510
  108.4 2.7 %collective-permute-done.9 = f32[8,8,128]{2,1,0:T(8,128)S(1)} collective-permute-done((f32[8,8,128]{2,1,0:T(8,128)}, f32[8,8,128]{2,1,0:T(8,128)S(1)}, u32[]{:S(2)}, u32[]{:S(2)}) %collective-permute-start.9) | collective-permute-done | bytes 32800 | tf_op jit(solution)/shard_map/ppermute | solution.py:510
  111.1 2.8 %collective-permute-start.10 = (f32[8,32,128]{2,1,0:T(8,128)S(1)}, f32[8,32,128]{2,1,0:T(8,128)S(1)}, u32[]{:S(2)}, u32[]{:S(2)}) collective-permute-start(f32[8,32,128]{2,1,0:T(8,128)S(1)} %constant_dynamic-update-slice_fusion.r_cat), channel_id=1, source_target_pairs={{0,16},{16,32},{32,48},{48,64},{64,80},{80,96},{96,112},{1,17},{17... | collective-permute-start | bytes 393224 | tf_op jit(solution)/shard_map/ppermute | solution.py:510
  113.9 1.9 collective-permute-start.11
  115.8 4.3 %collective-permute-done.11.r_xhi = f32[8,32,128]{2,1,0:T(8,128)S(1)} collective-permute-done((f32[8,32,128]{2,1,0:T(8,128)S(1)}, f32[8,32,128]{2,1,0:T(8,128)S(1)}, u32[]{:S(2)}, u32[]{:S(2)}) %collective-permute-start.11) | collective-permute-done | bytes 131104 | tf_op jit(solution)/shard_map/ppermute | solution.py:510
  120.8 5.6 %shard_map.99 = (f32[24,32,128]{2,1,0:T(8,128)}, f32[24,32,128]{2,1,0:T(8,128)}, f32[24,32,128]{2,1,0:T(8,128)}, f32[24,32,128]{2,1,0:T(8,128)}, f32[128,16,128]{2,1,0:T(8,128)}) custom-call(f32[4,16,256]{2,1,0:T(8,128)} %get-tuple-element.26.q_own, f32[20,8,256]{2,1,0:T(8,128)} %copy-done.3, f32[20,8,256]{2,1,0:T(8,128)} %copy-done.4, ...), custom_call_target="tpu_custom_call" | custom-call | tf_op jit(solution)/shard_map/pallas_call | solution.py:497
  126.4 9.9 %all-to-all-start.1 = ((f32[128,16,128]{2,1,0:T(8,128)}), f32[128,16,128]{2,1,0:T(8,128)S(1)}, u32[]{:S(2)}, u32[]{:S(2)}) async-start(f32[128,16,128]{2,1,0:T(8,128)} %get-tuple-element.37), calls=%async_computation.1 | async-start | bytes 2097152 | tf_op jit(solution)/shard_map/all_to_all | solution.py:568
  137.0 18.3 %all-to-all-done.1.r2_all = f32[128,16,128]{2,1,0:T(8,128)S(1)} async-done(((f32[128,16,128]{2,1,0:T(8,128)}), f32[128,16,128]{2,1,0:T(8,128)S(1)}, u32[]{:S(2)}, u32[]{:S(2)}) %all-to-all-start.1) | async-done | bytes 1048608 | tf_op jit(solution)/shard_map/all_to_all | solution.py:568
  156.2 53.4 %shard_map.100 = (f32[16,32,256]{2,1,0:T(8,128)}, f32[1,12288]{1,0:T(1,128)}) custom-call(s32[2]{0:T(128)} %pad_add_fusion.place_ref, f32[128,16,128]{2,1,0:T(8,128)} %copy-done, f32[128,16,128]{2,1,0:T(8,128)} %bitcast.11, f32[24,32,128]{2,1,0:T(8,128)} %get-tuple-element.39.q1, f32[24,32,128]{2,1,0:T(8,128)} %get-tuple-element.40.w1, ...), custom_call_target="tpu_custom_call" | custom-call | tf_op jit(solution)/shard_map/pallas_call | solution.py:497
  211.2 14.5 %all_to_all.25 = f32[128,1,96]{2,1,0:T(1,128)} all-to-all(f32[128,1,96]{2,1,0:T(1,128)S(1)} %bitcast.12), channel_id=1, replica_groups=mesh['bx'=8,'by'=16] {'bx','by'}, dimensions={0} | all-to-all | bytes 98304 | tf_op jit(solution)/shard_map/all_to_all | solution.py:584
  225.7 2.8 %shard_map.101 = f32[64,128]{1,0:T(8,128)} custom-call(s32[1]{0:T(128)S(6)} %copy.14.active_ref, s32[64,128]{1,0:T(8,128)} %bitcast.15, s32[64,128]{1,0:T(8,128)} %get-tuple-element.48.rank_ref, f32[128,96]{1,0:T(8,128)} %bitcast.13), custom_call_target="tpu_custom_call" | custom-call | tf_op jit(solution)/shard_map/pallas_call | solution.py:497
  (62 shorter events, 16.4 us)
Async XLA Ops:
  9.9 61.8 %copy-start.7 = (f32[4,16,256]{2,1,0:T(8,128)S(1)}, f32[4,16,256]{2,1,0:T(8,128)}, u32[]{:S(2)}) copy-start(f32[4,16,256]{2,1,0:T(8,128)} %get-tuple-element.26.q_own) | copy-start | bytes 196612
  9.9 61.7 %collective-permute-start = (f32[20,8,256]{2,1,0:T(8,128)}, f32[20,8,256]{2,1,0:T(8,128)S(1)}, u32[]{:S(2)}, u32[]{:S(2)}) collective-permute-start(f32[20,8,256]{2,1,0:T(8,128)} %get-tuple-element.27), channel_id=1, source_target_pairs={{0,1},{1,2},{2,3},{3,4},{4,5},{5,6},{6,7},{7,8},{8,9},{9,10},{10,1... | collective-permute-start | bytes 491528 | tf_op jit(solution)/shard_map/ppermute | solution.py:510
  14.4 57.3 %collective-permute-start.1 = (f32[20,8,256]{2,1,0:T(8,128)}, f32[20,8,256]{2,1,0:T(8,128)S(1)}, u32[]{:S(2)}, u32[]{:S(2)}) collective-permute-start(f32[20,8,256]{2,1,0:T(8,128)} %get-tuple-element.28), channel_id=1, source_target_pairs={{1,0},{2,1},{3,2},{4,3},{5,4},{6,5},{7,6},{8,7},{9,8},{10,9},{11,1... | collective-permute-start | bytes 491528 | tf_op jit(solution)/shard_map/ppermute | solution.py:510
  20.7 21.3 %all-to-all-start = ((f32[128,1,96]{2,1,0:T(1,128)}), f32[128,1,96]{2,1,0:T(1,128)S(1)}, u32[]{:S(2)}, u32[]{:S(2)}) async-start(f32[128,1,96]{2,1,0:T(1,128)} %bitcast.16), calls=%async_computation | async-start | bytes 131072 | tf_op jit(solution)/shard_map/all_to_all | solution.py:521
  32.3 122.9 %all-gather.3.cloned.1.call-start = ((), (), s32[]{:S(2)}) async-start(), calls=%async_computation.3 | async-start | bytes 1056768 | tf_op jit(solution)/shard_map/all_gather | solution.py:528
  66.8 10.3 %collective-permute-start.4 = (f32[16,8,256]{2,1,0:T(8,128)}, f32[16,8,256]{2,1,0:T(8,128)S(1)}, u32[]{:S(2)}, u32[]{:S(2)}) collective-permute-start(f32[16,8,256]{2,1,0:T(8,128)} %get-tuple-element.32), channel_id=1, source_target_pairs={{0,1},{1,2},{2,3},{3,4},{4,5},{5,6},{6,7},{7,8},{8,9},{9,10},{10,1... | collective-permute-start | bytes 393224 | tf_op jit(solution)/shard_map/ppermute | solution.py:510
  69.3 7.9 %collective-permute-start.5 = (f32[16,8,256]{2,1,0:T(8,128)}, f32[16,8,256]{2,1,0:T(8,128)S(1)}, u32[]{:S(2)}, u32[]{:S(2)}) collective-permute-start(f32[16,8,256]{2,1,0:T(8,128)} %get-tuple-element.33), channel_id=1, source_target_pairs={{1,0},{2,1},{3,2},{4,3},{5,4},{6,5},{7,6},{8,7},{9,8},{10,9},{11,1... | collective-permute-start | bytes 393224 | tf_op jit(solution)/shard_map/ppermute | solution.py:510
  71.6 5.5 %copy-start.3 = (f32[20,8,256]{2,1,0:T(8,128)}, f32[20,8,256]{2,1,0:T(8,128)S(1)}, u32[]{:S(2)}) copy-start(f32[20,8,256]{2,1,0:T(8,128)S(1)} %collective-permute-done.q_ylo) | copy-start | bytes 491524
  71.6 5.6 %copy-start.4 = (f32[20,8,256]{2,1,0:T(8,128)}, f32[20,8,256]{2,1,0:T(8,128)S(1)}, u32[]{:S(2)}) copy-start(f32[20,8,256]{2,1,0:T(8,128)S(1)} %collective-permute-done.1.q_yhi) | copy-start | bytes 491524
  71.8 16.6 %collective-permute-start.2 = (f32[10,48,256]{2,1,0:T(8,128)S(1)}, f32[10,48,256]{2,1,0:T(8,128)S(1)}, u32[]{:S(2)}, u32[]{:S(2)}) collective-permute-start(f32[10,48,256]{2,1,0:T(8,128)S(1)} %get-tuple-element.55), channel_id=1, source_target_pairs={{0,16},{16,32},{32,48},{48,64},{64,80},{80,96},{96,112},{1,17},{17... | collective-permute-start | bytes 1474568 | tf_op jit(solution)/shard_map/ppermute | solution.py:510
  75.2 13.2 %collective-permute-start.3 = (f32[10,48,256]{2,1,0:T(8,128)S(1)}, f32[10,48,256]{2,1,0:T(8,128)S(1)}, u32[]{:S(2)}, u32[]{:S(2)}) collective-permute-start(f32[10,48,256]{2,1,0:T(8,128)S(1)} %get-tuple-element.54), channel_id=1, source_target_pairs={{16,0},{32,16},{48,32},{64,48},{80,64},{96,80},{112,96},{17,1},{33... | collective-permute-start | bytes 1474568 | tf_op jit(solution)/shard_map/ppermute | solution.py:510
  77.1 11.3 %copy-start.5 = (f32[16,8,256]{2,1,0:T(8,128)}, f32[16,8,256]{2,1,0:T(8,128)S(1)}, u32[]{:S(2)}) copy-start(f32[16,8,256]{2,1,0:T(8,128)S(1)} %collective-permute-done.4.r_ylo) | copy-start | bytes 393220
  77.2 11.3 %copy-start.6 = (f32[16,8,256]{2,1,0:T(8,128)}, f32[16,8,256]{2,1,0:T(8,128)S(1)}, u32[]{:S(2)}) copy-start(f32[16,8,256]{2,1,0:T(8,128)S(1)} %collective-permute-done.5.r_yhi) | copy-start | bytes 393220
  77.2 6.8 %collective-permute-start.6 = (f32[5,48,256]{2,1,0:T(8,128)S(1)}, f32[5,48,256]{2,1,0:T(8,128)S(1)}, u32[]{:S(2)}, u32[]{:S(2)}) collective-permute-start(f32[5,48,256]{2,1,0:T(8,128)S(1)} %pad_maximum_fusion.2), channel_id=1, source_target_pairs={{0,16},{16,32},{32,48},{48,64},{64,80},{80,96},{96,112},{1,17},{17... | collective-permute-start | bytes 737288 | tf_op jit(solution)/shard_map/ppermute | solution.py:510
  80.9 7.5 %collective-permute-start.7 = (f32[5,48,256]{2,1,0:T(8,128)S(1)}, f32[5,48,256]{2,1,0:T(8,128)S(1)}, u32[]{:S(2)}, u32[]{:S(2)}) collective-permute-start(f32[5,48,256]{2,1,0:T(8,128)S(1)} %pad_maximum_fusion.3), channel_id=1, source_target_pairs={{16,0},{32,16},{48,32},{64,48},{80,64},{96,80},{112,96},{17,1},{33... | collective-permute-start | bytes 737288 | tf_op jit(solution)/shard_map/ppermute | solution.py:510
  84.0 4.5 %copy-start.8 = (f32[5,48,256]{2,1,0:T(8,128)}, f32[5,48,256]{2,1,0:T(8,128)S(1)}, u32[]{:S(2)}) copy-start(f32[5,48,256]{2,1,0:T(8,128)S(1)} %collective-permute-done.6.r_xlo) | copy-start | bytes 737284
  101.1 6.5 %collective-permute-start.8 = (f32[8,8,128]{2,1,0:T(8,128)}, f32[8,8,128]{2,1,0:T(8,128)S(1)}, u32[]{:S(2)}, u32[]{:S(2)}) collective-permute-start(f32[8,8,128]{2,1,0:T(8,128)} %get-tuple-element.34), channel_id=1, source_target_pairs={{0,1},{1,2},{2,3},{3,4},{4,5},{5,6},{6,7},{7,8},{8,9},{9,10},{10,1... | collective-permute-start | bytes 98312 | tf_op jit(solution)/shard_map/ppermute | solution.py:510
  106.2 4.9 %collective-permute-start.9 = (f32[8,8,128]{2,1,0:T(8,128)}, f32[8,8,128]{2,1,0:T(8,128)S(1)}, u32[]{:S(2)}, u32[]{:S(2)}) collective-permute-start(f32[8,8,128]{2,1,0:T(8,128)} %get-tuple-element.36), channel_id=1, source_target_pairs={{1,0},{2,1},{3,2},{4,3},{5,4},{6,5},{7,6},{8,7},{9,8},{10,9},{11,1... | collective-permute-start | bytes 98312 | tf_op jit(solution)/shard_map/ppermute | solution.py:510
  111.1 9.1 %copy-start.10 = (f32[8,32,128]{2,1,0:T(8,128)}, f32[8,32,128]{2,1,0:T(8,128)S(1)}, u32[]{:S(2)}) copy-start(f32[8,32,128]{2,1,0:T(8,128)S(1)} %constant_dynamic-update-slice_fusion.r_cat) | copy-start | bytes 393220
  111.1 4.7 %collective-permute-start.10 = (f32[8,32,128]{2,1,0:T(8,128)S(1)}, f32[8,32,128]{2,1,0:T(8,128)S(1)}, u32[]{:S(2)}, u32[]{:S(2)}) collective-permute-start(f32[8,32,128]{2,1,0:T(8,128)S(1)} %constant_dynamic-update-slice_fusion.r_cat), channel_id=1, source_target_pairs={{0,16},{16,32},{32,48},{48,64},{64,80},{80,96},{96,112},{1,17},{17... | collective-permute-start | bytes 393224 | tf_op jit(solution)/shard_map/ppermute | solution.py:510
  113.9 6.3 %collective-permute-start.11 = (f32[8,32,128]{2,1,0:T(8,128)S(1)}, f32[8,32,128]{2,1,0:T(8,128)S(1)}, u32[]{:S(2)}, u32[]{:S(2)}) collective-permute-start(f32[8,32,128]{2,1,0:T(8,128)S(1)} %constant_dynamic-update-slice_fusion.r_cat), channel_id=1, source_target_pairs={{16,0},{32,16},{48,32},{64,48},{80,64},{96,80},{112,96},{17,1},{33... | collective-permute-start | bytes 393224 | tf_op jit(solution)/shard_map/ppermute | solution.py:510
  115.8 4.4 %copy-start.11 = (f32[8,32,128]{2,1,0:T(8,128)}, f32[8,32,128]{2,1,0:T(8,128)S(1)}, u32[]{:S(2)}) copy-start(f32[8,32,128]{2,1,0:T(8,128)S(1)} %collective-permute-done.10.r_xlo) | copy-start | bytes 393220
  126.4 28.8 %all-to-all-start.1 = ((f32[128,16,128]{2,1,0:T(8,128)}), f32[128,16,128]{2,1,0:T(8,128)S(1)}, u32[]{:S(2)}, u32[]{:S(2)}) async-start(f32[128,16,128]{2,1,0:T(8,128)} %get-tuple-element.37), calls=%async_computation.1 | async-start | bytes 2097152 | tf_op jit(solution)/shard_map/all_to_all | solution.py:568
  155.3 1.0 copy-start
  (4 other events, 3.1 us)
Sparse Core Ops, SparseCore 0:
  36.0 66.3 all-gather.2

commit v3 on v2

--- a/solution.py
+++ b/solution.py
@@ -10,6 +10,7 @@
 NX, NY = 8, 16
 DEVICES = NX * NY
 CAP = 96
+LANES = 128
 ROWS = 8192
 SLOTS = DEVICES * CAP
 F32 = jnp.float32
@@ -80,7 +81,7 @@
     upper = as_bf16(iota((wide, wide), 0) < iota((wide, wide), 1))
     ones = jnp.ones((wide, wide), BF16)
     bricks = iota16((DEVICES, wide), 0)
-    ranks = iota16((CAP, wide), 0)
+    ranks = iota16((LANES, wide), 0)
     zero = jnp.zeros((), BF16)
     run_ref[...] = jnp.zeros_like(run_ref)
     acc_ref[...] = jnp.zeros_like(acc_ref)
@@ -113,7 +114,7 @@
     active = active_ref[0]
     wide = 256
     bricks = iota16((DEVICES, wide), 0)
-    ranks = iota((CAP, wide), 0)
+    ranks = iota((LANES, wide), 0)
     table = jnp.transpose(back_ref[...])
     hi, lo = pieces(table, 2)
 
@@ -132,7 +133,33 @@
     lax.fori_loop(0, ROWS // wide, step, 0, unroll=RANK_UNROLL)
 
 
-CHUNK = 2048
+CHUNK = 1536
+GROUP = 4 * CAP
+
+
+def to_groups(ref, out):
+    a = [ref[pl.ds(i, 32, stride=4), :] for i in range(4)]
+    lane = iota((32, 128), 1)
+
+    def moved(x, by):
+        return pltpu.roll(x, by, axis=1)
+
+    out[:, 0:128] = jnp.where(lane < 96, a[0], moved(a[1], 96))
+    out[:, 128:256] = jnp.where(lane < 64, moved(a[1], 96), moved(a[2], 64))
+    out[:, 256:384] = jnp.where(lane < 32, moved(a[2], 64), moved(a[3], 32))
+
+
+def from_groups(ref, out):
+    t = [ref[:, 128 * i : 128 * i + 128] for i in range(3)]
+    lane = iota((32, 128), 1)
+
+    def moved(x, by):
+        return pltpu.roll(x, by, axis=1)
+
+    out[pl.ds(0, 32, stride=4), :] = t[0]
+    out[pl.ds(1, 32, stride=4), :] = jnp.where(lane < 32, moved(t[0], 32), moved(t[1], 32))
+    out[pl.ds(2, 32, stride=4), :] = jnp.where(lane < 64, moved(t[1], 64), moved(t[2], 64))
+    out[pl.ds(3, 32, stride=4), :] = moved(t[2], 96)
 TOP = 32768.0
 
 
@@ -146,7 +173,12 @@
     return hi, x - hi.astype(F32)
 
 
-def deposit_kernel(value_ref, column_ref, depth_ref, factor_ref, rhs_ref, low_ref, high_ref, acc_ref):
+def depth_lane(depth):
+    return (depth & 1) * 128 + (depth >> 1)
+
+
+def deposit_kernel(slots_ref, column_ref, depth_ref, factor_ref, rhs_ref, low_ref, high_ref, acc_ref, value_ref):
+    to_groups(slots_ref, value_ref)
     up, down = scale_of(value_ref[...])
     acc_ref[...] = jnp.zeros_like(acc_ref)
     columns = iota16((512, CHUNK), 0)
@@ -155,14 +187,15 @@
 
     def step(i, carry):
         at = pl.ds(pl.multiple_of(i * CHUNK, CHUNK), CHUNK)
-        value = value_ref[:, at] * up
+        groups = [value_ref[pl.ds(i * (CHUNK // GROUP) + j, 1), :] for j in range(CHUNK // GROUP)]
+        value = jnp.concatenate(groups, axis=1) * up
         total = acc_ref[...]
         for k in range(4):
             amount = jnp.broadcast_to(factor_ref[k : k + 1, at] * value, (16, CHUNK))
             hi, lo = two_parts(amount)
             lo = lo.astype(BF16)
             hot = hot16(columns, row16(column_ref[k : k + 1, at]))
-            here = depths == row16(depth_ref[k : k + 1, at])
+            here = depths == row16(depth_lane(depth_ref[k : k + 1, at]))
             total = total + dot_nt(hot, jnp.where(here, hi[0:1], zero))
             total = total + dot_nt(hot.astype(F8), jnp.where(here, lo[0:1], zero).astype(F8))
         acc_ref[...] = total
@@ -187,6 +220,22 @@
         up = jnp.where(rows == 0, 0.0, up)
         down = jnp.where(rows == n - 1, 0.0, down)
     return v + up + down
+
+
+def box_parity(v):
+    n = v.shape[0]
+    even, odd = v[:, :128], v[:, 128:]
+    lane = iota((n, 128), 1)
+    both = even + odd
+    before = jnp.where(lane == 0, 0.0, pltpu.roll(odd, 1, axis=1))
+    after = jnp.where(lane == 127, 0.0, pltpu.roll(even, 127, axis=1))
+    v = jnp.concatenate([both + before, both + after], axis=1)
+    return v + pltpu.roll(v, 1, axis=0) + pltpu.roll(v, n - 1, axis=0)
+
+
+def parity(dim):
+    z, lane = iota((256, 256), dim), iota((256, 256), 1 - dim)
+    return as_bf16(z % 2 * 128 + z // 2 == lane)
 
 
 def near(ref, x):
@@ -236,12 +285,13 @@
 
 
 def halve(pairs):
-    thin = split_dot(pairs.reshape(256, 256), pair_lanes(256, 128))
-    return dot_split(pair_rows(128, 256), thin)
+    flat = pairs.reshape(256, 256)
+    return dot_split(pair_rows(128, 256), flat[:, :128] + flat[:, 128:])
 
 
 def kappa_kernel(base_ref, state_ref, q_ref, q1_ref, low_ref, high_ref, q2_ref):
     q = base_ref[...] * jnp.exp(0.4 * state_ref[...]) * (1.0 / 52.0)
+    q = split_dot(q.reshape(512, 256), parity(0)).reshape(16, 32, 256)
     q_ref[...] = q
     q1 = 0.125 * halve(jnp.sum(q.reshape(8, 2, 32, 256), axis=1)).reshape(8, 16, 128)
     packed = jnp.concatenate([q1[:4], q1[4:]], axis=2)
@@ -254,19 +304,18 @@
 
 
 def down_kernel(
-    q_own, q_ylo, q_yhi, q_xlo, q_xhi, r_own, r_ylo, r_yhi, r_xlo, r_xhi,
+    q_own, q_ylo, q_yhi, r_own, r_ylo, r_yhi, xlo, xhi,
     q, w, r, e, r1_ref, low_ref, high_ref,
     c, e2, c2, diag, pairs,
 ):
-    z = iota((48, 256), 1)
-    boxed = functools.partial(box, z=z, depth=256)
-    q[0:6] = q_xlo[0:6]
-    q[22:28] = q_xhi[0:6]
+    boxed = box_parity
+    q[0:6] = xlo[5:11]
+    q[22:28] = xhi[5:11]
     q[6:22, 0:8] = q_ylo[0:16]
     q[6:22, 8:40] = q_own[...]
     q[6:22, 40:48] = q_yhi[0:16]
-    r[1:6] = r_xlo[...]
-    r[22:27] = r_xhi[...]
+    r[1:6] = xlo[0:5]
+    r[22:27] = xhi[0:5]
     r[6:22, 0:8] = r_ylo[...]
     r[6:22, 8:40] = r_own[...]
     r[6:22, 40:48] = r_yhi[...]
@@ -289,25 +338,16 @@
     high_ref[...] = r1[:, 8:]
 
 
-def unpack_one(packed):
-    return jnp.concatenate([packed[..., :128], packed[..., 128:]], axis=0)
-
-
 def down_one_kernel(
-    q_own, q_ylo, q_yhi, q_xlo, q_xhi, r_cat, r_xlo, r_xhi,
+    own, xlo, xhi,
     q, w, r, e, out_ref,
     c, e2, c2, diag, pairs,
 ):
     z = iota((32, 128), 1)
     boxed = functools.partial(box, z=z, depth=128)
-    q[0:8] = unpack_one(q_xlo[6:10, 0:32])
-    q[16:24] = unpack_one(q_xhi[6:10, 0:32])
-    q[8:16, 0:8] = unpack_one(q_ylo[16:20])
-    q[8:16, 8:24] = unpack_one(q_own[...])
-    q[8:16, 24:32] = unpack_one(q_yhi[16:20])
-    r[0:8] = r_xlo[...]
-    r[8:16] = r_cat[...]
-    r[16:24] = r_xhi[...]
+    for i, side in enumerate((xlo, own, xhi)):
+        r[8 * i : 8 * i + 8] = side[0:8]
+        q[8 * i : 8 * i + 8] = side[8:16]
     set_weights(q, w, diag, 1, 23, boxed)
     first_guess(e, c, q, w, r, 1, 23)
     sweep(e, c, e2, c2, q, w, r, 2, 22, boxed)
@@ -343,22 +383,49 @@
                 ref[1 + bx * 4 + 2 + j, rows] = jnp.where(lane < 64, pltpu.roll(a, 64, axis=1), b)
 
 
+def lane_maps():
+    src, dst = iota((128, 128), 0), iota((128, 128), 1)
+    return [as_bf16(src // 64 * 64 + at + src % 64 // 2 == dst) for at in (0, 32)]
+
+
+def coarse_plane(low, high, maps):
+    return dot_split(pair_rows(64, 128), split_dot(low, maps[0]) + split_dot(high, maps[1]))
+
+
+def boxes():
+    z2, rows2 = iota((128, 128), 1) % 64, iota((128, 128), 0)
+    z3, rows3 = iota((64, 128), 1) % 32, iota((64, 128), 0)
+    return (
+        functools.partial(box, z=z2, depth=64, rows=rows2),
+        functools.partial(box, z=z3, depth=32, rows=rows3),
+    )
+
+
+def setup_kernel(q2_all, q2, w2, d2, q3, w3):
+    boxed2, boxed3 = boxes()
+    assemble_two(q2_all, q2)
+    ghosts(q2, 16, 64)
+    set_weights(q2, w2, d2, 1, 17, boxed2)
+    maps = lane_maps()
+    for x in range(4):
+        q3[1 + x] = 0.125 * coarse_plane(
+            q2[1 + 2 * x] + q2[2 + 2 * x], q2[9 + 2 * x] + q2[10 + 2 * x], maps
+        )
+    ghosts(q3, 4, 32)
+    set_weights(q3, w3, None, 1, 5, boxed3)
+
+
 def up_kernel(
-    place_ref, r2_all, q2_all, q1, w1, r1, e1, q0, w0, r0, e0,
+    place_ref, r2_all, q2, w2, d2, q3, w3, q1, w1, r1, e1, q0, w0, r0, e0,
     column_ref, depth_ref, factor_ref,
     grid_ref, back_ref,
-    q2, w2, d2, r2, a2, ca2, b2, cb2,
-    q3, w3, r3, a3, ca3, b3, cb3,
-    last2, s1, c1, t1, ct1, s0, c0, t0, ct0, hi_ref, lo_ref,
+    r2, a2, ca2, b2, cb2,
+    r3, a3, ca3, b3, cb3,
+    last2, s1, c1, t1, ct1, s0, c0, t0, ct0, hi_ref, lo_ref, slots_ref, last0,
 ):
     bx, by = place_ref[0], place_ref[1]
-    z2 = iota((128, 128), 1) % 64
-    rows2 = iota((128, 128), 0)
-    boxed2 = functools.partial(box, z=z2, depth=64, rows=rows2)
-    assemble_two(q2_all, q2)
+    boxed2, boxed3 = boxes()
     assemble_two(r2_all, r2)
-    ghosts(q2, 16, 64)
-    set_weights(q2, w2, d2, 1, 17, boxed2)
     first_guess(a2, ca2, q2, w2, r2, 1, 17)
 
     def sweep2(e, c, e_to, c_to):
@@ -370,29 +437,15 @@
     sweep2(b2, cb2, a2, ca2)
     ghosts(a2, 16, 64)
     ghosts(ca2, 16, 64)
-    lanes_low, lanes_high = pair_lanes(128, 128), None
-    src, dst = iota((128, 128), 0), iota((128, 128), 1)
-    lane_maps = [as_bf16(src // 64 * 64 + at + src % 64 // 2 == dst) for at in (0, 32)]
-    rows_half = pair_rows(64, 128)
+    maps = lane_maps()
 
     def left(x):
         return r2[x] + flow(a2, ca2, q2, x, boxed2) - d2[x] * a2[x]
 
-    def coarse_plane(low, high):
-        return dot_split(rows_half, split_dot(low, lane_maps[0]) + split_dot(high, lane_maps[1]))
-
     for x in range(4):
         r3[1 + x] = 0.5 * coarse_plane(
-            left(1 + 2 * x) + left(2 + 2 * x), left(9 + 2 * x) + left(10 + 2 * x)
+            left(1 + 2 * x) + left(2 + 2 * x), left(9 + 2 * x) + left(10 + 2 * x), maps
         )
-        q3[1 + x] = 0.125 * coarse_plane(
-            q2[1 + 2 * x] + q2[2 + 2 * x], q2[9 + 2 * x] + q2[10 + 2 * x]
-        )
-    z3 = iota((64, 128), 1) % 32
-    rows3 = iota((64, 128), 0)
-    boxed3 = functools.partial(box, z=z3, depth=32, rows=rows3)
-    ghosts(q3, 4, 32)
-    set_weights(q3, w3, None, 1, 5, boxed3)
     first_guess(a3, ca3, q3, w3, r3, 1, 5)
     now, later = (a3, ca3), (b3, cb3)
     for _ in range(7):
@@ -442,13 +495,12 @@
     sweep(s1, c1, t1, ct1, q1, w1, r1, 4, 20, boxed1)
     sweep(t1, ct1, s1, c1, q1, w1, r1, 5, 19, boxed1)
     sweep(s1, c1, t1, None, q1, w1, r1, 6, 18, boxed1)
-    z0 = iota((48, 256), 1)
-    boxed0 = functools.partial(box, z=z0, depth=256)
-    wide_lanes = as_bf16(iota((128, 256), 1) // 2 == iota((128, 256), 0))
+    boxed0 = box_parity
     wide_rows = as_bf16((iota((48, 32), 0) + 8) // 2 == iota((48, 32), 1))
 
     def widen(j, carry):
-        more = dot_split(wide_rows, split_dot(t1[6 + j], wide_lanes))
+        more = dot_split(wide_rows, t1[6 + j])
+        more = jnp.concatenate([more, more], axis=1)
         for p in (2 * j + 2, 2 * j + 3):
             new = e0[p] + more
             s0[p] = new
@@ -461,11 +513,13 @@
 
     def final0(x, carry):
         new = 0.4 * s0[x] + w0[x] * (r0[x] + flow(s0, c0, q0, x, boxed0))
-        grid_ref[x - 6] = new[8:40]
+        last0[x - 6] = new[8:40]
         return carry
 
     lax.fori_loop(6, 22, final0, 0, unroll=UNROLL)
-    grid = jnp.transpose(grid_ref[...].reshape(512, 256))
+    last = last0[...].reshape(512, 256)
+    grid_ref[...] = split_dot(last, parity(1)).reshape(16, 32, 256)
+    grid = jnp.transpose(last)
     up, down = scale_of(grid)
     hi, lo = two_parts(grid * up)
     hi_ref[...] = hi
@@ -479,13 +533,16 @@
         for k in range(4):
             hot = hot16(columns, row16(column_ref[k : k + 1, at]))
             found = dot(hi_ref[...], hot) + dot(lo_ref[...], hot.astype(F8))
-            here = depths == depth_ref[k : k + 1, at]
+            here = depths == depth_lane(depth_ref[k : k + 1, at])
             picked = jnp.sum(jnp.where(here, found, 0.0), axis=0, keepdims=True)
             total = total + factor_ref[k : k + 1, at] * picked
-        back_ref[:, at] = total * down
+        total = total * down
+        for j in range(CHUNK // GROUP):
+            slots_ref[pl.ds(i * (CHUNK // GROUP) + j, 1), :] = total[:, j * GROUP : (j + 1) * GROUP]
         return carry
 
     lax.fori_loop(0, SLOTS // CHUNK, step, 0)
+    from_groups(slots_ref, back_ref)
 
 
 def struct(*shape, dtype=F32):
@@ -514,12 +571,12 @@
     dest = dest.reshape(64, 128)
     outgoing, rank = call(
         rank_kernel,
-        (struct(DEVICES, CAP), struct(64, 128, dtype=jnp.int32)),
+        (struct(DEVICES, LANES), struct(64, 128, dtype=jnp.int32)),
         active, dest, values.reshape(64, 128),
-        smem=1, scratch=(((DEVICES, 256), F32), ((DEVICES, CAP), F32)),
-    )
+        smem=1, scratch=(((DEVICES, 256), F32), ((DEVICES, LANES), F32)),
+    )
+    outgoing, base, state = lax.optimization_barrier((outgoing, base, state))
     incoming = lax.all_to_all(outgoing, ("bx", "by"), split_axis=0, concat_axis=0, tiled=True)
-
     q, q1, q_low, q_high, q2 = call(
         kappa_kernel,
         (struct(16, 32, 256), struct(4, 16, 256), struct(20, 8, 256), struct(20, 8, 256), struct(16, 128)),
@@ -527,63 +584,62 @@
     )
     q2_all = lax.all_gather(q2[None], ("bx", "by"), axis=0, tiled=True)
     q_ylo, q_yhi = swap(q_low, q_high, "by", NY)
-    q1_cat = jnp.pad(jnp.concatenate([q_ylo[16:], q1, q_yhi[16:]], axis=1), ((0, 0), (0, 16), (0, 0)))
-
-    def faces(lo, own, hi, planes, extra=None):
-        cat = jnp.concatenate([lo[planes], own[planes], hi[planes]], axis=1)
-        return cat if extra is None else jnp.concatenate([cat, extra], axis=0)
-
-    q_xlo, q_xhi = swap(
-        faces(q_ylo, q, q_yhi, slice(0, 6), q1_cat), faces(q_ylo, q, q_yhi, slice(10, 16), q1_cat), "bx", NX
-    )
-
     rhs, r_low, r_high = call(
         deposit_kernel,
         (struct(16, 32, 256), struct(16, 8, 256), struct(16, 8, 256)),
-        incoming.reshape(1, SLOTS), column, depth, factor,
-        scratch=(((512, 256), F32),),
+        incoming, column, depth, factor,
+        scratch=(((512, 256), F32), ((32, GROUP), F32)),
     )
     r_ylo, r_yhi = swap(r_low, r_high, "by", NY)
-    r_xlo, r_xhi = swap(
-        faces(r_ylo, rhs, r_yhi, slice(0, 5)), faces(r_ylo, rhs, r_yhi, slice(11, 16)), "bx", NX
-    )
+
+    def faces(r_planes, q_planes):
+        return jnp.concatenate(
+            [
+                jnp.concatenate([lo[planes], own[planes], hi[planes]], axis=1)
+                for lo, own, hi, planes in ((r_ylo, rhs, r_yhi, r_planes), (q_ylo, q, q_yhi, q_planes))
+            ]
+        )
+
+    xlo, xhi = swap(faces(slice(0, 5), slice(0, 6)), faces(slice(11, 16), slice(10, 16)), "bx", NX)
 
     ext0, ext1 = (28, 48, 256), (24, 32, 128)
     q0e, w0e, r0e, e0e, r1, low1, high1 = call(
         down_kernel,
         (struct(*ext0),) * 4 + (struct(8, 16, 128), struct(8, 8, 128), struct(8, 8, 128)),
-        q, q_ylo, q_yhi, q_xlo, q_xhi, rhs, r_ylo, r_yhi, r_xlo, r_xhi,
+        q, q_ylo, q_yhi, rhs, r_ylo, r_yhi, xlo, xhi,
         scratch=((ext0, F32),) * 4 + (((8, 32, 256), F32),),
     )
     r1_ylo, r1_yhi = swap(low1, high1, "by", NY)
-    r1_cat = jnp.concatenate([r1_ylo, r1, r1_yhi], axis=1)
-    r1_xlo, r1_xhi = swap(r1_cat, r1_cat, "bx", NX)
+    q1_cat = jnp.concatenate([q_ylo[16:], q1, q_yhi[16:]], axis=1)
+    q1_cat = jnp.concatenate([q1_cat[:, :, :128], q1_cat[:, :, 128:]])
+    cat1 = jnp.concatenate([jnp.concatenate([r1_ylo, r1, r1_yhi], axis=1), q1_cat])
+    xlo1, xhi1 = swap(cat1, cat1, "bx", NX)
 
     q1e, w1e, r1e, e1e, r2_out = call(
         down_one_kernel,
         (struct(*ext1),) * 4 + (struct(DEVICES, 16, 128),),
-        q1, q_ylo, q_yhi, q_xlo, q_xhi, r1_cat, r1_xlo, r1_xhi,
+        cat1, xlo1, xhi1,
         scratch=((ext1, F32),) * 4 + (((4, 16, 128), F32),),
     )
+    q2_all, r2_out = lax.optimization_barrier((q2_all, r2_out))
     r2_all = lax.all_to_all(r2_out, ("bx", "by"), split_axis=0, concat_axis=0, tiled=True)
 
     place = jnp.stack([lax.axis_index("bx"), lax.axis_index("by")]).astype(jnp.int32)
     whole2, whole3 = (18, 128, 128), (6, 64, 128)
+    setup = call(setup_kernel, (struct(*whole2),) * 3 + (struct(*whole3),) * 2, q2_all)
     grid, back = call(
         up_kernel,
-        (struct(16, 32, 256), struct(1, SLOTS)),
-        place, r2_all, q2_all, q1e, w1e, r1e, e1e, q0e, w0e, r0e, e0e, column, depth, factor,
+        (struct(16, 32, 256), struct(DEVICES, LANES)),
+        place, r2_all, *setup, q1e, w1e, r1e, e1e, q0e, w0e, r0e, e0e, column, depth, factor,
         smem=1,
-        scratch=((whole2, F32),) * 8
-        + ((whole3, F32),) * 7
+        scratch=((whole2, F32),) * 5
+        + ((whole3, F32),) * 5
         + (((16, 144, 128), F32),)
         + ((ext1, F32),) * 4
         + ((ext0, F32),) * 4
-        + (((256, 512), BF16), ((256, 512), F8)),
-    )
-    returned = lax.all_to_all(
-        back.reshape(DEVICES, CAP), ("bx", "by"), split_axis=0, concat_axis=0, tiled=True
-    )
+        + (((256, 512), BF16), ((256, 512), F8), ((32, GROUP), F32), ((16, 32, 256), F32)),
+    )
+    returned = lax.all_to_all(back, ("bx", "by"), split_axis=0, concat_axis=0, tiled=True)
     (picked,) = call(pick_kernel, (struct(64, 128),), active, dest, rank, returned, smem=1)
     return grid, picked.reshape(ROWS)
 

time: 236 us -> 228 us (0.966)
  waiting for transfers between devices: 39.4 us -> 34.7 us
  local copies, waits for them, and re-layouts: 7.65 us -> 5.29 us
    all_to_all x1, waiting for transfers between devices: 7.78 us -> 0.86 us  [shards(): lax.all_to_all(outgoing, ('bx', 'by'), split_axis=0, concat_axis=0, tiled...]
    all_to_all x1, waiting for transfers between devices: 18.3 us -> 13.2 us  [shards(): lax.all_to_all(r2_out, ('bx', 'by'), split_axis=0, concat_axis=0, tiled=T...]
    ppermute x6 -> x5, waiting for transfers between devices: 1.2 us -> 5.93 us  [swap(): lax.ppermute(to_upper, axis, up)]
    all_to_all x1, starting transfers between devices: 9.91 us -> 13.4 us  [shards(): lax.all_to_all(r2_out, ('bx', 'by'), split_axis=0, concat_axis=0, tiled=T...]
    ppermute x6 -> x5, waiting for transfers between devices: 11.5 us -> 14.7 us  [swap(): lax.ppermute(to_lower, axis, down)]
    ppermute x6 -> x5, starting transfers between devices: 21.8 us -> 19.3 us  [swap(): lax.ppermute(to_upper, axis, up)]
    ppermute x6 -> x5, starting transfers between devices: 9.64 us -> 7.72 us  [swap(): lax.ppermute(to_lower, axis, down)]
    pallas_call x7 -> x8, Pallas kernels: 103 us -> 103 us  [call(): pl.pallas_call(kernel, out_shape=outs, in_specs=[pl.BlockSpec(memory_spac...]
  transfers between devices with their start and end apart: 15 -> 13, of which waited for: 6 -> 8; matrix products, arithmetic and copies ran while one was open for 2% -> 2% of each run, Pallas kernels for 19% -> 20%
where the time goes in v3:
time: 228 us; the launch traced here: 227 us
  Pallas kernels  103 us (45%)
  starting transfers between devices  52 us (23%)
  waiting for transfers between devices  34.7 us (15%)
  blocking collectives  15.5 us (7%)
  between operations  15 us (7%)
  local copies, waits for them, and re-layouts  5.29 us (2%)
    pallas_call x8, Pallas kernels, call(): pl.pallas_call(kernel, out_shape=outs, in_specs=[pl.BlockSpec(memory_spac...  103 us
    ppermute x5, starting transfers between devices, swap(): lax.ppermute(to_upper, axis, up)  19.3 us
    all_to_all x1, blocking collectives, shards(): lax.all_to_all(back, ('bx', 'by'), split_axis=0, concat_axis=0, tiled=True)  15.5 us
    ppermute x5, waiting for transfers between devices, swap(): lax.ppermute(to_lower, axis, down)  14.7 us
    all_to_all x1, starting transfers between devices, shards(): lax.all_to_all(r2_out, ('bx', 'by'), split_axis=0, concat_axis=0, tiled=T...  13.4 us
    all_to_all x1, waiting for transfers between devices, shards(): lax.all_to_all(r2_out, ('bx', 'by'), split_axis=0, concat_axis=0, tiled=T...  13.2 us
    all_to_all x1, starting transfers between devices, shards(): lax.all_to_all(outgoing, ('bx', 'by'), split_axis=0, concat_axis=0, tiled...  11.5 us
    ppermute x5, starting transfers between devices, swap(): lax.ppermute(to_lower, axis, down)  7.72 us
  transfers between devices with their start and end apart: 13, of which 8 were waited for; matrix products, arithmetic and copies ran while one was open for 2% of the time, Pallas kernels for 20%

profile of v3, /device:TPU:1, one launch (start us, length us, event | category | flops | bytes accessed | tf_op | source)
XLA Modules:
  0.0 227.5 jit_solution(16582087020093697055)
XLA Ops:
  7.8 4.3 %shard_map.95 = (f32[128,128]{1,0:T(8,128)}, s32[64,128]{1,0:T(8,128)}) custom-call(s32[1]{0:T(128)S(6)} %copy.12.active_ref, s32[64,128]{1,0:T(8,128)} %bitcast.17, f32[64,128]{1,0:T(8,128)} %bitcast.22), custom_call_target="tpu_custom_call" | custom-call | tf_op jit(solution)/shard_map/pallas_call | solution.py:554
  12.1 11.5 %all-to-all-start = ((f32[128,1,128]{2,1,0:T(1,128)}), f32[128,1,128]{2,1,0:T(1,128)S(1)}, u32[]{:S(2)}, u32[]{:S(2)}) async-start(f32[128,1,128]{2,1,0:T(1,128)} %bitcast.19), calls=%async_computation | async-start | bytes 131072 | tf_op jit(solution)/shard_map/all_to_all | solution.py:579
  23.7 2.9 %shard_map.96 = (f32[16,32,256]{2,1,0:T(8,128)}, f32[4,16,256]{2,1,0:T(8,128)}, f32[20,8,256]{2,1,0:T(8,128)}, f32[20,8,256]{2,1,0:T(8,128)}, f32[16,128]{1,0:T(8,128)}) custom-call(f32[16,32,256]{2,1,0:T(8,128)} %base_ref, f32[16,32,256]{2,1,0:T(8,128)} %state_ref), custom_call_target="tpu_custom_call" | custom-call | tf_op jit(solution)/shard_map/pallas_call | solution.py:554
  26.6 3.4 %collective-permute-start = (f32[20,8,256]{2,1,0:T(8,128)}, f32[20,8,256]{2,1,0:T(8,128)S(1)}, u32[]{:S(2)}, u32[]{:S(2)}) collective-permute-start(f32[20,8,256]{2,1,0:T(8,128)} %get-tuple-element.41), channel_id=1, source_target_pairs={{0,1},{1,2},{2,3},{3,4},{4,5},{5,6},{6,7},{7,8},{8,9},{9,10},{10,1... | collective-permute-start | bytes 491528 | tf_op jit(solution)/shard_map/ppermute | solution.py:567
  33.9 23.5 %shard_map.97 = (f32[16,32,256]{2,1,0:T(8,128)}, f32[16,8,256]{2,1,0:T(8,128)}, f32[16,8,256]{2,1,0:T(8,128)}) custom-call(f32[128,128]{1,0:T(8,128)} %bitcast.15, s32[4,12288]{1,0:T(4,128)} %column_ref.3, s32[4,12288]{1,0:T(4,128)} %depth_ref.3, f32[4,12288]{1,0:T(4,128)} %factor_ref.3), custom_call_target="tpu_custom_call" | custom-call | tf_op jit(solution)/shard_map/pallas_call | solution.py:554
  57.3 3.1 %collective-permute-start.2 = (f32[16,8,256]{2,1,0:T(8,128)}, f32[16,8,256]{2,1,0:T(8,128)S(1)}, u32[]{:S(2)}, u32[]{:S(2)}) collective-permute-start(f32[16,8,256]{2,1,0:T(8,128)} %get-tuple-element.45), channel_id=1, source_target_pairs={{0,1},{1,2},{2,3},{3,4},{4,5},{5,6},{6,7},{7,8},{8,9},{9,10},{10,1... | collective-permute-start | bytes 393224 | tf_op jit(solution)/shard_map/ppermute | solution.py:567
  62.9 3.9 %collective-permute-done.3.r_yhi = f32[16,8,256]{2,1,0:T(8,128)S(1)} collective-permute-done((f32[16,8,256]{2,1,0:T(8,128)}, f32[16,8,256]{2,1,0:T(8,128)S(1)}, u32[]{:S(2)}, u32[]{:S(2)}) %collective-permute-start.3) | collective-permute-done | bytes 131104 | tf_op jit(solution)/shard_map/ppermute | solution.py:567
  66.9 4.9 %collective-permute-start.4 = (f32[11,48,256]{2,1,0:T(8,128)S(1)}, f32[11,48,256]{2,1,0:T(8,128)S(1)}, u32[]{:S(2)}, u32[]{:S(2)}) collective-permute-start(f32[11,48,256]{2,1,0:T(8,128)S(1)} %maximum_maximum_fusion), channel_id=1, source_target_pairs={{0,16},{16,32},{32,48},{48,64},{64,80},{80,96},{96,112},{1,17},{17... | collective-permute-start | bytes 1622024 | tf_op jit(solution)/shard_map/ppermute | solution.py:567
  71.9 1.9 collective-permute-start.5
  74.0 4.7 %collective-permute-done.4.xlo = f32[11,48,256]{2,1,0:T(8,128)S(1)} collective-permute-done((f32[11,48,256]{2,1,0:T(8,128)S(1)}, f32[11,48,256]{2,1,0:T(8,128)S(1)}, u32[]{:S(2)}, u32[]{:S(2)}) %collective-permute-start.4) | collective-permute-done | bytes 540704 | tf_op jit(solution)/shard_map/ppermute | solution.py:567
  78.7 4.4 %collective-permute-done.5.xhi = f32[11,48,256]{2,1,0:T(8,128)S(1)} collective-permute-done((f32[11,48,256]{2,1,0:T(8,128)S(1)}, f32[11,48,256]{2,1,0:T(8,128)S(1)}, u32[]{:S(2)}, u32[]{:S(2)}) %collective-permute-start.5) | collective-permute-done | bytes 540704 | tf_op jit(solution)/shard_map/ppermute | solution.py:567
  84.0 9.3 %shard_map.98 = (f32[28,48,256]{2,1,0:T(8,128)}, f32[28,48,256]{2,1,0:T(8,128)}, f32[28,48,256]{2,1,0:T(8,128)}, f32[28,48,256]{2,1,0:T(8,128)}, f32[8,16,128]{2...) custom-call(f32[16,32,256]{2,1,0:T(8,128)} %get-tuple-element.40.q_own, f32[20,8,256]{2,1,0:T(8,128)} %copy-done.4, ...), custom_call_target="tpu_custom_call" | custom-call | tf_op jit(solution)/shard_map/pallas_call | solution.py:554
  93.3 4.2 %collective-permute-start.6 = (f32[8,8,128]{2,1,0:T(8,128)}, f32[8,8,128]{2,1,0:T(8,128)S(1)}, u32[]{:S(2)}, u32[]{:S(2)}) collective-permute-start(f32[8,8,128]{2,1,0:T(8,128)} %get-tuple-element.47), channel_id=1, source_target_pairs={{0,1},{1,2},{2,3},{3,4},{4,5},{5,6},{6,7},{7,8},{8,9},{9,10},{10,1... | collective-permute-start | bytes 98312 | tf_op jit(solution)/shard_map/ppermute | solution.py:567
  98.8 4.2 %collective-permute-done.7 = f32[8,8,128]{2,1,0:T(8,128)S(1)} collective-permute-done((f32[8,8,128]{2,1,0:T(8,128)}, f32[8,8,128]{2,1,0:T(8,128)S(1)}, u32[]{:S(2)}, u32[]{:S(2)}) %collective-permute-start.7) | collective-permute-done | bytes 32800 | tf_op jit(solution)/shard_map/ppermute | solution.py:567
  103.8 1.9 collective-permute-start.9
  105.8 3.6 %collective-permute-start.8 = (f32[16,32,128]{2,1,0:T(8,128)S(1)}, f32[16,32,128]{2,1,0:T(8,128)S(1)}, u32[]{:S(2)}, u32[]{:S(2)}) collective-permute-start(f32[16,32,128]{2,1,0:T(8,128)S(1)} %pad_maximum_fusion.own), channel_id=1, source_target_pairs={{0,16},{16,32},{32,48},{48,64},{64,80},{80,96},{96,112},{1,17},{17... | collective-permute-start | bytes 786440 | tf_op jit(solution)/shard_map/ppermute | solution.py:567
  109.4 2.1 collective-permute-done.9.xhi
  113.4 5.4 %shard_map.99 = (f32[24,32,128]{2,1,0:T(8,128)}, f32[24,32,128]{2,1,0:T(8,128)}, f32[24,32,128]{2,1,0:T(8,128)}, f32[24,32,128]{2,1,0:T(8,128)}, f32[128,16,128]{2,1,0:T(8,128)}) custom-call(f32[16,32,128]{2,1,0:T(8,128)} %copy-done.1, f32[16,32,128]{2,1,0:T(8,128)} %copy-done.9, f32[16,32,128]{2,1,0:T(8,128)} %copy-done.8), custom_call_target="tpu_custom_call" | custom-call | tf_op jit(solution)/shard_map/pallas_call | solution.py:554
  118.8 13.4 %all-to-all-start.1 = ((f32[128,16,128]{2,1,0:T(8,128)}), f32[128,16,128]{2,1,0:T(8,128)S(1)}, u32[]{:S(2)}, u32[]{:S(2)}) async-start(f32[128,16,128]{2,1,0:T(8,128)} %get-tuple-element.52), calls=%async_computation.1 | async-start | bytes 2097152 | tf_op jit(solution)/shard_map/all_to_all | solution.py:625
  132.9 5.0 %shard_map.100 = (f32[18,128,128]{2,1,0:T(8,128)}, f32[18,128,128]{2,1,0:T(8,128)}, f32[18,128,128]{2,1,0:T(8,128)}, f32[6,64,128]{2,1,0:T(8,128)}, f32[6,64,128]{2,1,0:T(8,128)}) custom-call(f32[128,16,128]{2,1,0:T(8,128)} %bitcast.14), custom_call_target="tpu_custom_call" | custom-call | tf_op jit(solution)/shard_map/pallas_call | solution.py:554
  137.9 13.2 %all-to-all-done.1.r2_all = f32[128,16,128]{2,1,0:T(8,128)S(1)} async-done(((f32[128,16,128]{2,1,0:T(8,128)}), f32[128,16,128]{2,1,0:T(8,128)S(1)}, u32[]{:S(2)}, u32[]{:S(2)}) %all-to-all-start.1) | async-done | bytes 1048608 | tf_op jit(solution)/shard_map/all_to_all | solution.py:625
  152.1 50.0 %shard_map.101 = (f32[16,32,256]{2,1,0:T(8,128)}, f32[128,128]{1,0:T(8,128)}) custom-call(s32[2]{0:T(128)} %pad_add_fusion.place_ref, f32[128,16,128]{2,1,0:T(8,128)} %copy-done, f32[18,128,128]{2,1,0:T(8,128)} %get-tuple-element.54.q2, f32[18,128,128]{2,1,0:T(8,128)} %get-tuple-element.55.w2, f32[18,128,128]{2,1,0:T(8,128)} %get-tuple-element.56.d2, ...), custom_call_target="tpu_custom_call" | custom-call | tf_op jit(solution)/shard_map/pallas_call | solution.py:554
  202.1 15.5 %all_to_all.27 = f32[128,1,128]{2,1,0:T(1,128)} all-to-all(f32[128,1,128]{2,1,0:T(1,128)} %bitcast.20), channel_id=1, replica_groups=mesh['bx'=8,'by'=16] {'bx','by'}, dimensions={0} | all-to-all | bytes 131072 | tf_op jit(solution)/shard_map/all_to_all | solution.py:642
  217.6 3.0 %shard_map.102 = f32[64,128]{1,0:T(8,128)} custom-call(s32[1]{0:T(128)S(6)} %copy.12.active_ref, s32[64,128]{1,0:T(8,128)} %bitcast.18, s32[64,128]{1,0:T(8,128)} %get-tuple-element.68.rank_ref, f32[128,128]{1,0:T(8,128)} %bitcast.16), custom_call_target="tpu_custom_call" | custom-call | tf_op jit(solution)/shard_map/pallas_call | solution.py:554
  (50 shorter events, 12.9 us)
Async XLA Ops:
  12.1 21.1 %all-to-all-start = ((f32[128,1,128]{2,1,0:T(1,128)}), f32[128,1,128]{2,1,0:T(1,128)S(1)}, u32[]{:S(2)}, u32[]{:S(2)}) async-start(f32[128,1,128]{2,1,0:T(1,128)} %bitcast.19), calls=%async_computation | async-start | bytes 131072 | tf_op jit(solution)/shard_map/all_to_all | solution.py:579
  23.6 95.1 %all-gather.3.cloned.1.call-start = ((), (), s32[]{:S(2)}) async-start(), calls=%async_computation.3 | async-start | bytes 1056768 | tf_op jit(solution)/shard_map/all_gather | solution.py:585
  26.6 36.2 %collective-permute-start = (f32[20,8,256]{2,1,0:T(8,128)}, f32[20,8,256]{2,1,0:T(8,128)S(1)}, u32[]{:S(2)}, u32[]{:S(2)}) collective-permute-start(f32[20,8,256]{2,1,0:T(8,128)} %get-tuple-element.41), channel_id=1, source_target_pairs={{0,1},{1,2},{2,3},{3,4},{4,5},{5,6},{6,7},{7,8},{8,9},{9,10},{10,1... | collective-permute-start | bytes 491528 | tf_op jit(solution)/shard_map/ppermute | solution.py:567
  30.0 32.8 %collective-permute-start.1 = (f32[20,8,256]{2,1,0:T(8,128)}, f32[20,8,256]{2,1,0:T(8,128)S(1)}, u32[]{:S(2)}, u32[]{:S(2)}) collective-permute-start(f32[20,8,256]{2,1,0:T(8,128)} %get-tuple-element.42), channel_id=1, source_target_pairs={{1,0},{2,1},{3,2},{4,3},{5,4},{6,5},{7,6},{8,7},{9,8},{10,9},{11,1... | collective-permute-start | bytes 491528 | tf_op jit(solution)/shard_map/ppermute | solution.py:567
  57.3 5.6 %collective-permute-start.2 = (f32[16,8,256]{2,1,0:T(8,128)}, f32[16,8,256]{2,1,0:T(8,128)S(1)}, u32[]{:S(2)}, u32[]{:S(2)}) collective-permute-start(f32[16,8,256]{2,1,0:T(8,128)} %get-tuple-element.45), channel_id=1, source_target_pairs={{0,1},{1,2},{2,3},{3,4},{4,5},{5,6},{6,7},{7,8},{8,9},{9,10},{10,1... | collective-permute-start | bytes 393224 | tf_op jit(solution)/shard_map/ppermute | solution.py:567
  60.5 6.4 %collective-permute-start.3 = (f32[16,8,256]{2,1,0:T(8,128)}, f32[16,8,256]{2,1,0:T(8,128)S(1)}, u32[]{:S(2)}, u32[]{:S(2)}) collective-permute-start(f32[16,8,256]{2,1,0:T(8,128)} %get-tuple-element.46), channel_id=1, source_target_pairs={{1,0},{2,1},{3,2},{4,3},{5,4},{6,5},{7,6},{8,7},{9,8},{10,9},{11,1... | collective-permute-start | bytes 393224 | tf_op jit(solution)/shard_map/ppermute | solution.py:567
  62.8 11.1 %copy-start.4 = (f32[20,8,256]{2,1,0:T(8,128)}, f32[20,8,256]{2,1,0:T(8,128)S(1)}, u32[]{:S(2)}) copy-start(f32[20,8,256]{2,1,0:T(8,128)S(1)} %collective-permute-done.q_ylo) | copy-start | bytes 491524
  62.8 11.1 %copy-start.11 = (f32[4,16,256]{2,1,0:T(8,128)S(1)}, f32[4,16,256]{2,1,0:T(8,128)}, u32[]{:S(2)}) copy-start(f32[4,16,256]{2,1,0:T(8,128)} %get-tuple-element.50) | copy-start | bytes 196612
  62.9 11.0 %copy-start.5 = (f32[20,8,256]{2,1,0:T(8,128)}, f32[20,8,256]{2,1,0:T(8,128)S(1)}, u32[]{:S(2)}) copy-start(f32[20,8,256]{2,1,0:T(8,128)S(1)} %collective-permute-done.1.q_yhi) | copy-start | bytes 491524
  62.9 11.0 %copy-start.6 = (f32[16,8,256]{2,1,0:T(8,128)}, f32[16,8,256]{2,1,0:T(8,128)S(1)}, u32[]{:S(2)}) copy-start(f32[16,8,256]{2,1,0:T(8,128)S(1)} %collective-permute-done.2.r_ylo) | copy-start | bytes 393220
  66.9 16.3 %copy-start.7 = (f32[16,8,256]{2,1,0:T(8,128)}, f32[16,8,256]{2,1,0:T(8,128)S(1)}, u32[]{:S(2)}) copy-start(f32[16,8,256]{2,1,0:T(8,128)S(1)} %collective-permute-done.3.r_yhi) | copy-start | bytes 393220
  66.9 11.8 %collective-permute-start.4 = (f32[11,48,256]{2,1,0:T(8,128)S(1)}, f32[11,48,256]{2,1,0:T(8,128)S(1)}, u32[]{:S(2)}, u32[]{:S(2)}) collective-permute-start(f32[11,48,256]{2,1,0:T(8,128)S(1)} %maximum_maximum_fusion), channel_id=1, source_target_pairs={{0,16},{16,32},{32,48},{48,64},{64,80},{80,96},{96,112},{1,17},{17... | collective-permute-start | bytes 1622024 | tf_op jit(solution)/shard_map/ppermute | solution.py:567
  71.9 11.2 %collective-permute-start.5 = (f32[11,48,256]{2,1,0:T(8,128)S(1)}, f32[11,48,256]{2,1,0:T(8,128)S(1)}, u32[]{:S(2)}, u32[]{:S(2)}) collective-permute-start(f32[11,48,256]{2,1,0:T(8,128)S(1)} %maximum_maximum_fusion.1), channel_id=1, source_target_pairs={{16,0},{32,16},{48,32},{64,48},{80,64},{96,80},{112,96},{17,1},{33... | collective-permute-start | bytes 1622024 | tf_op jit(solution)/shard_map/ppermute | solution.py:567
  78.7 4.5 %copy-start.2 = (f32[11,48,256]{2,1,0:T(8,128)}, f32[11,48,256]{2,1,0:T(8,128)S(1)}, u32[]{:S(2)}) copy-start(f32[11,48,256]{2,1,0:T(8,128)S(1)} %collective-permute-done.4.xlo) | copy-start | bytes 1622020
  83.1 0.8 copy-start.3
  93.3 5.5 %collective-permute-start.6 = (f32[8,8,128]{2,1,0:T(8,128)}, f32[8,8,128]{2,1,0:T(8,128)S(1)}, u32[]{:S(2)}, u32[]{:S(2)}) collective-permute-start(f32[8,8,128]{2,1,0:T(8,128)} %get-tuple-element.47), channel_id=1, source_target_pairs={{0,1},{1,2},{2,3},{3,4},{4,5},{5,6},{6,7},{7,8},{8,9},{9,10},{10,1... | collective-permute-start | bytes 98312 | tf_op jit(solution)/shard_map/ppermute | solution.py:567
  97.5 5.5 %collective-permute-start.7 = (f32[8,8,128]{2,1,0:T(8,128)}, f32[8,8,128]{2,1,0:T(8,128)S(1)}, u32[]{:S(2)}, u32[]{:S(2)}) collective-permute-start(f32[8,8,128]{2,1,0:T(8,128)} %get-tuple-element.49), channel_id=1, source_target_pairs={{1,0},{2,1},{3,2},{4,3},{5,4},{6,5},{7,6},{8,7},{9,8},{10,9},{11,1... | collective-permute-start | bytes 98312 | tf_op jit(solution)/shard_map/ppermute | solution.py:567
  103.8 8.9 %copy-start.1 = (f32[16,32,128]{2,1,0:T(8,128)}, f32[16,32,128]{2,1,0:T(8,128)S(1)}, u32[]{:S(2)}) copy-start(f32[16,32,128]{2,1,0:T(8,128)S(1)} %pad_maximum_fusion.own) | copy-start | bytes 786436
  103.8 7.7 %collective-permute-start.9 = (f32[16,32,128]{2,1,0:T(8,128)S(1)}, f32[16,32,128]{2,1,0:T(8,128)S(1)}, u32[]{:S(2)}, u32[]{:S(2)}) collective-permute-start(f32[16,32,128]{2,1,0:T(8,128)S(1)} %pad_maximum_fusion.own), channel_id=1, source_target_pairs={{16,0},{32,16},{48,32},{64,48},{80,64},{96,80},{112,96},{17,1},{33... | collective-permute-start | bytes 786440 | tf_op jit(solution)/shard_map/ppermute | solution.py:567
  105.8 6.9 %collective-permute-start.8 = (f32[16,32,128]{2,1,0:T(8,128)S(1)}, f32[16,32,128]{2,1,0:T(8,128)S(1)}, u32[]{:S(2)}, u32[]{:S(2)}) collective-permute-start(f32[16,32,128]{2,1,0:T(8,128)S(1)} %pad_maximum_fusion.own), channel_id=1, source_target_pairs={{0,16},{16,32},{32,48},{48,64},{64,80},{80,96},{96,112},{1,17},{17... | collective-permute-start | bytes 786440 | tf_op jit(solution)/shard_map/ppermute | solution.py:567
  111.5 1.2 copy-start.8
  112.7 0.7 copy-start.9
  118.8 32.3 %all-to-all-start.1 = ((f32[128,16,128]{2,1,0:T(8,128)}), f32[128,16,128]{2,1,0:T(8,128)S(1)}, u32[]{:S(2)}, u32[]{:S(2)}) async-start(f32[128,16,128]{2,1,0:T(8,128)} %get-tuple-element.52), calls=%async_computation.1 | async-start | bytes 2097152 | tf_op jit(solution)/shard_map/all_to_all | solution.py:625
  151.1 1.0 copy-start
  (1 other events, 0.6 us)
Sparse Core Ops, SparseCore 0:
  27.3 65.5 all-gather.2

commit v4 on v3

--- a/solution.py
+++ b/solution.py
@@ -5,10 +5,14 @@
 from jax import lax
 from jax.experimental import pallas as pl
 from jax.experimental.pallas import tpu as pltpu
+from jax.sharding import Mesh
 from jax.sharding import PartitionSpec as P
 
 NX, NY = 8, 16
 DEVICES = NX * NY
+CHIPS = DEVICES // 2
+BX = ("x", "core")
+ALL = ("x", "core", "by")
 CAP = 96
 LANES = 128
 ROWS = 8192
@@ -43,11 +47,11 @@
     return lax.dot_general(a, b, (((1,), (1,)), ((), ())), preferred_element_type=F32)
 
 
-def split_dot(x, m, count=3):
+def split_dot(x, m, count=2):
     return sum(dot(p, m) for p in pieces(x, count))
 
 
-def dot_split(m, x, count=3):
+def dot_split(m, x, count=2):
     return sum(dot(m, p) for p in pieces(x, count))
 
 
@@ -133,7 +137,7 @@
     lax.fori_loop(0, ROWS // wide, step, 0, unroll=RANK_UNROLL)
 
 
-CHUNK = 1536
+CHUNK = 3072
 GROUP = 4 * CAP
 
 
@@ -222,15 +226,19 @@
     return v + up + down
 
 
-def box_parity(v):
+def box_parity(v, group=128, rows=None):
     n = v.shape[0]
     even, odd = v[:, :128], v[:, 128:]
-    lane = iota((n, 128), 1)
+    lane = iota((n, 128), 1) & (group - 1)
     both = even + odd
     before = jnp.where(lane == 0, 0.0, pltpu.roll(odd, 1, axis=1))
-    after = jnp.where(lane == 127, 0.0, pltpu.roll(even, 127, axis=1))
+    after = jnp.where(lane == group - 1, 0.0, pltpu.roll(even, 127, axis=1))
     v = jnp.concatenate([both + before, both + after], axis=1)
-    return v + pltpu.roll(v, 1, axis=0) + pltpu.roll(v, n - 1, axis=0)
+    up, down = pltpu.roll(v, 1, axis=0), pltpu.roll(v, n - 1, axis=0)
+    if rows is not None:
+        up = jnp.where(rows == 0, 0.0, up)
+        down = jnp.where(rows == n - 1, 0.0, down)
+    return v + up + down
 
 
 def parity(dim):
@@ -244,6 +252,10 @@
 
 def flow(e, c, q, x, boxed):
     return q[x] * boxed(near(e, x)) + boxed(near(c, x)) - 2.0 * c[x]
+
+
+def unroll_of(ref):
+    return 2 if ref.shape[1] == 128 else UNROLL
 
 
 def set_weights(q, w, diag, lo, hi, boxed):
@@ -255,7 +267,7 @@
             diag[x] = d
         return carry
 
-    lax.fori_loop(lo, hi, body, 0, unroll=UNROLL)
+    lax.fori_loop(lo, hi, body, 0, unroll=unroll_of(q))
 
 
 def first_guess(e, c, q, w, r, lo, hi):
@@ -265,7 +277,7 @@
         c[x] = q[x] * first
         return carry
 
-    lax.fori_loop(lo, hi, body, 0, unroll=UNROLL)
+    lax.fori_loop(lo, hi, body, 0, unroll=unroll_of(q))
 
 
 def sweep(e, c, e2, c2, q, w, r, lo, hi, boxed):
@@ -276,12 +288,17 @@
             c2[x] = q[x] * new
         return carry
 
-    lax.fori_loop(lo, hi, body, 0, unroll=UNROLL)
+    lax.fori_loop(lo, hi, body, 0, unroll=unroll_of(q))
 
 
 def pack_two(pairs):
     both = dot_split(pair_rows(32, 64), pairs.reshape(64, 128))
-    return split_dot(both[:16], pair_lanes(128, 128)) + split_dot(both[16:], pair_lanes(128, 128, 64))
+    flat = jnp.concatenate([both[8 * x : 8 * x + 8] for x in range(4)], axis=1)
+    src, dst = iota((512, 256), 0), iota((512, 256), 1)
+    z = src % 128 // 2
+    lane = z % 2 * 128 + src // 128 * 32 + z // 2
+    packed = split_dot(flat, as_bf16(lane == dst))
+    return jnp.concatenate([packed[:, :128], packed[:, 128:]], axis=0)
 
 
 def halve(pairs):
@@ -305,8 +322,8 @@
 
 def down_kernel(
     q_own, q_ylo, q_yhi, r_own, r_ylo, r_yhi, xlo, xhi,
-    q, w, r, e, r1_ref, low_ref, high_ref,
-    c, e2, c2, diag, pairs,
+    q_out, w_out, r_out, e_out, r1_ref, low_ref, high_ref,
+    q, w, r, e, c, e2, c2, diag, pairs, sems,
 ):
     boxed = box_parity
     q[0:6] = xlo[5:11]
@@ -319,10 +336,16 @@
     r[6:22, 0:8] = r_ylo[...]
     r[6:22, 8:40] = r_own[...]
     r[6:22, 40:48] = r_yhi[...]
+    pairs_out = ((q, q_out), (r, r_out), (w, w_out), (e, e_out))
+    copies = [pltpu.make_async_copy(a, b, sems.at[i]) for i, (a, b) in enumerate(pairs_out)]
+    copies[0].start()
+    copies[1].start()
     set_weights(q, w, diag, 1, 27, boxed)
+    copies[2].start()
     first_guess(e, c, q, w, r, 1, 27)
     sweep(e, c, e2, c2, q, w, r, 2, 26, boxed)
     sweep(e2, c2, e, c, q, w, r, 3, 25, boxed)
+    copies[3].start()
 
     def left(x):
         return (r[x] + flow(e, c, q, x, boxed) - diag[x] * e[x])[8:40]
@@ -336,6 +359,8 @@
     r1_ref[...] = r1
     low_ref[...] = r1[:, :8]
     high_ref[...] = r1[:, 8:]
+    for copy in copies:
+        copy.wait()
 
 
 def down_one_kernel(
@@ -362,90 +387,110 @@
 
     lax.fori_loop(0, 4, body, 0, unroll=UNROLL // 2)
     r2 = 0.5 * pack_two(pairs[...])
-    out_ref[...] = jnp.broadcast_to(r2[None], (DEVICES, 16, 128))
+    out_ref[...] = jnp.broadcast_to(r2[None], (CHIPS, 16, 128))
 
 
 def ghosts(ref, count, group):
-    lane = iota(ref.shape[1:], 1)
-    ref[0] = jnp.where(lane >= group, pltpu.roll(ref[count], group, axis=1), 0.0)
-    ref[count + 1] = jnp.where(lane < 128 - group, pltpu.roll(ref[1], 128 - group, axis=1), 0.0)
-
-
-def assemble_two(gathered, ref):
-    lane = iota((8, 128), 1)
-    for bx in range(4):
-        for by in range(NY):
-            for j in range(2):
-                a = gathered[bx * NY + by, j * 8 : j * 8 + 8]
-                b = gathered[(bx + 4) * NY + by, j * 8 : j * 8 + 8]
-                rows = slice(by * 8, by * 8 + 8)
-                ref[1 + bx * 4 + j, rows] = jnp.where(lane < 64, a, pltpu.roll(b, 64, axis=1))
-                ref[1 + bx * 4 + 2 + j, rows] = jnp.where(lane < 64, pltpu.roll(a, 64, axis=1), b)
-
-
-def lane_maps():
-    src, dst = iota((128, 128), 0), iota((128, 128), 1)
-    return [as_bf16(src // 64 * 64 + at + src % 64 // 2 == dst) for at in (0, 32)]
-
-
-def coarse_plane(low, high, maps):
-    return dot_split(pair_rows(64, 128), split_dot(low, maps[0]) + split_dot(high, maps[1]))
+    lane = iota((ref.shape[1], 128), 1)
+    for at in range(0, ref.shape[2], 128):
+        half = slice(at, at + 128)
+        ref[0, :, half] = jnp.where(lane >= group, pltpu.roll(ref[count, :, half], group, axis=1), 0.0)
+        ref[count + 1, :, half] = jnp.where(
+            lane < 128 - group, pltpu.roll(ref[1, :, half], 128 - group, axis=1), 0.0
+        )
+
+
+def assemble_two(block, ref):
+    lane = iota((16, 128), 1)
+    low_half, low_quarter = lane < 64, (lane & 63) < 32
+
+    def moved(x, by):
+        return pltpu.roll(x, by, axis=1)
+
+    def body(by, carry):
+        rows = pl.ds(pl.multiple_of(by * 8, 8), 8)
+        for h in range(2):
+            a = [block(h, g, by) for g in range(4)]
+            b = [None] * 4
+            for i in range(2):
+                b[i] = jnp.where(low_half, a[i], moved(a[i + 2], 64))
+                b[i + 2] = jnp.where(low_half, moved(a[i], 64), a[i + 2])
+            for i in (0, 2):
+                first = jnp.where(low_quarter, b[i], moved(b[i + 1], 32))
+                second = jnp.where(low_quarter, moved(b[i], 96), b[i + 1])
+                for j, plane in ((i, first), (i + 1, second)):
+                    ref[1 + h * 4 + j, rows, 0:128] = plane[0:8]
+                    ref[1 + h * 4 + j, rows, 128:256] = plane[8:16]
+        return carry
+
+    lax.fori_loop(0, NY, body, 0, unroll=4)
+
+
+def coarse_planes(planes):
+    wide = jnp.concatenate([p[:, :128] + p[:, 128:] for p in planes], axis=1)
+    thin = dot_split(pair_rows(64, 128), wide)
+    return [thin[:, 128 * i : 128 * i + 128] for i in range(4)]
 
 
 def boxes():
-    z2, rows2 = iota((128, 128), 1) % 64, iota((128, 128), 0)
     z3, rows3 = iota((64, 128), 1) % 32, iota((64, 128), 0)
     return (
-        functools.partial(box, z=z2, depth=64, rows=rows2),
+        functools.partial(box_parity, group=32, rows=iota((128, 256), 0)),
         functools.partial(box, z=z3, depth=32, rows=rows3),
     )
 
 
 def setup_kernel(q2_all, q2, w2, d2, q3, w3):
     boxed2, boxed3 = boxes()
-    assemble_two(q2_all, q2)
-    ghosts(q2, 16, 64)
-    set_weights(q2, w2, d2, 1, 17, boxed2)
-    maps = lane_maps()
-    for x in range(4):
-        q3[1 + x] = 0.125 * coarse_plane(
-            q2[1 + 2 * x] + q2[2 + 2 * x], q2[9 + 2 * x] + q2[10 + 2 * x], maps
-        )
+    assemble_two(lambda core, g, by: q2_all[(2 * g + core) * NY + by], q2)
+    ghosts(q2, 8, 32)
+    set_weights(q2, w2, d2, 1, 9, boxed2)
+    for x, plane in enumerate(coarse_planes([q2[1 + 2 * x] + q2[2 + 2 * x] for x in range(4)])):
+        q3[1 + x] = 0.125 * plane
     ghosts(q3, 4, 32)
     set_weights(q3, w3, None, 1, 5, boxed3)
 
 
 def up_kernel(
-    place_ref, r2_all, q2, w2, d2, q3, w3, q1, w1, r1, e1, q0, w0, r0, e0,
-    column_ref, depth_ref, factor_ref,
-    grid_ref, back_ref,
-    r2, a2, ca2, b2, cb2,
-    r3, a3, ca3, b3, cb3,
-    last2, s1, c1, t1, ct1, s0, c0, t0, ct0, hi_ref, lo_ref, slots_ref, last0,
+    place_ref, r2_mine, r2_other, q2, w2, d2, q3, w3, *refs
 ):
+    hbm, (grid_ref, back_ref) = refs[:11], refs[11:13]
+    (
+        r2, a2, ca2, b2, cb2,
+        r3, a3, ca3, b3, cb3,
+        last2, s1, c1, t1, ct1, s0, c0, t0, ct0, hi_ref, lo_ref, slots_ref, last0,
+    ) = refs[13:36]
+    local, sems = refs[36:47], refs[47]
+    copies = [pltpu.make_async_copy(hbm[i], local[i], sems.at[i]) for i in range(11)]
+    for copy in copies:
+        copy.start()
+    q1, w1, r1, e1, q0, w0, r0, e0, column_ref, depth_ref, factor_ref = local
     bx, by = place_ref[0], place_ref[1]
     boxed2, boxed3 = boxes()
-    assemble_two(r2_all, r2)
-    first_guess(a2, ca2, q2, w2, r2, 1, 17)
+    core = lax.rem(bx, 2)
+
+    def block(of, g, by):
+        i = g * NY + by
+        return jnp.where(core == of, r2_mine[i], r2_other[i])
+
+    assemble_two(block, r2)
+    first_guess(a2, ca2, q2, w2, r2, 1, 9)
 
     def sweep2(e, c, e_to, c_to):
-        ghosts(e, 16, 64)
-        ghosts(c, 16, 64)
-        sweep(e, c, e_to, c_to, q2, w2, r2, 1, 17, boxed2)
+        ghosts(e, 8, 32)
+        ghosts(c, 8, 32)
+        sweep(e, c, e_to, c_to, q2, w2, r2, 1, 9, boxed2)
 
     sweep2(a2, ca2, b2, cb2)
     sweep2(b2, cb2, a2, ca2)
-    ghosts(a2, 16, 64)
-    ghosts(ca2, 16, 64)
-    maps = lane_maps()
+    ghosts(a2, 8, 32)
+    ghosts(ca2, 8, 32)
 
     def left(x):
         return r2[x] + flow(a2, ca2, q2, x, boxed2) - d2[x] * a2[x]
 
-    for x in range(4):
-        r3[1 + x] = 0.5 * coarse_plane(
-            left(1 + 2 * x) + left(2 + 2 * x), left(9 + 2 * x) + left(10 + 2 * x), maps
-        )
+    for x, plane in enumerate(coarse_planes([left(1 + 2 * x) + left(2 + 2 * x) for x in range(4)])):
+        r3[1 + x] = 0.5 * plane
     first_guess(a3, ca3, q3, w3, r3, 1, 5)
     now, later = (a3, ca3), (b3, cb3)
     for _ in range(7):
@@ -454,60 +499,65 @@
         sweep(*now, *later, q3, w3, r3, 1, 5, boxed3)
         now, later = later, now
     e3 = now[0]
-    src, dst = iota((128, 128), 1), iota((128, 128), 0)
-    lane_back = [as_bf16(src // 64 * 64 + at + src % 64 // 2 == dst) for at in (0, 32)]
     rows_double = as_bf16(iota((128, 64), 0) // 2 == iota((128, 64), 1))
-    for x in range(8):
-        more = dot_split(rows_double, split_dot(e3[1 + x % 4], lane_back[x // 4]))
-        for j in (1 + 2 * x, 2 + 2 * x):
-            new = a2[j] + more
-            a2[j] = new
-            ca2[j] = q2[j] * new
+    more = dot_split(rows_double, jnp.concatenate([e3[1 + x] for x in range(4)], axis=1))
+    for j in range(1, 9):
+        add = more[:, (j - 1) // 2 * 128 : (j - 1) // 2 * 128 + 128]
+        new = a2[j] + jnp.concatenate([add, add], axis=1)
+        a2[j] = new
+        ca2[j] = q2[j] * new
     sweep2(a2, ca2, b2, cb2)
     sweep2(b2, cb2, a2, ca2)
-    ghosts(a2, 16, 64)
-    ghosts(ca2, 16, 64)
-    last2[:, 0:8] = jnp.zeros((16, 8, 128), F32)
-    last2[:, 136:144] = jnp.zeros((16, 8, 128), F32)
+    ghosts(a2, 8, 32)
+    ghosts(ca2, 8, 32)
+    last2[:, 0:8] = jnp.zeros((8, 8, 256), F32)
+    last2[:, 136:144] = jnp.zeros((8, 8, 256), F32)
 
     def final2(x, carry):
         last2[x - 1, 8:136] = 0.4 * a2[x] + w2[x] * (r2[x] + flow(a2, ca2, q2, x, boxed2))
         return carry
 
-    lax.fori_loop(1, 17, final2, 0, unroll=UNROLL)
+    lax.fori_loop(1, 9, final2, 0, unroll=2)
     z1 = iota((32, 128), 1)
     boxed1 = functools.partial(box, z=z1, depth=128)
-    widen_lanes = as_bf16(iota((128, 128), 1) // 2 == iota((128, 128), 0))
+    src, dst = iota((256, 128), 0), iota((256, 128), 1)
+    widen_lanes = as_bf16(jnp.logical_and(dst // 4 == src % 128, dst // 2 % 2 == src // 128))
     widen_rows = as_bf16((iota((32, 24), 0) + 8) // 2 == iota((32, 24), 1))
+    windows = []
     for j in range(10):
         x = bx * 4 - 3 + j
         inside = jnp.logical_and(x >= 0, x < 32)
         at = jnp.clip(x, 0, 31)
-        window = last2[lax.rem(at, 16), pl.ds(pl.multiple_of(by * 8, 8), 24), :]
-        window = jnp.where(at >= 16, pltpu.roll(window, 64, axis=1), window)
-        window = jnp.where(inside, window, 0.0)
-        more = dot_split(widen_rows, split_dot(window, widen_lanes))
-        for p in (2 * j + 2, 2 * j + 3):
-            if 3 <= p < 21:
-                new = e1[p] + more
-                s1[p] = new
-                c1[p] = q1[p] * new
+        rows = pl.ds(pl.multiple_of(by * 8, 8), 24)
+        shift = lax.rem(128 - at // 8 * 32, 128)
+        halves = [
+            pltpu.roll(last2[lax.rem(at, 8), rows, lanes : lanes + 128], shift, axis=1) for lanes in (0, 128)
+        ]
+        windows.append(jnp.where(inside, jnp.concatenate(halves, axis=1), 0.0))
+    wide = split_dot(jnp.concatenate(windows, axis=0), widen_lanes)
+    wide = jnp.concatenate([wide[24 * j : 24 * j + 24] for j in range(10)], axis=1)
+    wide = dot_split(widen_rows, wide)
+    for copy in copies[:4]:
+        copy.wait()
+    for p in range(3, 21):
+        j = (p - 2) // 2
+        new = e1[p] + wide[:, 128 * j : 128 * j + 128]
+        s1[p] = new
+        c1[p] = q1[p] * new
     sweep(s1, c1, t1, ct1, q1, w1, r1, 4, 20, boxed1)
     sweep(t1, ct1, s1, c1, q1, w1, r1, 5, 19, boxed1)
     sweep(s1, c1, t1, None, q1, w1, r1, 6, 18, boxed1)
     boxed0 = box_parity
     wide_rows = as_bf16((iota((48, 32), 0) + 8) // 2 == iota((48, 32), 1))
 
-    def widen(j, carry):
-        more = dot_split(wide_rows, t1[6 + j])
-        more = jnp.concatenate([more, more], axis=1)
-        for p in (2 * j + 2, 2 * j + 3):
-            new = e0[p] + more
-            s0[p] = new
-            c0[p] = q0[p] * new
-        return carry
-
-    lax.fori_loop(0, 12, widen, 0, unroll=UNROLL)
+    wide = dot_split(wide_rows, jnp.concatenate([t1[6 + j] for j in range(12)], axis=1))
+    for copy in copies[4:]:
+        copy.wait()
+    for p in range(3, 25):
+        add = wide[:, (p - 2) // 2 * 128 : (p - 2) // 2 * 128 + 128]
+        new = e0[p] + jnp.concatenate([add, add], axis=1)
+        s0[p] = new
+        c0[p] = q0[p] * new
     sweep(s0, c0, t0, ct0, q0, w0, r0, 4, 24, boxed0)
     sweep(t0, ct0, s0, c0, q0, w0, r0, 5, 23, boxed0)
 
@@ -549,14 +599,18 @@
     return jax.ShapeDtypeStruct(shape, dtype)
 
 
-def call(kernel, outs, *args, smem=0, scratch=()):
+def call(kernel, outs, *args, smem=0, left=0, left_out=0, scratch=()):
     vmem = pl.BlockSpec(memory_space=pltpu.VMEM)
     return pl.pallas_call(
         kernel,
         out_shape=outs,
-        in_specs=[pl.BlockSpec(memory_space=pltpu.SMEM)] * smem + [vmem] * (len(args) - smem),
-        out_specs=tuple(vmem for _ in outs),
-        scratch_shapes=[pltpu.VMEM(s, d) for s, d in scratch],
+        in_specs=[pl.BlockSpec(memory_space=pltpu.SMEM)] * smem
+        + [vmem] * (len(args) - smem - left)
+        + [pl.BlockSpec(memory_space=pl.ANY)] * left,
+        out_specs=tuple(pl.BlockSpec(memory_space=pl.ANY) if i < left_out else vmem for i in range(len(outs))),
+        scratch_shapes=[pltpu.VMEM(s, d) for s, d in scratch]
+        + ([pltpu.VMEM(a.shape, a.dtype) for a in args[-left:]] + [pltpu.SemaphoreType.DMA((left,))] if left else [])
+        + ([pltpu.SemaphoreType.DMA((left_out,))] if left_out else []),
         compiler_params=pltpu.CompilerParams(vmem_limit_bytes=VMEM_BYTES),
     )(*args)
 
@@ -575,14 +629,13 @@
         active, dest, values.reshape(64, 128),
         smem=1, scratch=(((DEVICES, 256), F32), ((DEVICES, LANES), F32)),
     )
-    outgoing, base, state = lax.optimization_barrier((outgoing, base, state))
-    incoming = lax.all_to_all(outgoing, ("bx", "by"), split_axis=0, concat_axis=0, tiled=True)
+    incoming = lax.all_to_all(outgoing, ALL, split_axis=0, concat_axis=0, tiled=True)
     q, q1, q_low, q_high, q2 = call(
         kappa_kernel,
         (struct(16, 32, 256), struct(4, 16, 256), struct(20, 8, 256), struct(20, 8, 256), struct(16, 128)),
         base, state,
     )
-    q2_all = lax.all_gather(q2[None], ("bx", "by"), axis=0, tiled=True)
+    q2_all = lax.all_gather(q2[None], ALL, axis=0, tiled=True)
     q_ylo, q_yhi = swap(q_low, q_high, "by", NY)
     rhs, r_low, r_high = call(
         deposit_kernel,
@@ -600,65 +653,70 @@
             ]
         )
 
-    xlo, xhi = swap(faces(slice(0, 5), slice(0, 6)), faces(slice(11, 16), slice(10, 16)), "bx", NX)
+    xlo, xhi = swap(faces(slice(0, 5), slice(0, 6)), faces(slice(11, 16), slice(10, 16)), BX, NX)
 
     ext0, ext1 = (28, 48, 256), (24, 32, 128)
     q0e, w0e, r0e, e0e, r1, low1, high1 = call(
         down_kernel,
         (struct(*ext0),) * 4 + (struct(8, 16, 128), struct(8, 8, 128), struct(8, 8, 128)),
         q, q_ylo, q_yhi, rhs, r_ylo, r_yhi, xlo, xhi,
-        scratch=((ext0, F32),) * 4 + (((8, 32, 256), F32),),
+        left_out=4,
+        scratch=((ext0, F32),) * 8 + (((8, 32, 256), F32),),
     )
     r1_ylo, r1_yhi = swap(low1, high1, "by", NY)
     q1_cat = jnp.concatenate([q_ylo[16:], q1, q_yhi[16:]], axis=1)
     q1_cat = jnp.concatenate([q1_cat[:, :, :128], q1_cat[:, :, 128:]])
     cat1 = jnp.concatenate([jnp.concatenate([r1_ylo, r1, r1_yhi], axis=1), q1_cat])
-    xlo1, xhi1 = swap(cat1, cat1, "bx", NX)
+    xlo1, xhi1 = swap(cat1, cat1, BX, NX)
 
     q1e, w1e, r1e, e1e, r2_out = call(
         down_one_kernel,
-        (struct(*ext1),) * 4 + (struct(DEVICES, 16, 128),),
+        (struct(*ext1),) * 4 + (struct(CHIPS, 16, 128),),
         cat1, xlo1, xhi1,
         scratch=((ext1, F32),) * 4 + (((4, 16, 128), F32),),
     )
     q2_all, r2_out = lax.optimization_barrier((q2_all, r2_out))
-    r2_all = lax.all_to_all(r2_out, ("bx", "by"), split_axis=0, concat_axis=0, tiled=True)
-
-    place = jnp.stack([lax.axis_index("bx"), lax.axis_index("by")]).astype(jnp.int32)
-    whole2, whole3 = (18, 128, 128), (6, 64, 128)
+    r2_mine = lax.all_to_all(r2_out, ("x", "by"), split_axis=0, concat_axis=0, tiled=True)
+    whole2, whole3 = (10, 128, 256), (6, 64, 128)
     setup = call(setup_kernel, (struct(*whole2),) * 3 + (struct(*whole3),) * 2, q2_all)
+    r2_mine, setup = lax.optimization_barrier((r2_mine, setup))
+    r2_other = lax.ppermute(r2_mine, "core", [(0, 1), (1, 0)])
+
+    place = jnp.stack([lax.axis_index(BX), lax.axis_index("by")]).astype(jnp.int32)
     grid, back = call(
         up_kernel,
         (struct(16, 32, 256), struct(DEVICES, LANES)),
-        place, r2_all, *setup, q1e, w1e, r1e, e1e, q0e, w0e, r0e, e0e, column, depth, factor,
+        place, r2_mine, r2_other, *setup, q1e, w1e, r1e, e1e, q0e, w0e, r0e, e0e, column, depth, factor,
         smem=1,
+        left=11,
         scratch=((whole2, F32),) * 5
         + ((whole3, F32),) * 5
-        + (((16, 144, 128), F32),)
+        + (((8, 144, 256), F32),)
         + ((ext1, F32),) * 4
         + ((ext0, F32),) * 4
         + (((256, 512), BF16), ((256, 512), F8), ((32, GROUP), F32), ((16, 32, 256), F32)),
     )
-    returned = lax.all_to_all(back, ("bx", "by"), split_axis=0, concat_axis=0, tiled=True)
+    returned = lax.all_to_all(back, ALL, split_axis=0, concat_axis=0, tiled=True)
     (picked,) = call(pick_kernel, (struct(64, 128),), active, dest, rank, returned, smem=1)
     return grid, picked.reshape(ROWS)
 
 
 def solution(mesh):
     placed = (
-        P(("bx", "by")),
-        P(("bx", "by"), None),
-        P(("bx", "by")),
-        P(None, ("bx", "by")),
-        P(None, ("bx", "by")),
-        P(None, ("bx", "by")),
-        P("bx", "by", None),
-        P("bx", "by", None),
-    )
+        P(ALL),
+        P(ALL, None),
+        P(ALL),
+        P(None, ALL),
+        P(None, ALL),
+        P(None, ALL),
+        P(BX, "by", None),
+        P(BX, "by", None),
+    )
+    mesh = Mesh(mesh.devices.reshape(NX // 2, 2, NY), ALL)
     return jax.shard_map(
         shards,
         mesh=mesh,
         in_specs=placed,
-        out_specs=(P("bx", "by", None), P(("bx", "by"))),
+        out_specs=(P(BX, "by", None), P(ALL)),
         check_vma=False,
     )

time: 228 us -> 215 us (0.943)
  Pallas kernels: 103 us -> 94.8 us
  waiting for transfers between devices: 34.7 us -> 28.9 us
    pallas_call x8, Pallas kernels: 103 us -> 94.8 us  [call(): pl.pallas_call(kernel, out_shape=outs, in_specs=[pl.BlockSpec(memory_spac...]
    all_to_all x2, waiting for transfers between devices: 14 us -> 6.46 us  [the longest x1 5.53 us: shards(): lax.all_to_all(r2_out, ('x', 'by'), split_axis=0, concat_axis=0, tiled=True)]
    ppermute x0 -> x1, starting transfers between devices: none -> 3.06 us  [shards(): r2_other = lax.ppermute(r2_mine, 'core', [(0, 1), (1, 0)])]
  transfers between devices with their start and end apart: 13 -> 14, of which waited for: 8 -> 9; matrix products, arithmetic and copies ran while one was open for 2% -> 2% of each run, Pallas kernels for 20% -> 20%
where the time goes in v4:
time: 215 us; the launch traced here: 214 us
  Pallas kernels  94.8 us (44%)
  starting transfers between devices  53.9 us (25%)
  waiting for transfers between devices  28.9 us (13%)
  between operations  15 us (7%)
  blocking collectives  14.8 us (7%)
  local copies, waits for them, and re-layouts  5.11 us (2%)
    pallas_call x8, Pallas kernels, call(): pl.pallas_call(kernel, out_shape=outs, in_specs=[pl.BlockSpec(memory_spac...  94.8 us
    ppermute x5, starting transfers between devices, swap(): lax.ppermute(to_upper, axis, up)  18 us
    ppermute x5, waiting for transfers between devices, swap(): lax.ppermute(to_lower, axis, down)  16.1 us
    all_to_all x1, blocking collectives, shards(): lax.all_to_all(back, ALL, split_axis=0, concat_axis=0, tiled=True)  14.8 us
    all_to_all x1, starting transfers between devices, shards(): lax.all_to_all(r2_out, ('x', 'by'), split_axis=0, concat_axis=0, tiled=True)  13.5 us
    all_to_all x1, starting transfers between devices, shards(): lax.all_to_all(outgoing, ALL, split_axis=0, concat_axis=0, tiled=True)  11.5 us
    ppermute x5, starting transfers between devices, swap(): lax.ppermute(to_lower, axis, down)  7.72 us
    all_to_all x1, waiting for transfers between devices, shards(): lax.all_to_all(r2_out, ('x', 'by'), split_axis=0, concat_axis=0, tiled=True)  5.53 us
  transfers between devices with their start and end apart: 14, of which 9 were waited for; matrix products, arithmetic and copies ran while one was open for 2% of the time, Pallas kernels for 20%

profile of v4, /device:TPU:1, one launch (start us, length us, event | category | flops | bytes accessed | tf_op | source)
XLA Modules:
  0.0 214.0 jit_solution(1589154843195593013)
XLA Ops:
  7.8 4.3 %shard_map.96 = (f32[128,128]{1,0:T(8,128)}, s32[64,128]{1,0:T(8,128)}) custom-call(s32[1]{0:T(128)S(6)} %copy.12.active_ref, s32[64,128]{1,0:T(8,128)} %bitcast.17, f32[64,128]{1,0:T(8,128)} %bitcast.22), custom_call_target="tpu_custom_call" | custom-call | tf_op jit(solution)/shard_map/pallas_call | solution.py:604
  12.1 11.5 %all-to-all-start = ((f32[128,1,128]{2,1,0:T(1,128)}), f32[128,1,128]{2,1,0:T(1,128)S(1)}, u32[]{:S(2)}, u32[]{:S(2)}) async-start(f32[128,1,128]{2,1,0:T(1,128)} %bitcast.19), calls=%async_computation | async-start | bytes 131072 | tf_op jit(solution)/shard_map/all_to_all | solution.py:632
  23.7 2.8 %shard_map.95 = (f32[16,32,256]{2,1,0:T(8,128)}, f32[4,16,256]{2,1,0:T(8,128)}, f32[20,8,256]{2,1,0:T(8,128)}, f32[20,8,256]{2,1,0:T(8,128)}, f32[16,128]{1,0:T(8,128)}) custom-call(f32[16,32,256]{2,1,0:T(8,128)} %base_ref.1, f32[16,32,256]{2,1,0:T(8,128)} %state_ref.1), custom_call_target="tpu_custom_call" | custom-call | tf_op jit(solution)/shard_map/pallas_call | solution.py:604
  26.5 3.4 %collective-permute-start = (f32[20,8,256]{2,1,0:T(8,128)}, f32[20,8,256]{2,1,0:T(8,128)S(1)}, u32[]{:S(2)}, u32[]{:S(2)}) collective-permute-start(f32[20,8,256]{2,1,0:T(8,128)} %get-tuple-element.41), channel_id=1, source_target_pairs={{0,1},{1,2},{2,3},{3,4},{4,5},{5,6},{6,7},{7,8},{8,9},{9,10},{10,1... | collective-permute-start | bytes 491528 | tf_op jit(solution)/shard_map/ppermute | solution.py:621
  33.8 22.6 %shard_map.97 = (f32[16,32,256]{2,1,0:T(8,128)}, f32[16,8,256]{2,1,0:T(8,128)}, f32[16,8,256]{2,1,0:T(8,128)}) custom-call(f32[128,128]{1,0:T(8,128)} %bitcast.15, s32[4,12288]{1,0:T(4,128)} %refs_8_.1, s32[4,12288]{1,0:T(4,128)} %refs_9_.1, f32[4,12288]{1,0:T(4,128)} %refs_10_.1), custom_call_target="tpu_custom_call" | custom-call | tf_op jit(solution)/shard_map/pallas_call | solution.py:604
  56.4 3.1 %collective-permute-start.2 = (f32[16,8,256]{2,1,0:T(8,128)}, f32[16,8,256]{2,1,0:T(8,128)S(1)}, u32[]{:S(2)}, u32[]{:S(2)}) collective-permute-start(f32[16,8,256]{2,1,0:T(8,128)} %get-tuple-element.45), channel_id=1, source_target_pairs={{0,1},{1,2},{2,3},{3,4},{4,5},{5,6},{6,7},{7,8},{8,9},{9,10},{10,1... | collective-permute-start | bytes 393224 | tf_op jit(solution)/shard_map/ppermute | solution.py:621
  61.9 4.0 %collective-permute-done.3.r_yhi = f32[16,8,256]{2,1,0:T(8,128)S(1)} collective-permute-done((f32[16,8,256]{2,1,0:T(8,128)}, f32[16,8,256]{2,1,0:T(8,128)S(1)}, u32[]{:S(2)}, u32[]{:S(2)}) %collective-permute-start.3) | collective-permute-done | bytes 131104 | tf_op jit(solution)/shard_map/ppermute | solution.py:621
  66.0 4.9 %collective-permute-start.4 = (f32[11,48,256]{2,1,0:T(8,128)S(1)}, f32[11,48,256]{2,1,0:T(8,128)S(1)}, u32[]{:S(2)}, u32[]{:S(2)}) collective-permute-start(f32[11,48,256]{2,1,0:T(8,128)S(1)} %maximum_maximum_fusion), channel_id=1, source_target_pairs={{0,16},{16,32},{32,48},{48,64},{64,80},{80,96},{96,112},{1,17},{17... | collective-permute-start | bytes 1622024 | tf_op jit(solution)/shard_map/ppermute | solution.py:621
  70.9 1.9 collective-permute-start.5
  72.9 4.2 %collective-permute-done.4.xlo = f32[11,48,256]{2,1,0:T(8,128)S(1)} collective-permute-done((f32[11,48,256]{2,1,0:T(8,128)S(1)}, f32[11,48,256]{2,1,0:T(8,128)S(1)}, u32[]{:S(2)}, u32[]{:S(2)}) %collective-permute-start.4) | collective-permute-done | bytes 540704 | tf_op jit(solution)/shard_map/ppermute | solution.py:621
  77.1 5.3 %collective-permute-done.5.xhi = f32[11,48,256]{2,1,0:T(8,128)S(1)} collective-permute-done((f32[11,48,256]{2,1,0:T(8,128)S(1)}, f32[11,48,256]{2,1,0:T(8,128)S(1)}, u32[]{:S(2)}, u32[]{:S(2)}) %collective-permute-start.5) | collective-permute-done | bytes 540704 | tf_op jit(solution)/shard_map/ppermute | solution.py:621
  83.3 8.0 %shard_map.98 = (f32[28,48,256]{2,1,0:T(8,128)}, f32[28,48,256]{2,1,0:T(8,128)}, f32[28,48,256]{2,1,0:T(8,128)}, f32[28,48,256]{2,1,0:T(8,128)}, f32[8,16,128]{2...) custom-call(f32[16,32,256]{2,1,0:T(8,128)} %get-tuple-element.40.q_own, f32[20,8,256]{2,1,0:T(8,128)} %copy-done.4, ...), custom_call_target="tpu_custom_call" | custom-call | tf_op jit(solution)/shard_map/pallas_call | solution.py:604
  91.3 3.1 %collective-permute-start.6 = (f32[8,8,128]{2,1,0:T(8,128)}, f32[8,8,128]{2,1,0:T(8,128)S(1)}, u32[]{:S(2)}, u32[]{:S(2)}) collective-permute-start(f32[8,8,128]{2,1,0:T(8,128)} %get-tuple-element.47), channel_id=1, source_target_pairs={{0,1},{1,2},{2,3},{3,4},{4,5},{5,6},{6,7},{7,8},{8,9},{9,10},{10,1... | collective-permute-start | bytes 98312 | tf_op jit(solution)/shard_map/ppermute | solution.py:621
  95.7 4.6 %collective-permute-done.7 = f32[8,8,128]{2,1,0:T(8,128)S(1)} collective-permute-done((f32[8,8,128]{2,1,0:T(8,128)}, f32[8,8,128]{2,1,0:T(8,128)S(1)}, u32[]{:S(2)}, u32[]{:S(2)}) %collective-permute-start.7) | collective-permute-done | bytes 32800 | tf_op jit(solution)/shard_map/ppermute | solution.py:621
  103.1 3.6 %collective-permute-start.8 = (f32[16,32,128]{2,1,0:T(8,128)S(1)}, f32[16,32,128]{2,1,0:T(8,128)S(1)}, u32[]{:S(2)}, u32[]{:S(2)}) collective-permute-start(f32[16,32,128]{2,1,0:T(8,128)S(1)} %pad_maximum_fusion.own), channel_id=1, source_target_pairs={{0,16},{16,32},{32,48},{48,64},{64,80},{80,96},{96,112},{1,17},{17... | collective-permute-start | bytes 786440 | tf_op jit(solution)/shard_map/ppermute | solution.py:621
  106.8 2.1 collective-permute-done.9.xhi
  110.8 5.1 %shard_map.99 = (f32[24,32,128]{2,1,0:T(8,128)}, f32[24,32,128]{2,1,0:T(8,128)}, f32[24,32,128]{2,1,0:T(8,128)}, f32[24,32,128]{2,1,0:T(8,128)}, f32[64,16,128]{2,1,0:T(8,128)}) custom-call(f32[16,32,128]{2,1,0:T(8,128)} %copy-done.1, f32[16,32,128]{2,1,0:T(8,128)} %copy-done.10, f32[16,32,128]{2,1,0:T(8,128)} %copy-done.9), custom_call_target="tpu_custom_call" | custom-call | tf_op jit(solution)/shard_map/pallas_call | solution.py:604
  115.9 13.5 %all-to-all-start.1 = ((f32[64,16,128]{2,1,0:T(8,128)}), f32[64,16,128]{2,1,0:T(8,128)S(1)}, u32[]{:S(2)}, u32[]{:S(2)}) async-start(f32[64,16,128]{2,1,0:T(8,128)} %get-tuple-element.52), calls=%async_computation.1 | async-start | bytes 1048576 | tf_op jit(solution)/shard_map/all_to_all | solution.py:679
  129.5 5.3 %shard_map.100 = (f32[10,128,256]{2,1,0:T(8,128)}, f32[10,128,256]{2,1,0:T(8,128)}, f32[10,128,256]{2,1,0:T(8,128)}, f32[6,64,128]{2,1,0:T(8,128)}, f32[6,64,128]{2,1,0:T(8,128)}) custom-call(f32[128,16,128]{2,1,0:T(8,128)} %bitcast.14), custom_call_target="tpu_custom_call" | custom-call | tf_op jit(solution)/shard_map/pallas_call | solution.py:604
  134.7 5.5 %all-to-all-done.1.r2_mine = f32[64,16,128]{2,1,0:T(8,128)S(1)} async-done(((f32[64,16,128]{2,1,0:T(8,128)}), f32[64,16,128]{2,1,0:T(8,128)S(1)}, u32[]{:S(2)}, u32[]{:S(2)}) %all-to-all-start.1) | async-done | bytes 524320 | tf_op jit(solution)/shard_map/all_to_all | solution.py:679
  140.3 3.1 %collective-permute-start.10 = (f32[64,16,128]{2,1,0:T(8,128)S(1)}, f32[64,16,128]{2,1,0:T(8,128)S(1)}, u32[]{:S(2)}, u32[]{:S(2)}) collective-permute-start(f32[64,16,128]{2,1,0:T(8,128)S(1)} %all-to-all-done.1.r2_mine), channel_id=1, source_target_pairs={{0,16},{16,0},{1,17},{17,1},{2,18},{18,2},{3,19},{19,3},{4,20},{20... | collective-permute-start | bytes 1572872 | tf_op jit(solution)/shard_map/ppermute | solution.py:683
  145.7 43.7 %shard_map.101 = (f32[16,32,256]{2,1,0:T(8,128)}, f32[128,128]{1,0:T(8,128)}) custom-call(s32[2]{0:T(128)} %pad_add_fusion.place_ref, f32[64,16,128]{2,1,0:T(8,128)} %copy-done, f32[64,16,128]{2,1,0:T(8,128)} %copy-done.6, f32[10,128,256]{2,1,0:T(8,128)} %get-tuple-element.60.q2, f32[10,128,256]{2,1,0:T(8,128)} %get-tuple-element.61.w2, ...), custom_call_target="tpu_custom_call" | custom-call | tf_op jit(solution)/shard_map/pallas_call | solution.py:604
  189.3 14.8 %all_to_all.27 = f32[128,1,128]{2,1,0:T(1,128)} all-to-all(f32[128,1,128]{2,1,0:T(1,128)} %bitcast.20), channel_id=1, replica_groups=mesh['x'=4,'core'=2,'by'=16] {'x','core','by'}, dimensions={0} | all-to-all | bytes 131072 | tf_op jit(solution)/shard_map/all_to_all | solution.py:699
  204.1 3.0 %shard_map.102 = f32[64,128]{1,0:T(8,128)} custom-call(s32[1]{0:T(128)S(6)} %copy.12.active_ref, s32[64,128]{1,0:T(8,128)} %bitcast.18, s32[64,128]{1,0:T(8,128)} %get-tuple-element.74.rank_ref, f32[128,128]{1,0:T(8,128)} %bitcast.16), custom_call_target="tpu_custom_call" | custom-call | tf_op jit(solution)/shard_map/pallas_call | solution.py:604
  (54 shorter events, 15.6 us)
Async XLA Ops:
  12.1 21.1 %all-to-all-start = ((f32[128,1,128]{2,1,0:T(1,128)}), f32[128,1,128]{2,1,0:T(1,128)S(1)}, u32[]{:S(2)}, u32[]{:S(2)}) async-start(f32[128,1,128]{2,1,0:T(1,128)} %bitcast.19), calls=%async_computation | async-start | bytes 131072 | tf_op jit(solution)/shard_map/all_to_all | solution.py:632
  23.7 92.2 %all-gather.3.cloned.1.call-start = ((), (), s32[]{:S(2)}) async-start(), calls=%async_computation.3 | async-start | bytes 1056768 | tf_op jit(solution)/shard_map/all_gather | solution.py:638
  26.5 35.3 %collective-permute-start = (f32[20,8,256]{2,1,0:T(8,128)}, f32[20,8,256]{2,1,0:T(8,128)S(1)}, u32[]{:S(2)}, u32[]{:S(2)}) collective-permute-start(f32[20,8,256]{2,1,0:T(8,128)} %get-tuple-element.41), channel_id=1, source_target_pairs={{0,1},{1,2},{2,3},{3,4},{4,5},{5,6},{6,7},{7,8},{8,9},{9,10},{10,1... | collective-permute-start | bytes 491528 | tf_op jit(solution)/shard_map/ppermute | solution.py:621
  29.9 31.9 %collective-permute-start.1 = (f32[20,8,256]{2,1,0:T(8,128)}, f32[20,8,256]{2,1,0:T(8,128)S(1)}, u32[]{:S(2)}, u32[]{:S(2)}) collective-permute-start(f32[20,8,256]{2,1,0:T(8,128)} %get-tuple-element.42), channel_id=1, source_target_pairs={{1,0},{2,1},{3,2},{4,3},{5,4},{6,5},{7,6},{8,7},{9,8},{10,9},{11,1... | collective-permute-start | bytes 491528 | tf_op jit(solution)/shard_map/ppermute | solution.py:621
  56.4 5.5 %collective-permute-start.2 = (f32[16,8,256]{2,1,0:T(8,128)}, f32[16,8,256]{2,1,0:T(8,128)S(1)}, u32[]{:S(2)}, u32[]{:S(2)}) collective-permute-start(f32[16,8,256]{2,1,0:T(8,128)} %get-tuple-element.45), channel_id=1, source_target_pairs={{0,1},{1,2},{2,3},{3,4},{4,5},{5,6},{6,7},{7,8},{8,9},{9,10},{10,1... | collective-permute-start | bytes 393224 | tf_op jit(solution)/shard_map/ppermute | solution.py:621
  59.5 6.5 %collective-permute-start.3 = (f32[16,8,256]{2,1,0:T(8,128)}, f32[16,8,256]{2,1,0:T(8,128)S(1)}, u32[]{:S(2)}, u32[]{:S(2)}) collective-permute-start(f32[16,8,256]{2,1,0:T(8,128)} %get-tuple-element.46), channel_id=1, source_target_pairs={{1,0},{2,1},{3,2},{4,3},{5,4},{6,5},{7,6},{8,7},{9,8},{10,9},{11,1... | collective-permute-start | bytes 393224 | tf_op jit(solution)/shard_map/ppermute | solution.py:621
  61.8 11.0 %copy-start.4 = (f32[20,8,256]{2,1,0:T(8,128)}, f32[20,8,256]{2,1,0:T(8,128)S(1)}, u32[]{:S(2)}) copy-start(f32[20,8,256]{2,1,0:T(8,128)S(1)} %collective-permute-done.q_ylo) | copy-start | bytes 491524
  61.8 11.0 %copy-start.12 = (f32[4,16,256]{2,1,0:T(8,128)S(1)}, f32[4,16,256]{2,1,0:T(8,128)}, u32[]{:S(2)}) copy-start(f32[4,16,256]{2,1,0:T(8,128)} %get-tuple-element.50) | copy-start | bytes 196612
  61.9 11.0 %copy-start.5 = (f32[20,8,256]{2,1,0:T(8,128)}, f32[20,8,256]{2,1,0:T(8,128)S(1)}, u32[]{:S(2)}) copy-start(f32[20,8,256]{2,1,0:T(8,128)S(1)} %collective-permute-done.1.q_yhi) | copy-start | bytes 491524
  61.9 11.0 %copy-start.7 = (f32[16,8,256]{2,1,0:T(8,128)}, f32[16,8,256]{2,1,0:T(8,128)S(1)}, u32[]{:S(2)}) copy-start(f32[16,8,256]{2,1,0:T(8,128)S(1)} %collective-permute-done.2.r_ylo) | copy-start | bytes 393220
  65.9 16.5 %copy-start.8 = (f32[16,8,256]{2,1,0:T(8,128)}, f32[16,8,256]{2,1,0:T(8,128)S(1)}, u32[]{:S(2)}) copy-start(f32[16,8,256]{2,1,0:T(8,128)S(1)} %collective-permute-done.3.r_yhi) | copy-start | bytes 393220
  66.0 11.1 %collective-permute-start.4 = (f32[11,48,256]{2,1,0:T(8,128)S(1)}, f32[11,48,256]{2,1,0:T(8,128)S(1)}, u32[]{:S(2)}, u32[]{:S(2)}) collective-permute-start(f32[11,48,256]{2,1,0:T(8,128)S(1)} %maximum_maximum_fusion), channel_id=1, source_target_pairs={{0,16},{16,32},{32,48},{48,64},{64,80},{80,96},{96,112},{1,17},{17... | collective-permute-start | bytes 1622024 | tf_op jit(solution)/shard_map/ppermute | solution.py:621
  70.9 11.5 %collective-permute-start.5 = (f32[11,48,256]{2,1,0:T(8,128)S(1)}, f32[11,48,256]{2,1,0:T(8,128)S(1)}, u32[]{:S(2)}, u32[]{:S(2)}) collective-permute-start(f32[11,48,256]{2,1,0:T(8,128)S(1)} %maximum_maximum_fusion.1), channel_id=1, source_target_pairs={{16,0},{32,16},{48,32},{64,48},{80,64},{96,80},{112,96},{17,1},{33... | collective-permute-start | bytes 1622024 | tf_op jit(solution)/shard_map/ppermute | solution.py:621
  77.1 5.3 %copy-start.2 = (f32[11,48,256]{2,1,0:T(8,128)}, f32[11,48,256]{2,1,0:T(8,128)S(1)}, u32[]{:S(2)}) copy-start(f32[11,48,256]{2,1,0:T(8,128)S(1)} %collective-permute-done.4.xlo) | copy-start | bytes 1622020
  82.5 0.8 copy-start.3
  91.3 4.4 %collective-permute-start.6 = (f32[8,8,128]{2,1,0:T(8,128)}, f32[8,8,128]{2,1,0:T(8,128)S(1)}, u32[]{:S(2)}, u32[]{:S(2)}) collective-permute-start(f32[8,8,128]{2,1,0:T(8,128)} %get-tuple-element.47), channel_id=1, source_target_pairs={{0,1},{1,2},{2,3},{3,4},{4,5},{5,6},{6,7},{7,8},{8,9},{9,10},{10,1... | collective-permute-start | bytes 98312 | tf_op jit(solution)/shard_map/ppermute | solution.py:621
  94.3 6.0 %collective-permute-start.7 = (f32[8,8,128]{2,1,0:T(8,128)}, f32[8,8,128]{2,1,0:T(8,128)S(1)}, u32[]{:S(2)}, u32[]{:S(2)}) collective-permute-start(f32[8,8,128]{2,1,0:T(8,128)} %get-tuple-element.49), channel_id=1, source_target_pairs={{1,0},{2,1},{3,2},{4,3},{5,4},{6,5},{7,6},{8,7},{9,8},{10,9},{11,1... | collective-permute-start | bytes 98312 | tf_op jit(solution)/shard_map/ppermute | solution.py:621
  101.2 8.9 %copy-start.1 = (f32[16,32,128]{2,1,0:T(8,128)}, f32[16,32,128]{2,1,0:T(8,128)S(1)}, u32[]{:S(2)}) copy-start(f32[16,32,128]{2,1,0:T(8,128)S(1)} %pad_maximum_fusion.own) | copy-start | bytes 786436
  101.2 7.7 %collective-permute-start.9 = (f32[16,32,128]{2,1,0:T(8,128)S(1)}, f32[16,32,128]{2,1,0:T(8,128)S(1)}, u32[]{:S(2)}, u32[]{:S(2)}) collective-permute-start(f32[16,32,128]{2,1,0:T(8,128)S(1)} %pad_maximum_fusion.own), channel_id=1, source_target_pairs={{16,0},{32,16},{48,32},{64,48},{80,64},{96,80},{112,96},{17,1},{33... | collective-permute-start | bytes 786440 | tf_op jit(solution)/shard_map/ppermute | solution.py:621
  103.1 6.9 %collective-permute-start.8 = (f32[16,32,128]{2,1,0:T(8,128)S(1)}, f32[16,32,128]{2,1,0:T(8,128)S(1)}, u32[]{:S(2)}, u32[]{:S(2)}) collective-permute-start(f32[16,32,128]{2,1,0:T(8,128)S(1)} %pad_maximum_fusion.own), channel_id=1, source_target_pairs={{0,16},{16,32},{32,48},{48,64},{64,80},{80,96},{96,112},{1,17},{17... | collective-permute-start | bytes 786440 | tf_op jit(solution)/shard_map/ppermute | solution.py:621
  108.9 1.2 copy-start.9
  115.9 24.4 %all-to-all-start.1 = ((f32[64,16,128]{2,1,0:T(8,128)}), f32[64,16,128]{2,1,0:T(8,128)S(1)}, u32[]{:S(2)}, u32[]{:S(2)}) async-start(f32[64,16,128]{2,1,0:T(8,128)} %get-tuple-element.52), calls=%async_computation.1 | async-start | bytes 1048576 | tf_op jit(solution)/shard_map/all_to_all | solution.py:679
  140.3 4.6 %copy-start = (f32[64,16,128]{2,1,0:T(8,128)}, f32[64,16,128]{2,1,0:T(8,128)S(1)}, u32[]{:S(2)}) copy-start(f32[64,16,128]{2,1,0:T(8,128)S(1)} %all-to-all-done.1.r2_mine) | copy-start | bytes 1572868
  140.3 4.6 %collective-permute-start.10 = (f32[64,16,128]{2,1,0:T(8,128)S(1)}, f32[64,16,128]{2,1,0:T(8,128)S(1)}, u32[]{:S(2)}, u32[]{:S(2)}) collective-permute-start(f32[64,16,128]{2,1,0:T(8,128)S(1)} %all-to-all-done.1.r2_mine), channel_id=1, source_target_pairs={{0,16},{16,0},{1,17},{17,1},{2,18},{18,2},{3,19},{19,3},{4,20},{20... | collective-permute-start | bytes 1572872 | tf_op jit(solution)/shard_map/ppermute | solution.py:683
  (3 other events, 2.1 us)
Sparse Core Ops, SparseCore 0:
  27.3 66.3 all-gather.2

commit v5 on v4

--- a/solution.py
+++ b/solution.py
@@ -321,18 +321,18 @@
 
 
 def down_kernel(
-    q_own, q_ylo, q_yhi, r_own, r_ylo, r_yhi, xlo, xhi,
+    q_own, q_ylo, q_yhi, q_xlo, q_xhi, r_own, r_ylo, r_yhi, r_xlo, r_xhi,
     q_out, w_out, r_out, e_out, r1_ref, low_ref, high_ref,
     q, w, r, e, c, e2, c2, diag, pairs, sems,
 ):
     boxed = box_parity
-    q[0:6] = xlo[5:11]
-    q[22:28] = xhi[5:11]
+    q[0:6] = q_xlo[0:288].reshape(6, 48, 256)
+    q[22:28] = q_xhi[0:288].reshape(6, 48, 256)
     q[6:22, 0:8] = q_ylo[0:16]
     q[6:22, 8:40] = q_own[...]
     q[6:22, 40:48] = q_yhi[0:16]
-    r[1:6] = xlo[0:5]
-    r[22:27] = xhi[0:5]
+    r[1:6] = r_xlo[...]
+    r[22:27] = r_xhi[...]
     r[6:22, 0:8] = r_ylo[...]
     r[6:22, 8:40] = r_own[...]
     r[6:22, 40:48] = r_yhi[...]
@@ -364,15 +364,17 @@
 
 
 def down_one_kernel(
-    own, xlo, xhi,
+    own, xlo, xhi, q_own, q_xlo, q_xhi,
     q, w, r, e, out_ref,
     c, e2, c2, diag, pairs,
 ):
     z = iota((32, 128), 1)
     boxed = functools.partial(box, z=z, depth=128)
     for i, side in enumerate((xlo, own, xhi)):
-        r[8 * i : 8 * i + 8] = side[0:8]
-        q[8 * i : 8 * i + 8] = side[8:16]
+        r[8 * i : 8 * i + 8] = side[...]
+    for i, side in enumerate((q_xlo[288:416].reshape(4, 32, 256), q_own[...], q_xhi[288:416].reshape(4, 32, 256))):
+        q[8 * i : 8 * i + 4] = side[:, :, :128]
+        q[8 * i + 4 : 8 * i + 8] = side[:, :, 128:]
     set_weights(q, w, diag, 1, 23, boxed)
     first_guess(e, c, q, w, r, 1, 23)
     sweep(e, c, e2, c2, q, w, r, 2, 22, boxed)
@@ -637,6 +639,17 @@
     )
     q2_all = lax.all_gather(q2[None], ALL, axis=0, tiled=True)
     q_ylo, q_yhi = swap(q_low, q_high, "by", NY)
+
+    def faces(lo, own, hi, planes):
+        return jnp.concatenate([lo[planes], own[planes], hi[planes]], axis=1)
+
+    q1_cat = faces(q_ylo[16:], q1, q_yhi[16:], slice(0, 4))
+
+    def q_faces(planes):
+        return jnp.concatenate([faces(q_ylo, q, q_yhi, planes).reshape(288, 256), q1_cat.reshape(128, 256)])
+
+    q_xlo, q_xhi = swap(q_faces(slice(0, 6)), q_faces(slice(10, 16)), BX, NX)
+
     rhs, r_low, r_high = call(
         deposit_kernel,
         (struct(16, 32, 256), struct(16, 8, 256), struct(16, 8, 256)),
@@ -644,35 +657,26 @@
         scratch=(((512, 256), F32), ((32, GROUP), F32)),
     )
     r_ylo, r_yhi = swap(r_low, r_high, "by", NY)
-
-    def faces(r_planes, q_planes):
-        return jnp.concatenate(
-            [
-                jnp.concatenate([lo[planes], own[planes], hi[planes]], axis=1)
-                for lo, own, hi, planes in ((r_ylo, rhs, r_yhi, r_planes), (q_ylo, q, q_yhi, q_planes))
-            ]
-        )
-
-    xlo, xhi = swap(faces(slice(0, 5), slice(0, 6)), faces(slice(11, 16), slice(10, 16)), BX, NX)
+    r_xlo, r_xhi = swap(
+        faces(r_ylo, rhs, r_yhi, slice(0, 5)), faces(r_ylo, rhs, r_yhi, slice(11, 16)), BX, NX
+    )
 
     ext0, ext1 = (28, 48, 256), (24, 32, 128)
     q0e, w0e, r0e, e0e, r1, low1, high1 = call(
         down_kernel,
         (struct(*ext0),) * 4 + (struct(8, 16, 128), struct(8, 8, 128), struct(8, 8, 128)),
-        q, q_ylo, q_yhi, rhs, r_ylo, r_yhi, xlo, xhi,
+        q, q_ylo, q_yhi, q_xlo, q_xhi, rhs, r_ylo, r_yhi, r_xlo, r_xhi,
         left_out=4,
         scratch=((ext0, F32),) * 8 + (((8, 32, 256), F32),),
     )
     r1_ylo, r1_yhi = swap(low1, high1, "by", NY)
-    q1_cat = jnp.concatenate([q_ylo[16:], q1, q_yhi[16:]], axis=1)
-    q1_cat = jnp.concatenate([q1_cat[:, :, :128], q1_cat[:, :, 128:]])
-    cat1 = jnp.concatenate([jnp.concatenate([r1_ylo, r1, r1_yhi], axis=1), q1_cat])
+    cat1 = jnp.concatenate([r1_ylo, r1, r1_yhi], axis=1)
     xlo1, xhi1 = swap(cat1, cat1, BX, NX)
 
     q1e, w1e, r1e, e1e, r2_out = call(
         down_one_kernel,
         (struct(*ext1),) * 4 + (struct(CHIPS, 16, 128),),
-        cat1, xlo1, xhi1,
+        cat1, xlo1, xhi1, q1_cat, q_xlo, q_xhi,
         scratch=((ext1, F32),) * 4 + (((4, 16, 128), F32),),
     )
     q2_all, r2_out = lax.optimization_barrier((q2_all, r2_out))

time: 215 us -> 213 us (level)
  waiting for transfers between devices: 28.9 us -> 18 us
  starting transfers between devices: 53.9 us -> 61.1 us
    ppermute x5 -> x6, waiting for transfers between devices: 16.1 us -> 6.25 us  [swap(): lax.ppermute(to_lower, axis, down)]
    ppermute x5 -> x6, starting transfers between devices: 7.72 us -> 10.8 us  [swap(): lax.ppermute(to_lower, axis, down)]
    unnamed x26 -> x34, local copies, waits for them, and re-layouts: 2.99 us -> 5.12 us
    ppermute x5 -> x6, starting transfers between devices: 18 us -> 19.8 us  [swap(): lax.ppermute(to_upper, axis, up)]
    ppermute x5 -> x6, waiting for transfers between devices: 5.4 us -> 4.45 us  [swap(): lax.ppermute(to_upper, axis, up)]
  transfers between devices with their start and end apart: 14 -> 16, of which waited for: 9 -> 8; matrix products, arithmetic and copies ran while one was open for 2% -> 2% of each run, Pallas kernels for 20% -> 21%
where the time goes in v5:
time: 213 us; the launch traced here: 212 us
  Pallas kernels  95.1 us (45%)
  starting transfers between devices  61.1 us (29%)
  waiting for transfers between devices  18 us (8%)
  between operations  15 us (7%)
  blocking collectives  14.6 us (7%)
  local copies, waits for them, and re-layouts  7.23 us (3%)
    pallas_call x8, Pallas kernels, call(): pl.pallas_call(kernel, out_shape=outs, in_specs=[pl.BlockSpec(memory_spac...  95.1 us
    ppermute x6, starting transfers between devices, swap(): lax.ppermute(to_upper, axis, up)  19.8 us
    all_to_all x1, starting transfers between devices, shards(): lax.all_to_all(r2_out, ('x', 'by'), split_axis=0, concat_axis=0, tiled=True)  15.3 us
    all_to_all x1, blocking collectives, shards(): lax.all_to_all(back, ALL, split_axis=0, concat_axis=0, tiled=True)  14.6 us
    all_to_all x1, starting transfers between devices, shards(): lax.all_to_all(outgoing, ALL, split_axis=0, concat_axis=0, tiled=True)  11.5 us
    ppermute x6, starting transfers between devices, swap(): lax.ppermute(to_lower, axis, down)  10.8 us
    ppermute x6, waiting for transfers between devices, swap(): lax.ppermute(to_lower, axis, down)  6.25 us
    all_to_all x1, waiting for transfers between devices, shards(): lax.all_to_all(r2_out, ('x', 'by'), split_axis=0, concat_axis=0, tiled=True)  5.36 us
  transfers between devices with their start and end apart: 16, of which 8 were waited for; matrix products, arithmetic and copies ran while one was open for 2% of the time, Pallas kernels for 21%

profile of v5, /device:TPU:1, one launch (start us, length us, event | category | flops | bytes accessed | tf_op | source)
XLA Modules:
  0.0 211.8 jit_solution(13126757031280660483)
XLA Ops:
  7.8 4.3 %shard_map.96 = (f32[128,128]{1,0:T(8,128)}, s32[64,128]{1,0:T(8,128)}) custom-call(s32[1]{0:T(128)S(6)} %copy.14.active_ref, s32[64,128]{1,0:T(8,128)} %bitcast.23, f32[64,128]{1,0:T(8,128)} %bitcast.28), custom_call_target="tpu_custom_call" | custom-call | tf_op jit(solution)/shard_map/pallas_call | solution.py:606
  12.1 11.5 %all-to-all-start = ((f32[128,1,128]{2,1,0:T(1,128)}), f32[128,1,128]{2,1,0:T(1,128)S(1)}, u32[]{:S(2)}, u32[]{:S(2)}) async-start(f32[128,1,128]{2,1,0:T(1,128)} %bitcast.25), calls=%async_computation | async-start | bytes 131072 | tf_op jit(solution)/shard_map/all_to_all | solution.py:634
  23.7 2.8 %shard_map.95 = (f32[16,32,256]{2,1,0:T(8,128)}, f32[4,16,256]{2,1,0:T(8,128)}, f32[20,8,256]{2,1,0:T(8,128)}, f32[20,8,256]{2,1,0:T(8,128)}, f32[16,128]{1,0:T(8,128)}) custom-call(f32[16,32,256]{2,1,0:T(8,128)} %base_ref.1, f32[16,32,256]{2,1,0:T(8,128)} %state_ref.1), custom_call_target="tpu_custom_call" | custom-call | tf_op jit(solution)/shard_map/pallas_call | solution.py:606
  26.5 3.4 %collective-permute-start = (f32[20,8,256]{2,1,0:T(8,128)}, f32[20,8,256]{2,1,0:T(8,128)S(1)}, u32[]{:S(2)}, u32[]{:S(2)}) collective-permute-start(f32[20,8,256]{2,1,0:T(8,128)} %get-tuple-element.41), channel_id=1, source_target_pairs={{0,1},{1,2},{2,3},{3,4},{4,5},{5,6},{6,7},{7,8},{8,9},{9,10},{10,1... | collective-permute-start | bytes 491528 | tf_op jit(solution)/shard_map/ppermute | solution.py:623
  33.9 22.6 %shard_map.97 = (f32[16,32,256]{2,1,0:T(8,128)}, f32[16,8,256]{2,1,0:T(8,128)}, f32[16,8,256]{2,1,0:T(8,128)}) custom-call(f32[128,128]{1,0:T(8,128)} %bitcast.21, s32[4,12288]{1,0:T(4,128)} %refs_8_.1, s32[4,12288]{1,0:T(4,128)} %refs_9_.1, f32[4,12288]{1,0:T(4,128)} %refs_10_.1), custom_call_target="tpu_custom_call" | custom-call | tf_op jit(solution)/shard_map/pallas_call | solution.py:606
  56.4 3.0 %collective-permute-start.4 = (f32[16,8,256]{2,1,0:T(8,128)}, f32[16,8,256]{2,1,0:T(8,128)S(1)}, u32[]{:S(2)}, u32[]{:S(2)}) collective-permute-start(f32[16,8,256]{2,1,0:T(8,128)} %get-tuple-element.46), channel_id=1, source_target_pairs={{0,1},{1,2},{2,3},{3,4},{4,5},{5,6},{6,7},{7,8},{8,9},{9,10},{10,1... | collective-permute-start | bytes 393224 | tf_op jit(solution)/shard_map/ppermute | solution.py:623
  62.6 3.1 %collective-permute-start.3 = (f32[416,256]{1,0:T(8,128)S(1)}, f32[416,256]{1,0:T(8,128)S(1)}, u32[]{:S(2)}, u32[]{:S(2)}) collective-permute-start(f32[416,256]{1,0:T(8,128)S(1)} %get-tuple-element.88), channel_id=1, source_target_pairs={{16,0},{32,16},{48,32},{64,48},{80,64},{96,80},{112,96},{17,1},{33... | collective-permute-start | bytes 1277960 | tf_op jit(solution)/shard_map/ppermute | solution.py:623
  65.7 3.0 %collective-permute-start.2 = (f32[416,256]{1,0:T(8,128)S(1)}, f32[416,256]{1,0:T(8,128)S(1)}, u32[]{:S(2)}, u32[]{:S(2)}) collective-permute-start(f32[416,256]{1,0:T(8,128)S(1)} %get-tuple-element.89), channel_id=1, source_target_pairs={{0,16},{16,32},{32,48},{48,64},{64,80},{80,96},{96,112},{1,17},{17... | collective-permute-start | bytes 1277960 | tf_op jit(solution)/shard_map/ppermute | solution.py:623
  68.9 2.4 %collective-permute-start.6 = (f32[5,48,256]{2,1,0:T(8,128)S(1)}, f32[5,48,256]{2,1,0:T(8,128)S(1)}, u32[]{:S(2)}, u32[]{:S(2)}) collective-permute-start(f32[5,48,256]{2,1,0:T(8,128)S(1)} %pad_maximum_fusion.4), channel_id=1, source_target_pairs={{0,16},{16,32},{32,48},{48,64},{64,80},{80,96},{96,112},{1,17},{17... | collective-permute-start | bytes 737288 | tf_op jit(solution)/shard_map/ppermute | solution.py:623
  71.3 1.9 collective-permute-start.7
  73.2 3.2 %collective-permute-done.6.r_xlo = f32[5,48,256]{2,1,0:T(8,128)S(1)} collective-permute-done((f32[5,48,256]{2,1,0:T(8,128)S(1)}, f32[5,48,256]{2,1,0:T(8,128)S(1)}, u32[]{:S(2)}, u32[]{:S(2)}) %collective-permute-start.6) | collective-permute-done | bytes 245792 | tf_op jit(solution)/shard_map/ppermute | solution.py:623
  76.5 2.4 %collective-permute-done.7.r_xhi = f32[5,48,256]{2,1,0:T(8,128)S(1)} collective-permute-done((f32[5,48,256]{2,1,0:T(8,128)S(1)}, f32[5,48,256]{2,1,0:T(8,128)S(1)}, u32[]{:S(2)}, u32[]{:S(2)}) %collective-permute-start.7) | collective-permute-done | bytes 245792 | tf_op jit(solution)/shard_map/ppermute | solution.py:623
  80.5 8.0 %shard_map.98 = (f32[28,48,256]{2,1,0:T(8,128)}, f32[28,48,256]{2,1,0:T(8,128)}, f32[28,48,256]{2,1,0:T(8,128)}, f32[28,48,256]{2,1,0:T(8,128)}, f32[8,16,128]{2...) custom-call(f32[16,32,256]{2,1,0:T(8,128)} %get-tuple-element.40.q_own, f32[20,8,256]{2,1,0:T(8,128)} %copy-done.4, ...), custom_call_target="tpu_custom_call" | custom-call | tf_op jit(solution)/shard_map/pallas_call | solution.py:606
  88.5 4.3 %collective-permute-start.8 = (f32[8,8,128]{2,1,0:T(8,128)}, f32[8,8,128]{2,1,0:T(8,128)S(1)}, u32[]{:S(2)}, u32[]{:S(2)}) collective-permute-start(f32[8,8,128]{2,1,0:T(8,128)} %get-tuple-element.48), channel_id=1, source_target_pairs={{0,1},{1,2},{2,3},{3,4},{4,5},{5,6},{6,7},{7,8},{8,9},{9,10},{10,1... | collective-permute-start | bytes 98312 | tf_op jit(solution)/shard_map/ppermute | solution.py:623
  95.0 3.2 %collective-permute-done.9 = f32[8,8,128]{2,1,0:T(8,128)S(1)} collective-permute-done((f32[8,8,128]{2,1,0:T(8,128)}, f32[8,8,128]{2,1,0:T(8,128)S(1)}, u32[]{:S(2)}, u32[]{:S(2)}) %collective-permute-start.9) | collective-permute-done | bytes 32800 | tf_op jit(solution)/shard_map/ppermute | solution.py:623
  100.1 3.6 %collective-permute-start.10 = (f32[8,32,128]{2,1,0:T(8,128)S(1)}, f32[8,32,128]{2,1,0:T(8,128)S(1)}, u32[]{:S(2)}, u32[]{:S(2)}) collective-permute-start(f32[8,32,128]{2,1,0:T(8,128)S(1)} %constant_dynamic-update-slice_fusion.own), channel_id=1, source_target_pairs={{0,16},{16,32},{32,48},{48,64},{64,80},{80,96},{96,112},{1,17},{17... | collective-permute-start | bytes 393224 | tf_op jit(solution)/shard_map/ppermute | solution.py:623
  106.3 5.4 %shard_map.99 = (f32[24,32,128]{2,1,0:T(8,128)}, f32[24,32,128]{2,1,0:T(8,128)}, f32[24,32,128]{2,1,0:T(8,128)}, f32[24,32,128]{2,1,0:T(8,128)}, f32[64,16,128]{2,1,0:T(8,128)}) custom-call(f32[8,32,128]{2,1,0:T(8,128)} %copy-done.12, f32[8,32,128]{2,1,0:T(8,128)} %copy-done.14, f32[8,32,128]{2,1,0:T(8,128)} %copy-done.13, f32[4,32,256]{2,1,0:T(8,128)} %copy-done.3, ...), custom_call_target="tpu_custom_call" | custom-call | tf_op jit(solution)/shard_map/pallas_call | solution.py:606
  111.7 15.3 %all-to-all-start.1 = ((f32[64,16,128]{2,1,0:T(8,128)}), f32[64,16,128]{2,1,0:T(8,128)S(1)}, u32[]{:S(2)}, u32[]{:S(2)}) async-start(f32[64,16,128]{2,1,0:T(8,128)} %get-tuple-element.52), calls=%async_computation.1 | async-start | bytes 1048576 | tf_op jit(solution)/shard_map/all_to_all | solution.py:683
  127.1 5.3 %shard_map.100 = (f32[10,128,256]{2,1,0:T(8,128)}, f32[10,128,256]{2,1,0:T(8,128)}, f32[10,128,256]{2,1,0:T(8,128)}, f32[6,64,128]{2,1,0:T(8,128)}, f32[6,64,128]{2,1,0:T(8,128)}) custom-call(f32[128,16,128]{2,1,0:T(8,128)} %bitcast.20), custom_call_target="tpu_custom_call" | custom-call | tf_op jit(solution)/shard_map/pallas_call | solution.py:606
  132.4 5.4 %all-to-all-done.1.r2_mine = f32[64,16,128]{2,1,0:T(8,128)S(1)} async-done(((f32[64,16,128]{2,1,0:T(8,128)}), f32[64,16,128]{2,1,0:T(8,128)S(1)}, u32[]{:S(2)}, u32[]{:S(2)}) %all-to-all-start.1) | async-done | bytes 524320 | tf_op jit(solution)/shard_map/all_to_all | solution.py:683
  137.8 3.5 %collective-permute-start.12 = (f32[64,16,128]{2,1,0:T(8,128)S(1)}, f32[64,16,128]{2,1,0:T(8,128)S(1)}, u32[]{:S(2)}, u32[]{:S(2)}) collective-permute-start(f32[64,16,128]{2,1,0:T(8,128)S(1)} %all-to-all-done.1.r2_mine), channel_id=1, source_target_pairs={{0,16},{16,0},{1,17},{17,1},{2,18},{18,2},{3,19},{19,3},{4,20},{20... | collective-permute-start | bytes 1572872 | tf_op jit(solution)/shard_map/ppermute | solution.py:687
  143.6 43.7 %shard_map.101 = (f32[16,32,256]{2,1,0:T(8,128)}, f32[128,128]{1,0:T(8,128)}) custom-call(s32[2]{0:T(128)} %pad_add_fusion.place_ref, f32[64,16,128]{2,1,0:T(8,128)} %copy-done, f32[64,16,128]{2,1,0:T(8,128)} %copy-done.6, f32[10,128,256]{2,1,0:T(8,128)} %get-tuple-element.60.q2, f32[10,128,256]{2,1,0:T(8,128)} %get-tuple-element.61.w2, ...), custom_call_target="tpu_custom_call" | custom-call | tf_op jit(solution)/shard_map/pallas_call | solution.py:606
  187.3 14.6 %all_to_all.27 = f32[128,1,128]{2,1,0:T(1,128)} all-to-all(f32[128,1,128]{2,1,0:T(1,128)} %bitcast.26), channel_id=1, replica_groups=mesh['x'=4,'core'=2,'by'=16] {'x','core','by'}, dimensions={0} | all-to-all | bytes 131072 | tf_op jit(solution)/shard_map/all_to_all | solution.py:703
  201.9 3.0 %shard_map.102 = f32[64,128]{1,0:T(8,128)} custom-call(s32[1]{0:T(128)S(6)} %copy.14.active_ref, s32[64,128]{1,0:T(8,128)} %bitcast.24, s32[64,128]{1,0:T(8,128)} %get-tuple-element.74.rank_ref, f32[128,128]{1,0:T(8,128)} %bitcast.22), custom_call_target="tpu_custom_call" | custom-call | tf_op jit(solution)/shard_map/pallas_call | solution.py:606
  (67 shorter events, 17.7 us)
Async XLA Ops:
  12.1 21.1 %all-to-all-start = ((f32[128,1,128]{2,1,0:T(1,128)}), f32[128,1,128]{2,1,0:T(1,128)S(1)}, u32[]{:S(2)}, u32[]{:S(2)}) async-start(f32[128,1,128]{2,1,0:T(1,128)} %bitcast.25), calls=%async_computation | async-start | bytes 131072 | tf_op jit(solution)/shard_map/all_to_all | solution.py:634
  23.7 88.1 %all-gather.3.cloned.1.call-start = ((), (), s32[]{:S(2)}) async-start(), calls=%async_computation.3 | async-start | bytes 1056768 | tf_op jit(solution)/shard_map/all_gather | solution.py:640
  26.5 35.4 %copy-start.15 = (f32[4,16,256]{2,1,0:T(8,128)S(1)}, f32[4,16,256]{2,1,0:T(8,128)}, u32[]{:S(2)}) copy-start(f32[4,16,256]{2,1,0:T(8,128)} %get-tuple-element.43) | copy-start | bytes 196612
  26.5 35.3 %collective-permute-start = (f32[20,8,256]{2,1,0:T(8,128)}, f32[20,8,256]{2,1,0:T(8,128)S(1)}, u32[]{:S(2)}, u32[]{:S(2)}) collective-permute-start(f32[20,8,256]{2,1,0:T(8,128)} %get-tuple-element.41), channel_id=1, source_target_pairs={{0,1},{1,2},{2,3},{3,4},{4,5},{5,6},{6,7},{7,8},{8,9},{9,10},{10,1... | collective-permute-start | bytes 491528 | tf_op jit(solution)/shard_map/ppermute | solution.py:623
  29.9 31.9 %collective-permute-start.1 = (f32[20,8,256]{2,1,0:T(8,128)}, f32[20,8,256]{2,1,0:T(8,128)S(1)}, u32[]{:S(2)}, u32[]{:S(2)}) collective-permute-start(f32[20,8,256]{2,1,0:T(8,128)} %get-tuple-element.42), channel_id=1, source_target_pairs={{1,0},{2,1},{3,2},{4,3},{5,4},{6,5},{7,6},{8,7},{9,8},{10,9},{11,1... | collective-permute-start | bytes 491528 | tf_op jit(solution)/shard_map/ppermute | solution.py:623
  56.4 12.3 %collective-permute-start.4 = (f32[16,8,256]{2,1,0:T(8,128)}, f32[16,8,256]{2,1,0:T(8,128)S(1)}, u32[]{:S(2)}, u32[]{:S(2)}) collective-permute-start(f32[16,8,256]{2,1,0:T(8,128)} %get-tuple-element.46), channel_id=1, source_target_pairs={{0,1},{1,2},{2,3},{3,4},{4,5},{5,6},{6,7},{7,8},{8,9},{9,10},{10,1... | collective-permute-start | bytes 393224 | tf_op jit(solution)/shard_map/ppermute | solution.py:623
  59.5 9.3 %collective-permute-start.5 = (f32[16,8,256]{2,1,0:T(8,128)}, f32[16,8,256]{2,1,0:T(8,128)S(1)}, u32[]{:S(2)}, u32[]{:S(2)}) collective-permute-start(f32[16,8,256]{2,1,0:T(8,128)} %get-tuple-element.47), channel_id=1, source_target_pairs={{1,0},{2,1},{3,2},{4,3},{5,4},{6,5},{7,6},{8,7},{9,8},{10,9},{11,1... | collective-permute-start | bytes 393224 | tf_op jit(solution)/shard_map/ppermute | solution.py:623
  62.6 16.2 %collective-permute-start.3 = (f32[416,256]{1,0:T(8,128)S(1)}, f32[416,256]{1,0:T(8,128)S(1)}, u32[]{:S(2)}, u32[]{:S(2)}) collective-permute-start(f32[416,256]{1,0:T(8,128)S(1)} %get-tuple-element.88), channel_id=1, source_target_pairs={{16,0},{32,16},{48,32},{64,48},{80,64},{96,80},{112,96},{17,1},{33... | collective-permute-start | bytes 1277960 | tf_op jit(solution)/shard_map/ppermute | solution.py:623
  65.7 13.1 %collective-permute-start.2 = (f32[416,256]{1,0:T(8,128)S(1)}, f32[416,256]{1,0:T(8,128)S(1)}, u32[]{:S(2)}, u32[]{:S(2)}) collective-permute-start(f32[416,256]{1,0:T(8,128)S(1)} %get-tuple-element.89), channel_id=1, source_target_pairs={{0,16},{16,32},{32,48},{48,64},{64,80},{80,96},{96,112},{1,17},{17... | collective-permute-start | bytes 1277960 | tf_op jit(solution)/shard_map/ppermute | solution.py:623
  68.8 10.1 %copy-start.7 = (f32[16,8,256]{2,1,0:T(8,128)}, f32[16,8,256]{2,1,0:T(8,128)S(1)}, u32[]{:S(2)}) copy-start(f32[16,8,256]{2,1,0:T(8,128)S(1)} %collective-permute-done.4.r_ylo) | copy-start | bytes 393220
  68.8 10.0 %copy-start.8 = (f32[16,8,256]{2,1,0:T(8,128)}, f32[16,8,256]{2,1,0:T(8,128)S(1)}, u32[]{:S(2)}) copy-start(f32[16,8,256]{2,1,0:T(8,128)S(1)} %collective-permute-done.5.r_yhi) | copy-start | bytes 393220
  68.9 7.6 %collective-permute-start.6 = (f32[5,48,256]{2,1,0:T(8,128)S(1)}, f32[5,48,256]{2,1,0:T(8,128)S(1)}, u32[]{:S(2)}, u32[]{:S(2)}) collective-permute-start(f32[5,48,256]{2,1,0:T(8,128)S(1)} %pad_maximum_fusion.4), channel_id=1, source_target_pairs={{0,16},{16,32},{32,48},{48,64},{64,80},{80,96},{96,112},{1,17},{17... | collective-permute-start | bytes 737288 | tf_op jit(solution)/shard_map/ppermute | solution.py:623
  71.3 7.5 %collective-permute-start.7 = (f32[5,48,256]{2,1,0:T(8,128)S(1)}, f32[5,48,256]{2,1,0:T(8,128)S(1)}, u32[]{:S(2)}, u32[]{:S(2)}) collective-permute-start(f32[5,48,256]{2,1,0:T(8,128)S(1)} %pad_maximum_fusion.5), channel_id=1, source_target_pairs={{16,0},{32,16},{48,32},{64,48},{80,64},{96,80},{112,96},{17,1},{33... | collective-permute-start | bytes 737288 | tf_op jit(solution)/shard_map/ppermute | solution.py:623
  76.4 2.4 %copy-start.10 = (f32[5,48,256]{2,1,0:T(8,128)}, f32[5,48,256]{2,1,0:T(8,128)S(1)}, u32[]{:S(2)}) copy-start(f32[5,48,256]{2,1,0:T(8,128)S(1)} %collective-permute-done.6.r_xlo) | copy-start | bytes 737284
  78.8 0.8 copy-start.1
  88.5 5.7 %collective-permute-start.8 = (f32[8,8,128]{2,1,0:T(8,128)}, f32[8,8,128]{2,1,0:T(8,128)S(1)}, u32[]{:S(2)}, u32[]{:S(2)}) collective-permute-start(f32[8,8,128]{2,1,0:T(8,128)} %get-tuple-element.48), channel_id=1, source_target_pairs={{0,1},{1,2},{2,3},{3,4},{4,5},{5,6},{6,7},{7,8},{8,9},{9,10},{10,1... | collective-permute-start | bytes 98312 | tf_op jit(solution)/shard_map/ppermute | solution.py:623
  92.8 5.3 %collective-permute-start.9 = (f32[8,8,128]{2,1,0:T(8,128)}, f32[8,8,128]{2,1,0:T(8,128)S(1)}, u32[]{:S(2)}, u32[]{:S(2)}) collective-permute-start(f32[8,8,128]{2,1,0:T(8,128)} %get-tuple-element.50), channel_id=1, source_target_pairs={{1,0},{2,1},{3,2},{4,3},{5,4},{6,5},{7,6},{8,7},{9,8},{10,9},{11,1... | collective-permute-start | bytes 98312 | tf_op jit(solution)/shard_map/ppermute | solution.py:623
  98.2 7.5 %copy-start.12 = (f32[8,32,128]{2,1,0:T(8,128)}, f32[8,32,128]{2,1,0:T(8,128)S(1)}, u32[]{:S(2)}) copy-start(f32[8,32,128]{2,1,0:T(8,128)S(1)} %constant_dynamic-update-slice_fusion.own) | copy-start | bytes 393220
  98.2 6.3 %collective-permute-start.11 = (f32[8,32,128]{2,1,0:T(8,128)S(1)}, f32[8,32,128]{2,1,0:T(8,128)S(1)}, u32[]{:S(2)}, u32[]{:S(2)}) collective-permute-start(f32[8,32,128]{2,1,0:T(8,128)S(1)} %constant_dynamic-update-slice_fusion.own), channel_id=1, source_target_pairs={{16,0},{32,16},{48,32},{64,48},{80,64},{96,80},{112,96},{17,1},{33... | collective-permute-start | bytes 393224 | tf_op jit(solution)/shard_map/ppermute | solution.py:623
  100.1 5.6 %collective-permute-start.10 = (f32[8,32,128]{2,1,0:T(8,128)S(1)}, f32[8,32,128]{2,1,0:T(8,128)S(1)}, u32[]{:S(2)}, u32[]{:S(2)}) collective-permute-start(f32[8,32,128]{2,1,0:T(8,128)S(1)} %constant_dynamic-update-slice_fusion.own), channel_id=1, source_target_pairs={{0,16},{16,32},{32,48},{48,64},{64,80},{80,96},{96,112},{1,17},{17... | collective-permute-start | bytes 393224 | tf_op jit(solution)/shard_map/ppermute | solution.py:623
  104.4 1.2 copy-start.13
  111.7 26.0 %all-to-all-start.1 = ((f32[64,16,128]{2,1,0:T(8,128)}), f32[64,16,128]{2,1,0:T(8,128)S(1)}, u32[]{:S(2)}, u32[]{:S(2)}) async-start(f32[64,16,128]{2,1,0:T(8,128)} %get-tuple-element.52), calls=%async_computation.1 | async-start | bytes 1048576 | tf_op jit(solution)/shard_map/all_to_all | solution.py:683
  137.8 5.1 %copy-start = (f32[64,16,128]{2,1,0:T(8,128)}, f32[64,16,128]{2,1,0:T(8,128)S(1)}, u32[]{:S(2)}) copy-start(f32[64,16,128]{2,1,0:T(8,128)S(1)} %all-to-all-done.1.r2_mine) | copy-start | bytes 1572868
  137.8 5.1 %collective-permute-start.12 = (f32[64,16,128]{2,1,0:T(8,128)S(1)}, f32[64,16,128]{2,1,0:T(8,128)S(1)}, u32[]{:S(2)}, u32[]{:S(2)}) collective-permute-start(f32[64,16,128]{2,1,0:T(8,128)S(1)} %all-to-all-done.1.r2_mine), channel_id=1, source_target_pairs={{0,16},{16,0},{1,17},{17,1},{2,18},{18,2},{3,19},{19,3},{4,20},{20... | collective-permute-start | bytes 1572872 | tf_op jit(solution)/shard_map/ppermute | solution.py:687
  (8 other events, 5.7 us)
Sparse Core Ops, SparseCore 0:
  27.3 66.4 all-gather.2

commit v6 on v5

--- a/solution.py
+++ b/solution.py
@@ -280,7 +280,7 @@
     lax.fori_loop(lo, hi, body, 0, unroll=unroll_of(q))
 
 
-def sweep(e, c, e2, c2, q, w, r, lo, hi, boxed):
+def sweep(e, c, e2, c2, q, w, r, lo, hi, boxed, unroll=None):
     def body(x, carry):
         new = 0.4 * e[x] + w[x] * (r[x] + flow(e, c, q, x, boxed))
         e2[x] = new
@@ -288,7 +288,7 @@
             c2[x] = q[x] * new
         return carry
 
-    lax.fori_loop(lo, hi, body, 0, unroll=unroll_of(q))
+    lax.fori_loop(lo, hi, body, 0, unroll=unroll or unroll_of(q))
 
 
 def pack_two(pairs):
@@ -343,8 +343,8 @@
     set_weights(q, w, diag, 1, 27, boxed)
     copies[2].start()
     first_guess(e, c, q, w, r, 1, 27)
-    sweep(e, c, e2, c2, q, w, r, 2, 26, boxed)
-    sweep(e2, c2, e, c, q, w, r, 3, 25, boxed)
+    sweep(e, c, e2, c2, q, w, r, 2, 26, boxed, unroll=8)
+    sweep(e2, c2, e, c, q, w, r, 3, 25, boxed, unroll=8)
     copies[3].start()
 
     def left(x):
@@ -354,7 +354,7 @@
         pairs[i] = left(6 + 2 * i) + left(7 + 2 * i)
         return carry
 
-    lax.fori_loop(0, 8, body, 0, unroll=UNROLL // 2)
+    lax.fori_loop(0, 8, body, 0, unroll=4)
     r1 = 0.5 * halve(pairs[...]).reshape(8, 16, 128)
     r1_ref[...] = r1
     low_ref[...] = r1[:, :8]
@@ -377,8 +377,8 @@
         q[8 * i + 4 : 8 * i + 8] = side[:, :, 128:]
     set_weights(q, w, diag, 1, 23, boxed)
     first_guess(e, c, q, w, r, 1, 23)
-    sweep(e, c, e2, c2, q, w, r, 2, 22, boxed)
-    sweep(e2, c2, e, c, q, w, r, 3, 21, boxed)
+    sweep(e, c, e2, c2, q, w, r, 2, 22, boxed, unroll=8)
+    sweep(e2, c2, e, c, q, w, r, 3, 21, boxed, unroll=8)
 
     def left(x):
         return (r[x] + flow(e, c, q, x, boxed) - diag[x] * e[x])[8:24]
@@ -387,7 +387,7 @@
         pairs[i] = left(8 + 2 * i) + left(9 + 2 * i)
         return carry
 
-    lax.fori_loop(0, 4, body, 0, unroll=UNROLL // 2)
+    lax.fori_loop(0, 4, body, 0, unroll=4)
     r2 = 0.5 * pack_two(pairs[...])
     out_ref[...] = jnp.broadcast_to(r2[None], (CHIPS, 16, 128))
 
@@ -683,10 +683,10 @@
     r2_mine = lax.all_to_all(r2_out, ("x", "by"), split_axis=0, concat_axis=0, tiled=True)
     whole2, whole3 = (10, 128, 256), (6, 64, 128)
     setup = call(setup_kernel, (struct(*whole2),) * 3 + (struct(*whole3),) * 2, q2_all)
-    r2_mine, setup = lax.optimization_barrier((r2_mine, setup))
+    place = jnp.stack([lax.axis_index(BX), lax.axis_index("by")]).astype(jnp.int32)
+    r2_mine, setup, place = lax.optimization_barrier((r2_mine, setup, place))
     r2_other = lax.ppermute(r2_mine, "core", [(0, 1), (1, 0)])
 
-    place = jnp.stack([lax.axis_index(BX), lax.axis_index("by")]).astype(jnp.int32)
     grid, back = call(
         up_kernel,
         (struct(16, 32, 256), struct(DEVICES, LANES)),

time: 213 us -> 213 us (level)
  no operation moved by 1% of the time
where the time goes in v6:
time: 213 us; the launch traced here: 212 us
  Pallas kernels  94.9 us (45%)
  starting transfers between devices  61.1 us (29%)
  waiting for transfers between devices  18.2 us (9%)
  between operations  15 us (7%)
  blocking collectives  14.6 us (7%)
  local copies, waits for them, and re-layouts  7.23 us (3%)
    pallas_call x8, Pallas kernels, call(): pl.pallas_call(kernel, out_shape=outs, in_specs=[pl.BlockSpec(memory_spac...  94.9 us
    ppermute x6, starting transfers between devices, swap(): lax.ppermute(to_upper, axis, up)  19.8 us
    all_to_all x1, starting transfers between devices, shards(): lax.all_to_all(r2_out, ('x', 'by'), split_axis=0, concat_axis=0, tiled=True)  15.3 us
    all_to_all x1, blocking collectives, shards(): lax.all_to_all(back, ALL, split_axis=0, concat_axis=0, tiled=True)  14.6 us
    all_to_all x1, starting transfers between devices, shards(): lax.all_to_all(outgoing, ALL, split_axis=0, concat_axis=0, tiled=True)  11.5 us
    ppermute x6, starting transfers between devices, swap(): lax.ppermute(to_lower, axis, down)  10.8 us
    ppermute x6, waiting for transfers between devices, swap(): lax.ppermute(to_lower, axis, down)  6.25 us
    unnamed x34, local copies, waits for them, and re-layouts  5.12 us
  transfers between devices with their start and end apart: 16, of which 8 were waited for; matrix products, arithmetic and copies ran while one was open for 2% of the time, Pallas kernels for 21%

profile of v6, /device:TPU:1, one launch (start us, length us, event | category | flops | bytes accessed | tf_op | source)
XLA Modules:
  0.0 211.7 jit_solution(1949848537785970095)
XLA Ops:
  7.8 4.3 %shard_map.96 = (f32[128,128]{1,0:T(8,128)}, s32[64,128]{1,0:T(8,128)}) custom-call(s32[1]{0:T(128)S(6)} %copy.14.active_ref, s32[64,128]{1,0:T(8,128)} %bitcast.23, f32[64,128]{1,0:T(8,128)} %bitcast.28), custom_call_target="tpu_custom_call" | custom-call | tf_op jit(solution)/shard_map/pallas_call | solution.py:606
  12.1 11.5 %all-to-all-start = ((f32[128,1,128]{2,1,0:T(1,128)}), f32[128,1,128]{2,1,0:T(1,128)S(1)}, u32[]{:S(2)}, u32[]{:S(2)}) async-start(f32[128,1,128]{2,1,0:T(1,128)} %bitcast.25), calls=%async_computation | async-start | bytes 131072 | tf_op jit(solution)/shard_map/all_to_all | solution.py:634
  23.7 2.8 %shard_map.95 = (f32[16,32,256]{2,1,0:T(8,128)}, f32[4,16,256]{2,1,0:T(8,128)}, f32[20,8,256]{2,1,0:T(8,128)}, f32[20,8,256]{2,1,0:T(8,128)}, f32[16,128]{1,0:T(8,128)}) custom-call(f32[16,32,256]{2,1,0:T(8,128)} %base_ref.1, f32[16,32,256]{2,1,0:T(8,128)} %state_ref.1), custom_call_target="tpu_custom_call" | custom-call | tf_op jit(solution)/shard_map/pallas_call | solution.py:606
  26.5 3.4 %collective-permute-start = (f32[20,8,256]{2,1,0:T(8,128)}, f32[20,8,256]{2,1,0:T(8,128)S(1)}, u32[]{:S(2)}, u32[]{:S(2)}) collective-permute-start(f32[20,8,256]{2,1,0:T(8,128)} %get-tuple-element.42), channel_id=1, source_target_pairs={{0,1},{1,2},{2,3},{3,4},{4,5},{5,6},{6,7},{7,8},{8,9},{9,10},{10,1... | collective-permute-start | bytes 491528 | tf_op jit(solution)/shard_map/ppermute | solution.py:623
  33.9 22.6 %shard_map.97 = (f32[16,32,256]{2,1,0:T(8,128)}, f32[16,8,256]{2,1,0:T(8,128)}, f32[16,8,256]{2,1,0:T(8,128)}) custom-call(f32[128,128]{1,0:T(8,128)} %bitcast.21, s32[4,12288]{1,0:T(4,128)} %refs_8_.1, s32[4,12288]{1,0:T(4,128)} %refs_9_.1, f32[4,12288]{1,0:T(4,128)} %refs_10_.1), custom_call_target="tpu_custom_call" | custom-call | tf_op jit(solution)/shard_map/pallas_call | solution.py:606
  56.4 3.0 %collective-permute-start.4 = (f32[16,8,256]{2,1,0:T(8,128)}, f32[16,8,256]{2,1,0:T(8,128)S(1)}, u32[]{:S(2)}, u32[]{:S(2)}) collective-permute-start(f32[16,8,256]{2,1,0:T(8,128)} %get-tuple-element.47), channel_id=1, source_target_pairs={{0,1},{1,2},{2,3},{3,4},{4,5},{5,6},{6,7},{7,8},{8,9},{9,10},{10,1... | collective-permute-start | bytes 393224 | tf_op jit(solution)/shard_map/ppermute | solution.py:623
  62.6 3.1 %collective-permute-start.3 = (f32[416,256]{1,0:T(8,128)S(1)}, f32[416,256]{1,0:T(8,128)S(1)}, u32[]{:S(2)}, u32[]{:S(2)}) collective-permute-start(f32[416,256]{1,0:T(8,128)S(1)} %get-tuple-element.90), channel_id=1, source_target_pairs={{16,0},{32,16},{48,32},{64,48},{80,64},{96,80},{112,96},{17,1},{33... | collective-permute-start | bytes 1277960 | tf_op jit(solution)/shard_map/ppermute | solution.py:623
  65.7 3.0 %collective-permute-start.2 = (f32[416,256]{1,0:T(8,128)S(1)}, f32[416,256]{1,0:T(8,128)S(1)}, u32[]{:S(2)}, u32[]{:S(2)}) collective-permute-start(f32[416,256]{1,0:T(8,128)S(1)} %get-tuple-element.91), channel_id=1, source_target_pairs={{0,16},{16,32},{32,48},{48,64},{64,80},{80,96},{96,112},{1,17},{17... | collective-permute-start | bytes 1277960 | tf_op jit(solution)/shard_map/ppermute | solution.py:623
  68.9 2.4 %collective-permute-start.6 = (f32[5,48,256]{2,1,0:T(8,128)S(1)}, f32[5,48,256]{2,1,0:T(8,128)S(1)}, u32[]{:S(2)}, u32[]{:S(2)}) collective-permute-start(f32[5,48,256]{2,1,0:T(8,128)S(1)} %pad_maximum_fusion.4), channel_id=1, source_target_pairs={{0,16},{16,32},{32,48},{48,64},{64,80},{80,96},{96,112},{1,17},{17... | collective-permute-start | bytes 737288 | tf_op jit(solution)/shard_map/ppermute | solution.py:623
  71.3 1.9 collective-permute-start.7
  73.2 3.2 %collective-permute-done.6.r_xlo = f32[5,48,256]{2,1,0:T(8,128)S(1)} collective-permute-done((f32[5,48,256]{2,1,0:T(8,128)S(1)}, f32[5,48,256]{2,1,0:T(8,128)S(1)}, u32[]{:S(2)}, u32[]{:S(2)}) %collective-permute-start.6) | collective-permute-done | bytes 245792 | tf_op jit(solution)/shard_map/ppermute | solution.py:623
  76.5 2.4 %collective-permute-done.7.r_xhi = f32[5,48,256]{2,1,0:T(8,128)S(1)} collective-permute-done((f32[5,48,256]{2,1,0:T(8,128)S(1)}, f32[5,48,256]{2,1,0:T(8,128)S(1)}, u32[]{:S(2)}, u32[]{:S(2)}) %collective-permute-start.7) | collective-permute-done | bytes 245792 | tf_op jit(solution)/shard_map/ppermute | solution.py:623
  80.5 8.1 %shard_map.98 = (f32[28,48,256]{2,1,0:T(8,128)}, f32[28,48,256]{2,1,0:T(8,128)}, f32[28,48,256]{2,1,0:T(8,128)}, f32[28,48,256]{2,1,0:T(8,128)}, f32[8,16,128]{2...) custom-call(f32[16,32,256]{2,1,0:T(8,128)} %get-tuple-element.41.q_own, f32[20,8,256]{2,1,0:T(8,128)} %copy-done.4, ...), custom_call_target="tpu_custom_call" | custom-call | tf_op jit(solution)/shard_map/pallas_call | solution.py:606
  88.5 4.3 %collective-permute-start.8 = (f32[8,8,128]{2,1,0:T(8,128)}, f32[8,8,128]{2,1,0:T(8,128)S(1)}, u32[]{:S(2)}, u32[]{:S(2)}) collective-permute-start(f32[8,8,128]{2,1,0:T(8,128)} %get-tuple-element.49), channel_id=1, source_target_pairs={{0,1},{1,2},{2,3},{3,4},{4,5},{5,6},{6,7},{7,8},{8,9},{9,10},{10,1... | collective-permute-start | bytes 98312 | tf_op jit(solution)/shard_map/ppermute | solution.py:623
  95.0 3.2 %collective-permute-done.9 = f32[8,8,128]{2,1,0:T(8,128)S(1)} collective-permute-done((f32[8,8,128]{2,1,0:T(8,128)}, f32[8,8,128]{2,1,0:T(8,128)S(1)}, u32[]{:S(2)}, u32[]{:S(2)}) %collective-permute-start.9) | collective-permute-done | bytes 32800 | tf_op jit(solution)/shard_map/ppermute | solution.py:623
  100.1 3.6 %collective-permute-start.10 = (f32[8,32,128]{2,1,0:T(8,128)S(1)}, f32[8,32,128]{2,1,0:T(8,128)S(1)}, u32[]{:S(2)}, u32[]{:S(2)}) collective-permute-start(f32[8,32,128]{2,1,0:T(8,128)S(1)} %constant_dynamic-update-slice_fusion.own), channel_id=1, source_target_pairs={{0,16},{16,32},{32,48},{48,64},{64,80},{80,96},{96,112},{1,17},{17... | collective-permute-start | bytes 393224 | tf_op jit(solution)/shard_map/ppermute | solution.py:623
  106.4 5.1 %shard_map.99 = (f32[24,32,128]{2,1,0:T(8,128)}, f32[24,32,128]{2,1,0:T(8,128)}, f32[24,32,128]{2,1,0:T(8,128)}, f32[24,32,128]{2,1,0:T(8,128)}, f32[64,16,128]{2,1,0:T(8,128)}) custom-call(f32[8,32,128]{2,1,0:T(8,128)} %copy-done.12, f32[8,32,128]{2,1,0:T(8,128)} %copy-done.14, f32[8,32,128]{2,1,0:T(8,128)} %copy-done.13, f32[4,32,256]{2,1,0:T(8,128)} %copy-done.3, ...), custom_call_target="tpu_custom_call" | custom-call | tf_op jit(solution)/shard_map/pallas_call | solution.py:606
  111.5 15.3 %all-to-all-start.1 = ((f32[64,16,128]{2,1,0:T(8,128)}), f32[64,16,128]{2,1,0:T(8,128)S(1)}, u32[]{:S(2)}, u32[]{:S(2)}) async-start(f32[64,16,128]{2,1,0:T(8,128)} %get-tuple-element.53), calls=%async_computation.1 | async-start | bytes 1048576 | tf_op jit(solution)/shard_map/all_to_all | solution.py:683
  127.4 5.3 %shard_map.100 = (f32[10,128,256]{2,1,0:T(8,128)}, f32[10,128,256]{2,1,0:T(8,128)}, f32[10,128,256]{2,1,0:T(8,128)}, f32[6,64,128]{2,1,0:T(8,128)}, f32[6,64,128]{2,1,0:T(8,128)}) custom-call(f32[128,16,128]{2,1,0:T(8,128)} %bitcast.20), custom_call_target="tpu_custom_call" | custom-call | tf_op jit(solution)/shard_map/pallas_call | solution.py:606
  132.7 5.0 %all-to-all-done.1.r2_mine = f32[64,16,128]{2,1,0:T(8,128)S(1)} async-done(((f32[64,16,128]{2,1,0:T(8,128)}), f32[64,16,128]{2,1,0:T(8,128)S(1)}, u32[]{:S(2)}, u32[]{:S(2)}) %all-to-all-start.1) | async-done | bytes 524320 | tf_op jit(solution)/shard_map/all_to_all | solution.py:683
  137.7 3.5 %collective-permute-start.12 = (f32[64,16,128]{2,1,0:T(8,128)S(1)}, f32[64,16,128]{2,1,0:T(8,128)S(1)}, u32[]{:S(2)}, u32[]{:S(2)}) collective-permute-start(f32[64,16,128]{2,1,0:T(8,128)S(1)} %all-to-all-done.1.r2_mine), channel_id=1, source_target_pairs={{0,16},{16,0},{1,17},{17,1},{2,18},{18,2},{3,19},{19,3},{4,20},{20... | collective-permute-start | bytes 1572872 | tf_op jit(solution)/shard_map/ppermute | solution.py:688
  143.6 43.7 %shard_map.101 = (f32[16,32,256]{2,1,0:T(8,128)}, f32[128,128]{1,0:T(8,128)}) custom-call(s32[2]{0:T(128)} %pad_add_fusion.place_ref, f32[64,16,128]{2,1,0:T(8,128)} %copy-done, f32[64,16,128]{2,1,0:T(8,128)} %copy-done.6, f32[10,128,256]{2,1,0:T(8,128)} %get-tuple-element.62.q2, f32[10,128,256]{2,1,0:T(8,128)} %get-tuple-element.63.w2, ...), custom_call_target="tpu_custom_call" | custom-call | tf_op jit(solution)/shard_map/pallas_call | solution.py:606
  187.2 14.6 %all_to_all.27 = f32[128,1,128]{2,1,0:T(1,128)} all-to-all(f32[128,1,128]{2,1,0:T(1,128)} %bitcast.26), channel_id=1, replica_groups=mesh['x'=4,'core'=2,'by'=16] {'x','core','by'}, dimensions={0} | all-to-all | bytes 131072 | tf_op jit(solution)/shard_map/all_to_all | solution.py:703
  201.8 3.0 %shard_map.102 = f32[64,128]{1,0:T(8,128)} custom-call(s32[1]{0:T(128)S(6)} %copy.14.active_ref, s32[64,128]{1,0:T(8,128)} %bitcast.24, s32[64,128]{1,0:T(8,128)} %get-tuple-element.76.rank_ref, f32[128,128]{1,0:T(8,128)} %bitcast.22), custom_call_target="tpu_custom_call" | custom-call | tf_op jit(solution)/shard_map/pallas_call | solution.py:606
  (67 shorter events, 18.3 us)
Async XLA Ops:
  12.1 21.1 %all-to-all-start = ((f32[128,1,128]{2,1,0:T(1,128)}), f32[128,1,128]{2,1,0:T(1,128)S(1)}, u32[]{:S(2)}, u32[]{:S(2)}) async-start(f32[128,1,128]{2,1,0:T(1,128)} %bitcast.25), calls=%async_computation | async-start | bytes 131072 | tf_op jit(solution)/shard_map/all_to_all | solution.py:634
  23.7 87.8 %all-gather.3.cloned.1.call-start = ((), (), s32[]{:S(2)}) async-start(), calls=%async_computation.3 | async-start | bytes 1056768 | tf_op jit(solution)/shard_map/all_gather | solution.py:640
  26.5 35.4 %copy-start.15 = (f32[4,16,256]{2,1,0:T(8,128)S(1)}, f32[4,16,256]{2,1,0:T(8,128)}, u32[]{:S(2)}) copy-start(f32[4,16,256]{2,1,0:T(8,128)} %get-tuple-element.44) | copy-start | bytes 196612
  26.5 35.3 %collective-permute-start = (f32[20,8,256]{2,1,0:T(8,128)}, f32[20,8,256]{2,1,0:T(8,128)S(1)}, u32[]{:S(2)}, u32[]{:S(2)}) collective-permute-start(f32[20,8,256]{2,1,0:T(8,128)} %get-tuple-element.42), channel_id=1, source_target_pairs={{0,1},{1,2},{2,3},{3,4},{4,5},{5,6},{6,7},{7,8},{8,9},{9,10},{10,1... | collective-permute-start | bytes 491528 | tf_op jit(solution)/shard_map/ppermute | solution.py:623
  29.9 31.9 %collective-permute-start.1 = (f32[20,8,256]{2,1,0:T(8,128)}, f32[20,8,256]{2,1,0:T(8,128)S(1)}, u32[]{:S(2)}, u32[]{:S(2)}) collective-permute-start(f32[20,8,256]{2,1,0:T(8,128)} %get-tuple-element.43), channel_id=1, source_target_pairs={{1,0},{2,1},{3,2},{4,3},{5,4},{6,5},{7,6},{8,7},{9,8},{10,9},{11,1... | collective-permute-start | bytes 491528 | tf_op jit(solution)/shard_map/ppermute | solution.py:623
  56.4 12.3 %collective-permute-start.4 = (f32[16,8,256]{2,1,0:T(8,128)}, f32[16,8,256]{2,1,0:T(8,128)S(1)}, u32[]{:S(2)}, u32[]{:S(2)}) collective-permute-start(f32[16,8,256]{2,1,0:T(8,128)} %get-tuple-element.47), channel_id=1, source_target_pairs={{0,1},{1,2},{2,3},{3,4},{4,5},{5,6},{6,7},{7,8},{8,9},{9,10},{10,1... | collective-permute-start | bytes 393224 | tf_op jit(solution)/shard_map/ppermute | solution.py:623
  59.5 9.3 %collective-permute-start.5 = (f32[16,8,256]{2,1,0:T(8,128)}, f32[16,8,256]{2,1,0:T(8,128)S(1)}, u32[]{:S(2)}, u32[]{:S(2)}) collective-permute-start(f32[16,8,256]{2,1,0:T(8,128)} %get-tuple-element.48), channel_id=1, source_target_pairs={{1,0},{2,1},{3,2},{4,3},{5,4},{6,5},{7,6},{8,7},{9,8},{10,9},{11,1... | collective-permute-start | bytes 393224 | tf_op jit(solution)/shard_map/ppermute | solution.py:623
  62.6 16.2 %collective-permute-start.3 = (f32[416,256]{1,0:T(8,128)S(1)}, f32[416,256]{1,0:T(8,128)S(1)}, u32[]{:S(2)}, u32[]{:S(2)}) collective-permute-start(f32[416,256]{1,0:T(8,128)S(1)} %get-tuple-element.90), channel_id=1, source_target_pairs={{16,0},{32,16},{48,32},{64,48},{80,64},{96,80},{112,96},{17,1},{33... | collective-permute-start | bytes 1277960 | tf_op jit(solution)/shard_map/ppermute | solution.py:623
  65.7 13.1 %collective-permute-start.2 = (f32[416,256]{1,0:T(8,128)S(1)}, f32[416,256]{1,0:T(8,128)S(1)}, u32[]{:S(2)}, u32[]{:S(2)}) collective-permute-start(f32[416,256]{1,0:T(8,128)S(1)} %get-tuple-element.91), channel_id=1, source_target_pairs={{0,16},{16,32},{32,48},{48,64},{64,80},{80,96},{96,112},{1,17},{17... | collective-permute-start | bytes 1277960 | tf_op jit(solution)/shard_map/ppermute | solution.py:623
  68.8 10.1 %copy-start.7 = (f32[16,8,256]{2,1,0:T(8,128)}, f32[16,8,256]{2,1,0:T(8,128)S(1)}, u32[]{:S(2)}) copy-start(f32[16,8,256]{2,1,0:T(8,128)S(1)} %collective-permute-done.4.r_ylo) | copy-start | bytes 393220
  68.8 10.0 %copy-start.8 = (f32[16,8,256]{2,1,0:T(8,128)}, f32[16,8,256]{2,1,0:T(8,128)S(1)}, u32[]{:S(2)}) copy-start(f32[16,8,256]{2,1,0:T(8,128)S(1)} %collective-permute-done.5.r_yhi) | copy-start | bytes 393220
  68.9 7.6 %collective-permute-start.6 = (f32[5,48,256]{2,1,0:T(8,128)S(1)}, f32[5,48,256]{2,1,0:T(8,128)S(1)}, u32[]{:S(2)}, u32[]{:S(2)}) collective-permute-start(f32[5,48,256]{2,1,0:T(8,128)S(1)} %pad_maximum_fusion.4), channel_id=1, source_target_pairs={{0,16},{16,32},{32,48},{48,64},{64,80},{80,96},{96,112},{1,17},{17... | collective-permute-start | bytes 737288 | tf_op jit(solution)/shard_map/ppermute | solution.py:623
  71.3 7.5 %collective-permute-start.7 = (f32[5,48,256]{2,1,0:T(8,128)S(1)}, f32[5,48,256]{2,1,0:T(8,128)S(1)}, u32[]{:S(2)}, u32[]{:S(2)}) collective-permute-start(f32[5,48,256]{2,1,0:T(8,128)S(1)} %pad_maximum_fusion.5), channel_id=1, source_target_pairs={{16,0},{32,16},{48,32},{64,48},{80,64},{96,80},{112,96},{17,1},{33... | collective-permute-start | bytes 737288 | tf_op jit(solution)/shard_map/ppermute | solution.py:623
  76.4 2.4 %copy-start.10 = (f32[5,48,256]{2,1,0:T(8,128)}, f32[5,48,256]{2,1,0:T(8,128)S(1)}, u32[]{:S(2)}) copy-start(f32[5,48,256]{2,1,0:T(8,128)S(1)} %collective-permute-done.6.r_xlo) | copy-start | bytes 737284
  78.8 0.8 copy-start.1
  88.5 5.7 %collective-permute-start.8 = (f32[8,8,128]{2,1,0:T(8,128)}, f32[8,8,128]{2,1,0:T(8,128)S(1)}, u32[]{:S(2)}, u32[]{:S(2)}) collective-permute-start(f32[8,8,128]{2,1,0:T(8,128)} %get-tuple-element.49), channel_id=1, source_target_pairs={{0,1},{1,2},{2,3},{3,4},{4,5},{5,6},{6,7},{7,8},{8,9},{9,10},{10,1... | collective-permute-start | bytes 98312 | tf_op jit(solution)/shard_map/ppermute | solution.py:623
  92.9 5.3 %collective-permute-start.9 = (f32[8,8,128]{2,1,0:T(8,128)}, f32[8,8,128]{2,1,0:T(8,128)S(1)}, u32[]{:S(2)}, u32[]{:S(2)}) collective-permute-start(f32[8,8,128]{2,1,0:T(8,128)} %get-tuple-element.51), channel_id=1, source_target_pairs={{1,0},{2,1},{3,2},{4,3},{5,4},{6,5},{7,6},{8,7},{9,8},{10,9},{11,1... | collective-permute-start | bytes 98312 | tf_op jit(solution)/shard_map/ppermute | solution.py:623
  98.2 7.5 %copy-start.12 = (f32[8,32,128]{2,1,0:T(8,128)}, f32[8,32,128]{2,1,0:T(8,128)S(1)}, u32[]{:S(2)}) copy-start(f32[8,32,128]{2,1,0:T(8,128)S(1)} %constant_dynamic-update-slice_fusion.own) | copy-start | bytes 393220
  98.2 6.3 %collective-permute-start.11 = (f32[8,32,128]{2,1,0:T(8,128)S(1)}, f32[8,32,128]{2,1,0:T(8,128)S(1)}, u32[]{:S(2)}, u32[]{:S(2)}) collective-permute-start(f32[8,32,128]{2,1,0:T(8,128)S(1)} %constant_dynamic-update-slice_fusion.own), channel_id=1, source_target_pairs={{16,0},{32,16},{48,32},{64,48},{80,64},{96,80},{112,96},{17,1},{33... | collective-permute-start | bytes 393224 | tf_op jit(solution)/shard_map/ppermute | solution.py:623
  100.1 5.6 %collective-permute-start.10 = (f32[8,32,128]{2,1,0:T(8,128)S(1)}, f32[8,32,128]{2,1,0:T(8,128)S(1)}, u32[]{:S(2)}, u32[]{:S(2)}) collective-permute-start(f32[8,32,128]{2,1,0:T(8,128)S(1)} %constant_dynamic-update-slice_fusion.own), channel_id=1, source_target_pairs={{0,16},{16,32},{32,48},{48,64},{64,80},{80,96},{96,112},{1,17},{17... | collective-permute-start | bytes 393224 | tf_op jit(solution)/shard_map/ppermute | solution.py:623
  104.5 1.2 copy-start.13
  111.5 26.2 %all-to-all-start.1 = ((f32[64,16,128]{2,1,0:T(8,128)}), f32[64,16,128]{2,1,0:T(8,128)S(1)}, u32[]{:S(2)}, u32[]{:S(2)}) async-start(f32[64,16,128]{2,1,0:T(8,128)} %get-tuple-element.53), calls=%async_computation.1 | async-start | bytes 1048576 | tf_op jit(solution)/shard_map/all_to_all | solution.py:683
  137.7 5.1 %copy-start = (f32[64,16,128]{2,1,0:T(8,128)}, f32[64,16,128]{2,1,0:T(8,128)S(1)}, u32[]{:S(2)}) copy-start(f32[64,16,128]{2,1,0:T(8,128)S(1)} %all-to-all-done.1.r2_mine) | copy-start | bytes 1572868
  137.7 5.1 %collective-permute-start.12 = (f32[64,16,128]{2,1,0:T(8,128)S(1)}, f32[64,16,128]{2,1,0:T(8,128)S(1)}, u32[]{:S(2)}, u32[]{:S(2)}) collective-permute-start(f32[64,16,128]{2,1,0:T(8,128)S(1)} %all-to-all-done.1.r2_mine), channel_id=1, source_target_pairs={{0,16},{16,0},{1,17},{17,1},{2,18},{18,2},{3,19},{19,3},{4,20},{20... | collective-permute-start | bytes 1572872 | tf_op jit(solution)/shard_map/ppermute | solution.py:688
  (8 other events, 5.7 us)
Sparse Core Ops, SparseCore 0:
  27.3 66.3 all-gather.2
